TPU v7x, 32 devices: a whole 2x2x4 slice. The times are simulated.
32 devices in a mesh: leaf: 8 (over z, x), rows: 4 (over y, core).
Axes of the slice: x: 2, y: 2, z: 4, core: 2. Of those that a mesh axis runs over, the one named last changes fastest.
Arguments:
- leaf_basis: float32 [1024, 64, 256], P(('leaf', 'rows')), may hold values from -0.375 to 0.375
- leaf_transfer: float32 [1024, 64, 64], P(('leaf', 'rows'))
- device_transfer: float32 [32, 64, 64], P(('leaf', 'rows'))
- upper_transfer: float32 [30, 64, 64], replicated
- couplings: float32 [1024, 64, 64], P(('leaf', 'rows')), may hold values from -0.1875 to 0.1875
- couple_offset: int32 [1024], P(('leaf', 'rows')), may hold values from 4 to 28, as said below
Outputs:
- leaf_orth: float32 [1024, 64, 256], P(('leaf', 'rows'))
- leaf_bridge: float32 [1024, 64, 64], P(('leaf', 'rows'))
- new_transfers: float32 [32, 5, 64, 64], P(('leaf', 'rows'))
- coupled: float32 [1024, 64, 64], P(('leaf', 'rows'))
Inputs may be any that keep to these rules, and one draw needn't show every extreme that they name: couple_offset[b] is 4 times a number of 1 to 7, so block b couples device cluster b // 32 with a cluster of another branch at the same position within its branch; among the 32 blocks of one device cluster, at most 6 name the same column cluster, and on every device some column cluster is named exactly 6 times.
All inputs are finite; a program needn't handle non-finite values.
Results may differ from a plain program's by a relative error of at most 0.0001.
Values sent between devices are 32-bit elements; how exact they have to be, the bound alone decides.
No kernel may reach another device: no remote copies, remote signals or barrier semaphores. Data moves between devices by JAX's collectives and lax.ppermute only.
A program may use at most 128 MiB of HBM per device.

v0:
```python
import jax
import jax.numpy as jnp
from jax import lax
from jax.sharding import PartitionSpec as P

HIGH = lax.Precision.HIGHEST


def swapped(value, axis, apart):
    mask = 2**apart
    pairs = [(source, source ^ mask) for source in range(lax.axis_size(axis))]
    return lax.ppermute(value, axis, pairs)


def lower_solve(low, right):
    return lax.linalg.triangular_solve(low, right, left_side=True, lower=True)


def lift(grams, trans):
    inner = jnp.einsum("nkl,nlj->nkj", grams, trans, precision=HIGH)
    return jnp.einsum("nki,nkj->nij", trans, inner, precision=HIGH)


def per_device(
    leaf_basis, leaf_transfer, device_transfer, upper_transfer, couplings, couple_offset
):
    n_rows = lax.axis_size("rows")
    n_leaf = lax.axis_size("leaf")
    row_bits = n_rows.bit_length() - 1
    leaf_bits = n_leaf.bit_length() - 1
    levels = row_bits + leaf_bits
    clusters = n_rows * n_leaf
    branch = lax.axis_index("leaf")
    row_id = lax.axis_index("rows")
    myself = branch * n_rows + row_id
    leaf_gram = jnp.einsum("nrk,nsk->nrs", leaf_basis, leaf_basis, precision=HIGH)
    leaf_low = jnp.linalg.cholesky(leaf_gram)
    leaf_orth = lower_solve(leaf_low, leaf_basis)
    own_gram = jnp.sum(lift(leaf_gram, leaf_transfer), axis=0)
    own_lift = lift(own_gram[None], device_transfer)
    row_grams, row_lifts = (
        lax.all_gather(own_gram[None], "rows", axis=0, tiled=True),
        lax.all_gather(own_lift, "rows", axis=0, tiled=True),
    )
    path = [own_gram]
    lifted = row_lifts
    level = levels
    start = branch * n_rows
    for step in range(row_bits):
        gram = lifted[0::2] + lifted[1::2]
        level -= 1
        start = start // 2
        path.append(lax.dynamic_index_in_dim(gram, row_id >> step + 1, 0, keepdims=False))
        trans = lax.dynamic_slice_in_dim(upper_transfer, 2**level - 2 + start, gram.shape[0], 0)
        lifted = lift(gram, trans)
    blocks = couplings.shape[0]
    targets = (myself + couple_offset) % clusters
    column_grams = None
    carry = lifted[0]
    for bit in range(leaf_bits):
        gram = carry + swapped(carry, "leaf", bit)
        level -= 1
        path.append(gram)
        if level > 0:
            node = branch >> bit + 1
            trans = lax.dynamic_slice_in_dim(upper_transfer, 2**level - 2 + node, 1, 0)
            carry = lift(gram[None], trans)[0]
    piece = lax.all_gather(row_grams, "leaf", axis=0, tiled=True)
    labels = lax.broadcasted_iota(jnp.int32, (blocks, piece.shape[0]), 1)
    onehot = (targets[:, None] == labels).astype(jnp.float32)
    column_grams = jnp.einsum("bp,pij->bij", onehot, piece, precision=HIGH)
    lows = jnp.linalg.cholesky(jnp.stack(path, axis=0))
    edges = [device_transfer[0]]
    for step in range(1, levels):
        node_level = levels - step
        edges.append(
            lax.dynamic_index_in_dim(
                upper_transfer, 2**node_level - 2 + (myself >> step), 0, keepdims=False
            )
        )
    edge_stack = jnp.stack(edges, axis=0)
    right = jnp.einsum("nki,nkj->nij", edge_stack, lows[:levels], precision=HIGH)
    fresh = jnp.swapaxes(lower_solve(lows[1:], right), 1, 2)
    new_transfers = fresh[None]
    device_low = jnp.broadcast_to(lows[0], leaf_transfer.shape)
    bridge_right = jnp.einsum("nki,nkj->nij", leaf_transfer, leaf_low, precision=HIGH)
    leaf_bridge = jnp.swapaxes(lower_solve(device_low, bridge_right), 1, 2)
    column_low = jnp.linalg.cholesky(column_grams)
    inner = jnp.einsum("nkl,nlj->nkj", couplings, column_low, precision=HIGH)
    coupled = jnp.einsum("ki,nkj->nij", lows[0], inner, precision=HIGH)
    return (leaf_orth, leaf_bridge, new_transfers, coupled)


def solution(mesh):
    in_specs = (
        P(("leaf", "rows"), None, None),
        P(("leaf", "rows"), None, None),
        P(("leaf", "rows"), None, None),
        P(),
        P(("leaf", "rows"), None, None),
        P(("leaf", "rows")),
    )
    out_specs = (
        P(("leaf", "rows"), None, None),
        P(("leaf", "rows"), None, None),
        P(("leaf", "rows"), None, None, None),
        P(("leaf", "rows"), None, None),
    )
    return jax.shard_map(
        per_device, mesh=mesh, in_specs=in_specs, out_specs=out_specs, check_vma=False
    )
```

profile of v0, /device:TPU:0, one launch (start us, length us, event | category | flops | bytes accessed | tf_op | source)
XLA Modules:
  0.0 714.9 jit_solution(10042921623259399778)
XLA Ops:
  7.9 6.5 all-gather
  26.5 5.4 all-gather.1
  31.9 33.3 %all_gather.11 = f32[32,64,64]{2,1,0:T(8,128)S(1)} all-gather(f32[4,64,64]{2,1,0:T(8,128)S(1)} %bitcast.100), channel_id=1, replica_groups=mesh['leaf'=8,'rows'=4] {'leaf'}, dimensions={0}, use_global_device_ids=true | all-gather | bytes 589824 | tf_op jit(solution)/shard_map/all_gather | solution.py:68
  65.2 2.3 fusion.2
  67.5 2.7 copy.118
  70.2 3.2 fusion
  73.4 189.1 %custom-call.22 = f32[32,64,64]{2,1,0:T(8,128)} custom-call(f32[32,64,64]{2,1,0:T(8,128)} %fusion), custom_call_target="Cholesky" | custom-call | tf_op jit(solution)/shard_map/jit(cholesky)/cholesky | solution.py:88
  271.1 2.4 fusion.1
  273.4 188.2 %custom-call.21 = f32[32,64,64]{2,1,0:T(8,128)S(1)} custom-call(f32[32,64,64]{2,1,0:T(8,128)} %fusion.1), custom_call_target="Cholesky" | custom-call | tf_op jit(solution)/shard_map/jit(cholesky)/cholesky | solution.py:37
  465.9 2.8 select_bitcast_fusion
  468.7 4.0 copy.91
  472.7 3.4 fusion.63
  476.0 68.7 %custom-call.16 = f32[32,1,64,64]{0,2,3,1:T(8,128)} custom-call(f32[32,1,64,64]{0,3,2,1:T(8,128)} %get-tuple-element.21), custom_call_target="InvertDiagBlocksLowerTriangular" | custom-call | tf_op jit(solution)/shard_map/triangular_solve | solution.py:16
  544.7 2.9 copy.90
  547.7 3.2 fusion.62
  556.6 3.1 collective-permute-done.1
  561.9 4.8 collective-permute-done.2
  567.5 35.9 %custom-call.17 = f32[6,64,64]{2,1,0:T(8,128)S(1)} custom-call(f32[6,64,64]{2,1,0:T(8,128)} %fusion.10), custom_call_target="Cholesky" | custom-call | tf_op jit(solution)/shard_map/jit(cholesky)/cholesky | solution.py:72
  606.3 2.6 copy.121
  609.3 25.3 %custom-call.19 = f32[5,1,64,64]{2,3,1,0:T(8,128)S(1)} custom-call(f32[5,1,64,64]{3,2,1,0:T(8,128)} %fusion.11), custom_call_target="InvertDiagBlocksLowerTriangular" | custom-call | tf_op jit(solution)/shard_map/triangular_solve | solution.py:16
  634.6 2.6 broadcast_select_fusion
  637.2 68.8 %custom-call.18 = f32[32,1,64,64]{0,2,3,1:T(8,128)} custom-call(f32[32,1,64,64]{0,3,2,1:T(8,128)} %broadcast_select_fusion), custom_call_target="InvertDiagBlocksLowerTriangular" | custom-call | tf_op jit(solution)/shard_map/triangular_solve | solution.py:16
  706.1 3.9 copy.108
  710.9 4.0 fusion.65
  (93 shorter events, 44.7 us)
Async XLA Ops:
  0.6 1.6 copy-start
  2.2 2.1 copy-start.2
  4.3 3.1 copy-start.7
  22.5 530.6 %collective-permute-start = (f32[64,64]{0,1:T(8,128)}, f32[64,64]{0,1:T(8,128)}, u32[]{:S(2)}, u32[]{:S(2)}) collective-permute-start(f32[64,64]{0,1:T(8,128)} %fusion.30), channel_id=1, source_target_pairs={{0,4},{4,0},{8,12},{12,8},{16,20},{20,16},{24,28},{28,24},{1,5},{5... | collective-permute-start | bytes 49160 | tf_op jit(solution)/shard_map/ppermute | solution.py:12
  25.1 1.3 copy-start.16
  70.2 196.5 %copy-start.10 = (f32[1,64,64]{1,2,0:T(8,128)S(1)}, f32[1,64,64]{1,2,0:T(8,128)}, u32[]{:S(2)}) copy-start(f32[1,64,64]{1,2,0:T(8,128)} %copy.113) | copy-start | bytes 49156
  463.7 2.2 copy-start.1
  468.7 4.0 copy-start.3
  547.7 3.3 copy-start.5
  547.7 3.2 copy-start.6
  547.7 3.2 copy-start.15
  550.9 2.0 copy-start.11
  550.9 2.1 copy-start.14
  551.0 2.1 copy-start.12
  551.0 2.1 copy-start.13
  553.1 0.7 copy-start.8
  555.8 4.0 collective-permute-start.1
  561.8 4.9 collective-permute-start.2
  606.3 2.6 copy-start.9
  637.2 73.7 %copy-start.4 = (f32[32,64,64]{2,1,0:T(8,128)S(1)}, f32[32,64,64]{2,1,0:T(8,128)}, u32[]{:S(2)}) copy-start(f32[32,64,64]{2,1,0:T(8,128)} %fusion.63) | copy-start | bytes 1572868
where the time goes:
time: 717 us; the launch traced here: 715 us
  other arithmetic  594 us (83%)
  blocking collectives  45.2 us (6%)
  matrix products  32.6 us (5%)
  local copies, waits for them, and re-layouts  31.6 us (4%)
  waiting for transfers between devices  7.91 us (1%)
    another operation x3, other arithmetic, per_device(): column_low = jnp.linalg.cholesky(column_grams)  191 us
    another operation x4, other arithmetic, per_device(): leaf_low = jnp.linalg.cholesky(leaf_gram)  190 us
    another operation x7, other arithmetic, lower_solve(): return lax.linalg.triangular_solve(low, right, left_side=True, lower=True)  169 us
    another operation x4, other arithmetic, per_device(): lows = jnp.linalg.cholesky(jnp.stack(path, axis=0))  36.1 us
    all_gather x1, blocking collectives, per_device(): piece = lax.all_gather(row_grams, 'leaf', axis=0, tiled=True)  33.3 us
  transfers between devices with their start and end apart: 3, of which 2 were waited for; matrix products, arithmetic and copies ran while one was open for 69% of the time, Pallas kernels for 0%

commit v1 on v0

v1 whole, which is shorter than its diff:
```python
import functools

import jax
import jax.numpy as jnp
from jax import lax
from jax.experimental import pallas as pl
from jax.experimental.pallas import tpu as pltpu
from jax.sharding import PartitionSpec as P

HIGH = lax.Precision.HIGHEST
SUB = 8


def mm(a, b):
    return lax.dot_general(
        a, b, (((1,), (0,)), ((), ())), precision=HIGH, preferred_element_type=jnp.float32
    )


def mm_nt(a, b):
    return lax.dot_general(
        a, b, (((1,), (1,)), ((), ())), precision=HIGH, preferred_element_type=jnp.float32
    )


def mm_tn(a, b):
    return lax.dot_general(
        a, b, (((0,), (0,)), ((), ())), precision=HIGH, preferred_element_type=jnp.float32
    )


def lift(gram, trans):
    return mm_tn(trans, mm(gram, trans))


def eliminate(w_ref, f_ref, s_ref):
    rank = w_ref.shape[0]
    lanes = w_ref.shape[2]
    groups = rank // SUB
    place = lax.broadcasted_iota(jnp.int32, (SUB, lanes), 0)

    def block(rows, cols):
        return w_ref[pl.ds(rows * SUB, SUB), pl.ds(cols * SUB, SUB), :]

    def spread(value, at):
        return jnp.broadcast_to(value[at : at + 1, :], (SUB, lanes))

    def corner(kb):
        rows = [w_ref[kb * SUB + p, pl.ds(kb * SUB, SUB), :] for p in range(SUB)]
        inverses = []
        for q in range(SUB):
            pivot = spread(rows[q], q)
            inverse = 1.0 / pivot
            root = lax.rsqrt(pivot)
            root = root * (1.5 - 0.5 * pivot * root * root)
            s_ref[kb * SUB + q] = root
            inverses.append(inverse)
            scaled = rows[q] * inverse
            unit = jnp.where(place == q, 1.0, rows[q])
            for p in range(q + 1, SUB):
                kept = jnp.where(place == q, 0.0, rows[p])
                rows[p] = kept - spread(scaled, p) * unit
        for p in range(SUB):
            w_ref[kb * SUB + p, pl.ds(kb * SUB, SUB), :] = rows[p]
        return rows, inverses

    def panel(kb, rows, inverses):
        mult = {(p, q): spread(rows[p], q) for p in range(SUB) for q in range(p)}
        for jv in range(groups):
            if jv == kb:
                continue
            old = [w_ref[kb * SUB + p, pl.ds(jv * SUB, SUB), :] for p in range(SUB)]
            for p in range(SUB):
                new = old[p]
                for q in range(p):
                    new = new + mult[p, q] * old[q]
                if p:
                    w_ref[kb * SUB + p, pl.ds(jv * SUB, SUB), :] = new
                if jv > kb:
                    scaled = new * inverses[p]
                    for s in range(SUB):
                        f_ref[p, jv * SUB + s] = spread(scaled, s)

    def trail(kb, rows, ib, jv):
        if jv == kb:
            acc = None
        else:
            acc = block(ib, jv)
        for q in range(SUB):
            if jv == kb:
                source = jnp.where(place < q, rows[q], jnp.where(place == q, 1.0, 0.0))
            else:
                source = w_ref[kb * SUB + q, pl.ds(jv * SUB, SUB), :]
            term = f_ref[q, pl.ds(ib * SUB, SUB)] * source[None]
            acc = -term if acc is None else acc - term
        w_ref[pl.ds(ib * SUB, SUB), pl.ds(jv * SUB, SUB), :] = acc

    rows, inverses = corner(0)
    for kb in range(groups):
        panel(kb, rows, inverses)
        if kb + 1 == groups:
            break
        trail(kb, rows, kb + 1, kb + 1)
        ahead = corner(kb + 1)
        for jv in range(groups):
            for ib in range(kb + 1, groups):
                if (ib, jv) == (kb + 1, kb + 1):
                    continue
                if jv > kb and ib > jv:
                    continue
                trail(kb, rows, ib, jv)
        rows, inverses = ahead


def read_factors(w_ref, s_ref, k):
    rank = w_ref.shape[0]
    lanes = w_ref.shape[2]
    row = w_ref[k]
    root = jnp.broadcast_to(s_ref[k][:1], (rank, lanes))
    place = lax.broadcasted_iota(jnp.int32, (rank, lanes), 0)
    upper = jnp.where(place >= k, row * root, 0.0)
    inverse = jnp.where(place < k, row * root, jnp.where(place == k, root, 0.0))
    return jnp.concatenate([upper, inverse], axis=0).T


def gram_kernel(steps, basis_ref, trans_ref, dev_ref, grams_ref, lift_ref, acc_ref):
    step = pl.program_id(0)
    chunk, rank = basis_ref.shape[0], basis_ref.shape[1]
    parts = []
    for n in range(chunk):
        basis = basis_ref[n]
        gram = mm_nt(basis, basis)
        grams_ref[step * chunk + n] = gram
        parts.append(mm(gram, trans_ref[n]))
    inner = jnp.concatenate(parts, axis=0)
    total = mm_tn(trans_ref[...].reshape(chunk * rank, rank), inner)

    @pl.when(step == 0)
    def _():
        acc_ref[...] = total

    @pl.when(step > 0)
    def _():
        acc_ref[...] += total

    @pl.when(step == steps - 1)
    def _():
        gram = acc_ref[...]
        grams_ref[steps * chunk] = gram
        lift_ref[...] = lift(gram, dev_ref[0])


def factor_kernel(grams_ref, out_ref, w_ref, f_ref, s_ref):
    count, rank = grams_ref.shape[0], grams_ref.shape[1]
    flat = grams_ref.reshape(count * rank, rank)
    for i in range(rank):
        w_ref[i] = flat[pl.ds(i, count, stride=rank), :].T
    eliminate(w_ref, f_ref, s_ref)
    out = out_ref.reshape(count * rank, 2 * rank)
    for k in range(rank):
        out[pl.ds(k, count, stride=rank), :] = read_factors(w_ref, s_ref, k)


def branch_kernel(n_rows, n_leaf, *refs):
    own_ref = refs[0]
    got = refs[1:n_rows]
    upper_ref, factor_ref, send_ref, path_ref = refs[n_rows:]
    rank = own_ref.shape[0]
    branch, row = lax.axis_index("leaf"), lax.axis_index("rows")
    lifted = [own_ref[...]] + [ref[...] for ref in got]
    level = (n_rows * n_leaf).bit_length() - 1
    node = branch * n_rows + row
    step = 0
    while len(lifted) > 1:
        grams = [lifted[2 * n] + lifted[2 * n + 1] for n in range(len(lifted) // 2)]
        level -= 1
        node = node >> 1
        path_ref[step] = grams[0]
        step += 1
        lifted = [
            lift(gram, upper_ref[2**level - 2 + (node ^ n)]) for n, gram in enumerate(grams)
        ]
    send_ref[0] = factor_ref[0, :, :rank]
    send_ref[1] = lifted[0]


def leaf_kernel(basis_ref, trans_ref, coup_ref, factor_ref, own_ref, orth_ref, bridge_ref, half_ref):
    chunk, rank = basis_ref.shape[0], basis_ref.shape[1]
    own_upper = own_ref[0, :, :rank]
    own_inverse = own_ref[0, :, rank:]
    parts = []
    for n in range(chunk):
        upper = factor_ref[n, :, :rank]
        inverse = factor_ref[n, :, rank:]
        orth_ref[n] = mm(inverse, basis_ref[n])
        parts.append(mm(upper, trans_ref[n]))
        half_ref[n] = mm(own_upper, coup_ref[n])
    moved = mm_nt(jnp.concatenate(parts, axis=0), own_inverse)
    bridge_ref[...] = moved.reshape(chunk, rank, rank)


def top_kernel(n_rows, n_leaf, *refs):
    send_ref = refs[0]
    got = refs[1:n_leaf]
    (
        upper_ref,
        dev_ref,
        path_ref,
        own_ref,
        half_ref,
        offset_ref,
        fresh_ref,
        coupled_ref,
        grams_ref,
        cols_ref,
        out_ref,
        w_ref,
        f_ref,
        s_ref,
    ) = refs[n_leaf:]
    rank = send_ref.shape[1]
    row_bits = n_rows.bit_length() - 1
    leaf_bits = n_leaf.bit_length() - 1
    levels = row_bits + leaf_bits
    branch, row = lax.axis_index("leaf"), lax.axis_index("rows")
    myself = branch * n_rows + row
    every = [send_ref] + list(got)
    for n, ref in enumerate(every):
        cols_ref[n] = ref[0]
    lifted = [ref[1] for ref in every]
    for n in range(row_bits):
        grams_ref[n] = path_ref[n]
    level, node, step = leaf_bits, branch, row_bits
    while len(lifted) > 1:
        grams = [lifted[2 * n] + lifted[2 * n + 1] for n in range(len(lifted) // 2)]
        level -= 1
        node = node >> 1
        grams_ref[step] = grams[0]
        step += 1
        if level == 0:
            break
        lifted = [
            lift(gram, upper_ref[2**level - 2 + (node ^ n)]) for n, gram in enumerate(grams)
        ]
    flat = grams_ref.reshape(levels * rank, rank)
    for i in range(rank):
        w_ref[i] = flat[pl.ds(i, levels, stride=rank), :].T
    eliminate(w_ref, f_ref, s_ref)
    out = out_ref.reshape(levels * rank, 2 * rank)
    for k in range(rank):
        out[pl.ds(k, levels, stride=rank), :] = read_factors(w_ref, s_ref, k)
    for k in range(levels):
        node_level = levels - k
        if k == 0:
            edge = dev_ref[0]
            low = own_ref[0, :, :rank]
        else:
            edge = upper_ref[2**node_level - 2 + (myself >> k)]
            low = out_ref[k - 1, :, :rank]
        fresh_ref[0, k] = mm_nt(mm(low, edge), out_ref[k, :, rank:])
    for b in range(half_ref.shape[0]):
        target = lax.rem(myself + offset_ref[b], n_rows * n_leaf)
        column = (target // n_rows) ^ branch
        coupled_ref[b] = mm_nt(half_ref[b], cols_ref[column])


def swaps(value, axis):
    size = lax.axis_size(axis)
    return [
        lax.ppermute(value, axis, [(source, source ^ mask) for source in range(size)])
        for mask in range(1, size)
    ]


def cost(flops, moved):
    return pl.CostEstimate(flops=flops, bytes_accessed=moved, transcendentals=0)


def per_device(
    leaf_basis, leaf_transfer, device_transfer, upper_transfer, couplings, couple_offset
):
    n_rows = lax.axis_size("rows")
    n_leaf = lax.axis_size("leaf")
    row_bits = n_rows.bit_length() - 1
    levels = row_bits + n_leaf.bit_length() - 1
    leaves, rank, points = leaf_basis.shape
    blocks = couplings.shape[0]
    f32 = jnp.float32
    params = pltpu.CompilerParams(vmem_limit_bytes=40 * 1024 * 1024)
    vmem = pl.BlockSpec(memory_space=pltpu.VMEM)
    smem = pl.BlockSpec(memory_space=pltpu.SMEM)
    chunk = 8
    steps = leaves // chunk

    def scratch(count):
        return [
            pltpu.VMEM((rank, rank, count), f32),
            pltpu.VMEM((SUB, rank, SUB, count), f32),
            pltpu.VMEM((rank, SUB, count), f32),
        ]

    def part(*tail):
        return pl.BlockSpec((chunk,) + tail, lambda n: (n,) + (0,) * len(tail))

    def whole(*shape):
        return pl.BlockSpec(shape, lambda n: (0,) * len(shape))

    grams, own_lift = pl.pallas_call(
        functools.partial(gram_kernel, steps),
        grid=(steps,),
        in_specs=[part(rank, points), part(rank, rank), whole(1, rank, rank)],
        out_specs=[whole(leaves + 1, rank, rank), whole(rank, rank)],
        out_shape=[
            jax.ShapeDtypeStruct((leaves + 1, rank, rank), f32),
            jax.ShapeDtypeStruct((rank, rank), f32),
        ],
        scratch_shapes=[pltpu.VMEM((rank, rank), f32)],
        compiler_params=params,
        cost_estimate=cost(10**9, 4 * 10**6),
        name="gram",
    )(leaf_basis, leaf_transfer, device_transfer)
    row_lifts = swaps(own_lift, "rows")
    factors = pl.pallas_call(
        factor_kernel,
        in_specs=[vmem],
        out_specs=vmem,
        out_shape=jax.ShapeDtypeStruct((leaves + 1, rank, 2 * rank), f32),
        scratch_shapes=scratch(leaves + 1),
        compiler_params=params,
        cost_estimate=cost(5 * 10**9, 8 * 10**6),
        name="factor",
    )(grams)
    sent, path = pl.pallas_call(
        functools.partial(branch_kernel, n_rows, n_leaf),
        grid=(1,),
        in_specs=[vmem] * (n_rows + 1)
        + [pl.BlockSpec((1, rank, 2 * rank), lambda n: (leaves, 0, 0))],
        out_specs=[vmem, vmem],
        out_shape=[
            jax.ShapeDtypeStruct((2, rank, rank), f32),
            jax.ShapeDtypeStruct((row_bits, rank, rank), f32),
        ],
        compiler_params=params,
        name="branch",
    )(own_lift, *row_lifts, upper_transfer, factors)
    others = swaps(sent, "leaf")
    leaf_orth, leaf_bridge, half = pl.pallas_call(
        leaf_kernel,
        grid=(steps,),
        in_specs=[
            part(rank, points),
            part(rank, rank),
            part(rank, rank),
            part(rank, 2 * rank),
            pl.BlockSpec((1, rank, 2 * rank), lambda n: (leaves, 0, 0)),
        ],
        out_specs=[part(rank, points), part(rank, rank), part(rank, rank)],
        out_shape=[
            jax.ShapeDtypeStruct(leaf_basis.shape, f32),
            jax.ShapeDtypeStruct(leaf_transfer.shape, f32),
            jax.ShapeDtypeStruct(couplings.shape, f32),
        ],
        compiler_params=params,
        cost_estimate=cost(5 * 10**9, 8 * 10**6),
        name="leaf",
    )(leaf_basis, leaf_transfer, couplings, factors, factors)
    new_transfers, coupled = pl.pallas_call(
        functools.partial(top_kernel, n_rows, n_leaf),
        grid=(1,),
        in_specs=[vmem] * (n_leaf + 3)
        + [pl.BlockSpec((1, rank, 2 * rank), lambda n: (leaves, 0, 0)), vmem, smem],
        out_specs=[vmem, vmem],
        out_shape=[
            jax.ShapeDtypeStruct((1, levels, rank, rank), f32),
            jax.ShapeDtypeStruct(couplings.shape, f32),
        ],
        scratch_shapes=[
            pltpu.VMEM((levels, rank, rank), f32),
            pltpu.VMEM((n_leaf, rank, rank), f32),
            pltpu.VMEM((levels, rank, 2 * rank), f32),
        ]
        + scratch(levels),
        compiler_params=params,
        name="top",
    )(sent, *others, upper_transfer, device_transfer, path, factors, half, couple_offset)
    return (leaf_orth, leaf_bridge, new_transfers, coupled)


def solution(mesh):
    in_specs = (
        P(("leaf", "rows"), None, None),
        P(("leaf", "rows"), None, None),
        P(("leaf", "rows"), None, None),
        P(),
        P(("leaf", "rows"), None, None),
        P(("leaf", "rows")),
    )
    out_specs = (
        P(("leaf", "rows"), None, None),
        P(("leaf", "rows"), None, None),
        P(("leaf", "rows"), None, None, None),
        P(("leaf", "rows"), None, None),
    )
    return jax.shard_map(
        per_device, mesh=mesh, in_specs=in_specs, out_specs=out_specs, check_vma=False
    )
```

time: 717 us -> 54.2 us (0.08)
  other arithmetic: 594 us -> 0 us
  blocking collectives: 45.2 us -> 0 us
  Pallas kernels: 0 us -> 33.9 us
  matrix products: 32.6 us -> 0 us
  local copies, waits for them, and re-layouts: 31.6 us -> 3.59 us
  starting transfers between devices: 2 us -> 14.4 us
    another operation x18 -> x0, other arithmetic: 587 us -> none  [the longest x3 191 us: per_device(): column_low = jnp.linalg.cholesky(column_grams)]
    all_gather x3 -> x0, blocking collectives: 45.2 us -> none  [the longest x1 33.3 us: per_device(): piece = lax.all_gather(row_grams, 'leaf', axis=0, tiled=True)]
    pallas_call x0 -> x5, Pallas kernels: none -> 33.9 us  [the longest x1 11.7 us: per_device(): pl.pallas_call(functools.partial(top_kernel, n_rows, n_leaf), grid=(1,),...]
    dot_general x18 -> x0, matrix products: 24.4 us -> none  [the longest x6 6.31 us: lift(): inner = jnp.einsum('nkl,nlj->nkj', grams, trans, precision=HIGH)]
    ppermute x3 -> x10, starting transfers between devices: 2 us -> 14.4 us  [swaps(): lax.ppermute(value, axis, [(source, source ^ mask) for source in range(si...]
    another operation x5 -> x0, local copies, waits for them, and re-layouts: 8.99 us -> none  [the longest x2 6.87 us: lower_solve(): return lax.linalg.triangular_solve(low, right, left_side=True, lower=True)]
    unnamed x47 -> x16, local copies, waits for them, and re-layouts: 12.3 us -> 3.59 us
    another operation x3 -> x0, matrix products: 8.16 us -> none  [lower_solve(): return lax.linalg.triangular_solve(low, right, left_side=True, lower=True)]
  transfers between devices with their start and end apart: 3 -> 10, of which waited for: 2 -> 1; matrix products, arithmetic and copies ran while one was open for 69% -> 0% of each run, Pallas kernels for 0% -> 24%
where the time goes in v1:
time: 54.2 us; the launch traced here: 54 us
  Pallas kernels  33.9 us (63%)
  starting transfers between devices  14.4 us (27%)
  local copies, waits for them, and re-layouts  3.59 us (7%)
  waiting for transfers between devices  1.39 us (3%)
  between operations  0.73 us (1%)
    ppermute x10, starting transfers between devices, swaps(): lax.ppermute(value, axis, [(source, source ^ mask) for source in range(si...  14.4 us
    pallas_call x1, Pallas kernels, per_device(): pl.pallas_call(functools.partial(top_kernel, n_rows, n_leaf), grid=(1,),...  11.7 us
    pallas_call x1, Pallas kernels, per_device(): pl.pallas_call(functools.partial(gram_kernel, steps), grid=(steps,), in_s...  8.31 us
    pallas_call x1, Pallas kernels, per_device(): pl.pallas_call(factor_kernel, in_specs=[vmem], out_specs=vmem, out_shape=...  7.55 us
    pallas_call x1, Pallas kernels, per_device(): pl.pallas_call(leaf_kernel, grid=(steps,), in_specs=[part(rank, points),...  5.63 us
    unnamed x16, local copies, waits for them, and re-layouts  3.59 us
    ppermute x10, waiting for transfers between devices, swaps(): lax.ppermute(value, axis, [(source, source ^ mask) for source in range(si...  1.39 us
  transfers between devices with their start and end apart: 10, of which 1 were waited for; matrix products, arithmetic and copies ran while one was open for 0% of the time, Pallas kernels for 24%

profile of v1, /device:TPU:0, one launch (start us, length us, event | category | flops | bytes accessed | tf_op | source)
XLA Modules:
  0.0 54.0 jit_solution(5562420108960402990)
XLA Ops:
  0.6 0.0 copy-start.1
  0.6 0.7 %copy-done.1 = f32[1,64,64]{2,1,0:T(8,128)S(1)} copy-done((f32[1,64,64]{2,1,0:T(8,128)S(1)}, f32[1,64,64]{2,1,0:T(8,128)}, u32[]{:S(2)}) %copy-start.1) | copy-done | bytes 16408
  1.4 1.6 %copy-done.4 = f32[32,64,256]{2,1,0:T(8,128)S(1)} copy-done((f32[32,64,256]{2,1,0:T(8,128)S(1)}, f32[32,64,256]{2,1,0:T(8,128)}, u32[]{:S(2)}) %copy-start.4) | copy-done | bytes 2097176
  3.0 1.2 %copy-done.6 = f32[32,64,64]{2,1,0:T(8,128)S(1)} copy-done((f32[32,64,64]{2,1,0:T(8,128)S(1)}, f32[32,64,64]{2,1,0:T(8,128)}, u32[]{:S(2)}) %copy-start.6) | copy-done | bytes 524312
  4.2 8.3 %gram.1 = (f32[33,64,64]{2,1,0:T(8,128)S(1)}, f32[64,64]{1,0:T(8,128)S(1)}) custom-call(f32[32,64,256]{2,1,0:T(8,128)S(1)} %copy-done.4, f32[32,64,64]{2,1,0:T(8,128)S(1)} %copy-done.6, f32[1,64,64]{2,1,0:T(8,128)S(1)} %copy-done.1), custom_call_target="tpu_custom_call" | custom-call | flops 1000000000 | bytes 4000000 | tf_op jit(solution)/shard_map/gram/pallas_call | solution.py:308
  12.5 0.5 collective-permute-start
  13.0 2.6 %collective-permute-start.1 = (f32[64,64]{1,0:T(8,128)S(1)}, f32[64,64]{1,0:T(8,128)S(1)}, u32[]{:S(2)}, u32[]{:S(2)}) collective-permute-start(f32[64,64]{1,0:T(8,128)S(1)} %get-tuple-element.16.refs_0_), channel_id=1, source_target_pairs={{0,2},{1,3},{2,0},{3,1},{4,6},{5,7},{6,4},{7,5},{8,10},{9,11},{10,... | collective-permute-start | bytes 49160 | tf_op jit(solution)/shard_map/ppermute | solution.py:270
  15.6 0.1 collective-permute-start.2
  15.7 7.5 %factor.1.factor_ref.own_ref.refs_5_.refs_11_ = f32[33,64,128]{2,1,0:T(8,128)S(1)} custom-call(f32[33,64,64]{2,1,0:T(8,128)S(1)} %get-tuple-element.13.grams_ref), custom_call_target="tpu_custom_call" | custom-call | flops 5000000000 | bytes 8000000 | tf_op jit(solution)/shard_map/factor/pallas_call | solution.py:323
  23.2 0.0 copy-start.5
  23.2 0.0 collective-permute-done.refs_1_
  23.3 0.7 %branch.1 = (f32[2,64,64]{2,1,0:T(8,128)S(1)}, f32[2,64,64]{2,1,0:T(8,128)S(1)}) custom-call(f32[64,64]{1,0:T(8,128)S(1)} %get-tuple-element.16.refs_0_, f32[64,64]{1,0:T(8,128)S(1)} %collective-permute-done.refs_1_, f32[64,64]{1,0:T(8,128)S(1)} %collective-permute-done.1.refs_2_, f32[64,64]{1,0:T(8,128)S(1)} %collective-permute-done.2.refs_3_, ...), custom_call_target="tpu_custom_call" | custom-call | tf_op jit(solution)/shard_map/branch/pallas_call | solution.py:333
  24.0 0.0 copy-start.3
  24.0 1.7 %collective-permute-start.3 = (f32[2,64,64]{2,1,0:T(8,128)S(1)}, f32[2,64,64]{2,1,0:T(8,128)S(1)}, u32[]{:S(2)}, u32[]{:S(2)}) collective-permute-start(f32[2,64,64]{2,1,0:T(8,128)S(1)} %get-tuple-element.17.refs_0_), channel_id=1, source_target_pairs={{0,4},{4,0},{8,12},{12,8},{16,20},{20,16},{24,28},{28,24},{1,5},{5... | collective-permute-start | bytes 98312 | tf_op jit(solution)/shard_map/ppermute | solution.py:270
  25.8 1.6 %collective-permute-start.4 = (f32[2,64,64]{2,1,0:T(8,128)S(1)}, f32[2,64,64]{2,1,0:T(8,128)S(1)}, u32[]{:S(2)}, u32[]{:S(2)}) collective-permute-start(f32[2,64,64]{2,1,0:T(8,128)S(1)} %get-tuple-element.17.refs_0_), channel_id=1, source_target_pairs={{0,8},{4,12},{8,0},{12,4},{16,24},{20,28},{24,16},{28,20},{1,9},{5... | collective-permute-start | bytes 98312 | tf_op jit(solution)/shard_map/ppermute | solution.py:270
  27.4 0.2 collective-permute-start.5
  27.6 2.8 %collective-permute-start.6 = (f32[2,64,64]{2,1,0:T(8,128)S(1)}, f32[2,64,64]{2,1,0:T(8,128)S(1)}, u32[]{:S(2)}, u32[]{:S(2)}) collective-permute-start(f32[2,64,64]{2,1,0:T(8,128)S(1)} %get-tuple-element.17.refs_0_), channel_id=1, source_target_pairs={{0,16},{4,20},{8,24},{12,28},{16,0},{20,4},{24,8},{28,12},{1,17},{... | collective-permute-start | bytes 98312 | tf_op jit(solution)/shard_map/ppermute | solution.py:270
  30.4 1.3 %collective-permute-start.7 = (f32[2,64,64]{2,1,0:T(8,128)S(1)}, f32[2,64,64]{2,1,0:T(8,128)S(1)}, u32[]{:S(2)}, u32[]{:S(2)}) collective-permute-start(f32[2,64,64]{2,1,0:T(8,128)S(1)} %get-tuple-element.17.refs_0_), channel_id=1, source_target_pairs={{0,20},{4,16},{8,28},{12,24},{16,4},{20,0},{24,12},{28,8},{1,21},{... | collective-permute-start | bytes 98312 | tf_op jit(solution)/shard_map/ppermute | solution.py:270
  31.6 0.0 collective-permute-done.3.refs_1_
  31.6 3.6 %collective-permute-start.8 = (f32[2,64,64]{2,1,0:T(8,128)S(1)}, f32[2,64,64]{2,1,0:T(8,128)S(1)}, u32[]{:S(2)}, u32[]{:S(2)}) collective-permute-start(f32[2,64,64]{2,1,0:T(8,128)S(1)} %get-tuple-element.17.refs_0_), channel_id=1, source_target_pairs={{0,24},{4,28},{8,16},{12,20},{16,8},{20,12},{24,0},{28,4},{1,25},{... | collective-permute-start | bytes 98312 | tf_op jit(solution)/shard_map/ppermute | solution.py:270
  35.2 0.0 collective-permute-start.9
  35.3 5.6 %leaf.1 = (f32[32,64,256]{2,1,0:T(8,128)}, f32[32,64,64]{2,1,0:T(8,128)}, f32[32,64,64]{2,1,0:T(8,128)S(1)}) custom-call(f32[32,64,256]{2,1,0:T(8,128)S(1)} %copy-done.5, f32[32,64,64]{2,1,0:T(8,128)S(1)} %copy-done.6, f32[32,64,64]{2,1,0:T(8,128)S(1)} %copy-done.7, f32[33,64,128]{2,1,0:T(8,128)S(1)} %factor.1.factor_ref.own_ref.refs_5_.refs_11_, ...), custom_call_target="tpu_custom_call" | custom-call | flops 5000000000 | bytes 8000000 | tf_op jit(solution)/shard_map/leaf/pallas_call | solution.py:347
  40.9 1.4 %collective-permute-done.9.refs_7_ = f32[2,64,64]{2,1,0:T(8,128)S(1)} collective-permute-done((f32[2,64,64]{2,1,0:T(8,128)S(1)}, f32[2,64,64]{2,1,0:T(8,128)S(1)}, u32[]{:S(2)}, u32[]{:S(2)}) %collective-permute-start.9) | collective-permute-done | bytes 32800 | tf_op jit(solution)/shard_map/ppermute | solution.py:270
  42.3 11.7 %top.1 = (f32[1,5,64,64]{3,2,1,0:T(8,128)}, f32[32,64,64]{2,1,0:T(8,128)}) custom-call(f32[2,64,64]{2,1,0:T(8,128)S(1)} %get-tuple-element.17.refs_0_, f32[2,64,64]{2,1,0:T(8,128)S(1)} %collective-permute-done.3.refs_1_, f32[2,64,64]{2,1,0:T(8,128)S(1)} %collective-permute-done.4.refs_2_, f32[2,64,64]{2,1,0:T(8,128)S(1)} %collective-permute-done.5.refs_3_, ...), custom_call_target="tpu_custom_call" | custom-call | tf_op jit(solution)/shard_map/top/pallas_call | solution.py:367
  (17 shorter events, 0.0 us)
Async XLA Ops:
  0.6 0.8 %copy-start.1 = (f32[1,64,64]{2,1,0:T(8,128)S(1)}, f32[1,64,64]{2,1,0:T(8,128)}, u32[]{:S(2)}) copy-start(f32[1,64,64]{2,1,0:T(8,128)} %refs_9_.1) | copy-start | bytes 49156
  1.4 1.6 %copy-start.4 = (f32[32,64,256]{2,1,0:T(8,128)S(1)}, f32[32,64,256]{2,1,0:T(8,128)}, u32[]{:S(2)}) copy-start(f32[32,64,256]{2,1,0:T(8,128)} %basis_ref.3) | copy-start | bytes 6291460
  3.0 1.2 %copy-start.6 = (f32[32,64,64]{2,1,0:T(8,128)S(1)}, f32[32,64,64]{2,1,0:T(8,128)}, u32[]{:S(2)}) copy-start(f32[32,64,64]{2,1,0:T(8,128)} %trans_ref.3) | copy-start | bytes 1572868
  12.5 10.7 %collective-permute-start = (f32[64,64]{1,0:T(8,128)S(1)}, f32[64,64]{1,0:T(8,128)S(1)}, u32[]{:S(2)}, u32[]{:S(2)}) collective-permute-start(f32[64,64]{1,0:T(8,128)S(1)} %get-tuple-element.16.refs_0_), channel_id=1, source_target_pairs={{0,1},{1,0},{2,3},{3,2},{4,5},{5,4},{6,7},{7,6},{8,9},{9,8},{10,11... | collective-permute-start | bytes 49160 | tf_op jit(solution)/shard_map/ppermute | solution.py:270
  13.0 10.2 %collective-permute-start.1 = (f32[64,64]{1,0:T(8,128)S(1)}, f32[64,64]{1,0:T(8,128)S(1)}, u32[]{:S(2)}, u32[]{:S(2)}) collective-permute-start(f32[64,64]{1,0:T(8,128)S(1)} %get-tuple-element.16.refs_0_), channel_id=1, source_target_pairs={{0,2},{1,3},{2,0},{3,1},{4,6},{5,7},{6,4},{7,5},{8,10},{9,11},{10,... | collective-permute-start | bytes 49160 | tf_op jit(solution)/shard_map/ppermute | solution.py:270
  15.6 7.7 %collective-permute-start.2 = (f32[64,64]{1,0:T(8,128)S(1)}, f32[64,64]{1,0:T(8,128)S(1)}, u32[]{:S(2)}, u32[]{:S(2)}) collective-permute-start(f32[64,64]{1,0:T(8,128)S(1)} %get-tuple-element.16.refs_0_), channel_id=1, source_target_pairs={{0,3},{1,2},{2,1},{3,0},{4,7},{5,6},{6,5},{7,4},{8,11},{9,10},{10,... | collective-permute-start | bytes 49160 | tf_op jit(solution)/shard_map/ppermute | solution.py:270
  15.6 7.6 %copy-start = (f32[30,64,64]{2,1,0:T(8,128)S(1)}, f32[30,64,64]{2,1,0:T(8,128)}, u32[]{:S(2)}) copy-start(f32[30,64,64]{2,1,0:T(8,128)} %refs_8_.1) | copy-start | bytes 1474564
  15.7 19.6 %copy-start.7 = (f32[32,64,64]{2,1,0:T(8,128)S(1)}, f32[32,64,64]{2,1,0:T(8,128)}, u32[]{:S(2)}) copy-start(f32[32,64,64]{2,1,0:T(8,128)} %coup_ref.1) | copy-start | bytes 1572868
  23.2 12.1 %copy-start.5 = (f32[32,64,256]{2,1,0:T(8,128)S(1)}, f32[32,64,256]{2,1,0:T(8,128)}, u32[]{:S(2)}) copy-start(f32[32,64,256]{2,1,0:T(8,128)} %basis_ref.3) | copy-start | bytes 6291460
  24.0 18.3 %copy-start.2 = (f32[1,64,64]{2,1,0:T(8,128)S(1)}, f32[1,64,64]{2,1,0:T(8,128)}, u32[]{:S(2)}) copy-start(f32[1,64,64]{2,1,0:T(8,128)} %refs_9_.1) | copy-start | bytes 49156
  24.0 18.3 %copy-start.3 = (s32[32]{0:T(128)S(1)}, s32[32]{0:T(128)}, u32[]{:S(2)}) copy-start(s32[32]{0:T(128)} %refs_13_.1) | copy-start | bytes 388
  24.0 7.6 %collective-permute-start.3 = (f32[2,64,64]{2,1,0:T(8,128)S(1)}, f32[2,64,64]{2,1,0:T(8,128)S(1)}, u32[]{:S(2)}, u32[]{:S(2)}) collective-permute-start(f32[2,64,64]{2,1,0:T(8,128)S(1)} %get-tuple-element.17.refs_0_), channel_id=1, source_target_pairs={{0,4},{4,0},{8,12},{12,8},{16,20},{20,16},{24,28},{28,24},{1,5},{5... | collective-permute-start | bytes 98312 | tf_op jit(solution)/shard_map/ppermute | solution.py:270
  25.8 9.5 %collective-permute-start.4 = (f32[2,64,64]{2,1,0:T(8,128)S(1)}, f32[2,64,64]{2,1,0:T(8,128)S(1)}, u32[]{:S(2)}, u32[]{:S(2)}) collective-permute-start(f32[2,64,64]{2,1,0:T(8,128)S(1)} %get-tuple-element.17.refs_0_), channel_id=1, source_target_pairs={{0,8},{4,12},{8,0},{12,4},{16,24},{20,28},{24,16},{28,20},{1,9},{5... | collective-permute-start | bytes 98312 | tf_op jit(solution)/shard_map/ppermute | solution.py:270
  27.4 13.6 %collective-permute-start.5 = (f32[2,64,64]{2,1,0:T(8,128)S(1)}, f32[2,64,64]{2,1,0:T(8,128)S(1)}, u32[]{:S(2)}, u32[]{:S(2)}) collective-permute-start(f32[2,64,64]{2,1,0:T(8,128)S(1)} %get-tuple-element.17.refs_0_), channel_id=1, source_target_pairs={{0,12},{4,8},{8,4},{12,0},{16,28},{20,24},{24,20},{28,16},{1,13},{... | collective-permute-start | bytes 98312 | tf_op jit(solution)/shard_map/ppermute | solution.py:270
  27.6 13.3 %collective-permute-start.6 = (f32[2,64,64]{2,1,0:T(8,128)S(1)}, f32[2,64,64]{2,1,0:T(8,128)S(1)}, u32[]{:S(2)}, u32[]{:S(2)}) collective-permute-start(f32[2,64,64]{2,1,0:T(8,128)S(1)} %get-tuple-element.17.refs_0_), channel_id=1, source_target_pairs={{0,16},{4,20},{8,24},{12,28},{16,0},{20,4},{24,8},{28,12},{1,17},{... | collective-permute-start | bytes 98312 | tf_op jit(solution)/shard_map/ppermute | solution.py:270
  30.4 10.6 %collective-permute-start.7 = (f32[2,64,64]{2,1,0:T(8,128)S(1)}, f32[2,64,64]{2,1,0:T(8,128)S(1)}, u32[]{:S(2)}, u32[]{:S(2)}) collective-permute-start(f32[2,64,64]{2,1,0:T(8,128)S(1)} %get-tuple-element.17.refs_0_), channel_id=1, source_target_pairs={{0,20},{4,16},{8,28},{12,24},{16,4},{20,0},{24,12},{28,8},{1,21},{... | collective-permute-start | bytes 98312 | tf_op jit(solution)/shard_map/ppermute | solution.py:270
  31.6 9.3 %collective-permute-start.8 = (f32[2,64,64]{2,1,0:T(8,128)S(1)}, f32[2,64,64]{2,1,0:T(8,128)S(1)}, u32[]{:S(2)}, u32[]{:S(2)}) collective-permute-start(f32[2,64,64]{2,1,0:T(8,128)S(1)} %get-tuple-element.17.refs_0_), channel_id=1, source_target_pairs={{0,24},{4,28},{8,16},{12,20},{16,8},{20,12},{24,0},{28,4},{1,25},{... | collective-permute-start | bytes 98312 | tf_op jit(solution)/shard_map/ppermute | solution.py:270
  35.2 7.1 %collective-permute-start.9 = (f32[2,64,64]{2,1,0:T(8,128)S(1)}, f32[2,64,64]{2,1,0:T(8,128)S(1)}, u32[]{:S(2)}, u32[]{:S(2)}) collective-permute-start(f32[2,64,64]{2,1,0:T(8,128)S(1)} %get-tuple-element.17.refs_0_), channel_id=1, source_target_pairs={{0,28},{4,24},{8,20},{12,16},{16,12},{20,8},{24,4},{28,0},{1,29},{... | collective-permute-start | bytes 98312 | tf_op jit(solution)/shard_map/ppermute | solution.py:270

commit v2 on v0

v2 whole, which is shorter than its diff:
```python
import functools

import jax
import jax.numpy as jnp
from jax import lax
from jax.experimental import pallas as pl
from jax.experimental.pallas import tpu as pltpu
from jax.sharding import PartitionSpec as P

HIGH = lax.Precision.HIGHEST
SUB = 8
LANES = 128
SET = LANES // SUB
F32 = jnp.float32
B16 = jnp.bfloat16


def mm(a, b, dims=((1,), (0,)), precision=None):
    return lax.dot_general(
        a, b, (dims, ((), ())), precision=precision, preferred_element_type=F32
    )


def mm_nt(a, b, precision=None):
    return mm(a, b, ((1,), (1,)), precision)


def mm_tn(a, b, precision=None):
    return mm(a, b, ((0,), (0,)), precision)


def lift(gram, trans):
    return mm_tn(trans, mm(gram, trans, precision=HIGH), HIGH)


def halves(x):
    high = x.astype(B16).astype(F32)
    return high, x - high


def pair(x):
    return jnp.concatenate(halves(x), axis=1).astype(B16)


def twice(x):
    return jnp.concatenate([x, x], axis=1)


def tall(x):
    high, low = halves(x)
    high, low = high.astype(B16), low.astype(B16)
    return jnp.concatenate([high, high, low, low], axis=0)


def broad(x):
    high, low = halves(x)
    return jnp.concatenate([high, high, low, low], axis=1).astype(B16)


def fold(x):
    half = x.shape[1] // 2
    return x[:, :half] + x[:, half:]


def spread(value, at):
    return jnp.broadcast_to(value[at : at + 1, :], (SUB, LANES))


def load_sets(flat, w_ref):
    sets, groups, rank = w_ref.shape[0], w_ref.shape[1], w_ref.shape[2]
    for t in range(sets):
        for ib in range(groups):
            rows = [
                flat[pl.ds(t * SET * rank + ib * SUB + s, SET, stride=rank), :]
                for s in range(SUB)
            ]
            w_ref[t, ib] = jnp.concatenate(rows, axis=0).T


def eliminate(w_ref, g_ref, out):
    sets, groups, rank = w_ref.shape[0], w_ref.shape[1], w_ref.shape[2]
    place = lax.broadcasted_iota(jnp.int32, (SUB, LANES), 0)
    lane = lax.broadcasted_iota(jnp.int32, (SUB, LANES), 1)
    group = lane // SET
    picks = [p * SET + lane % SET for p in range(SUB)]

    def tile(t, ib, jv):
        return w_ref[t, ib, pl.ds(jv * SUB, SUB), :]

    def picked(value, p):
        return jnp.take_along_axis(value, picks[p], axis=1, mode="promise_in_bounds")

    def corner(t, kb):
        diagonal = tile(t, kb, kb)
        rows = [picked(diagonal, p) for p in range(SUB)]
        inverses, roots = [], []
        for q in range(SUB):
            pivot = spread(rows[q], q)
            inverse = 1.0 / pivot
            root = lax.rsqrt(pivot)
            roots.append(root * (1.5 - 0.5 * pivot * root * root))
            inverses.append(inverse)
            scaled = rows[q] * inverse
            unit = jnp.where(place == q, 1.0, rows[q])
            for p in range(q + 1, SUB):
                kept = jnp.where(place == q, 0.0, rows[p])
                rows[p] = kept - spread(scaled, p) * unit
        return rows, inverses, roots

    def merged(parts):
        value = parts[0]
        for p in range(1, SUB):
            value = jnp.where(group == p, parts[p], value)
        return value

    def panel(t, kb, rows, inverses, roots):
        mult = {(p, q): spread(rows[p], q) for p in range(SUB) for q in range(p)}
        root = merged(roots)
        upper, lower = [], []
        for jv in range(groups):
            if jv == kb:
                for p in range(SUB):
                    unit = jnp.where(place == p, 1.0, 0.0)
                    g_ref[t, p, pl.ds(jv * SUB, SUB), :] = jnp.where(place < p, rows[p], unit)
                final = merged(rows) * root
                upper.append(jnp.where(place >= group, final, 0.0))
                unit = jnp.where(place == group, root, 0.0)
                lower.append(jnp.where(place < group, final, unit))
                continue
            value = tile(t, kb, jv)
            old = [picked(value, p) for p in range(SUB)]
            new = []
            for p in range(SUB):
                term = old[p]
                for q in range(p):
                    term = term + mult[p, q] * old[q]
                g_ref[t, p, pl.ds(jv * SUB, SUB), :] = term
                new.append(term)
            final = merged(new) * root
            zero = jnp.zeros((SUB, LANES), F32)
            upper.append(final if jv > kb else zero)
            lower.append(final if jv < kb else zero)
        return mult, jnp.concatenate(upper + lower, axis=0)

    def store(t, kb, factors):
        turned = factors.T
        for s in range(SUB):
            out[pl.ds(t * SET * rank + kb * SUB + s, SET, stride=rank), :] = turned[
                s * SET : (s + 1) * SET
            ]

    def weights(t, kb, ib, mult, inverses):
        value = tile(t, ib, kb)
        columns = [spread(value, q) for q in range(SUB)]
        found = []
        for q in range(SUB):
            term = columns[q]
            for r in range(q):
                term = term + mult[q, r] * columns[r]
            found.append(term * inverses[q])
        return found

    def trail(t, kb, ib, jv, found):
        acc = None if jv == kb else tile(t, ib, jv)
        for q in range(SUB):
            term = found[q] * g_ref[t, q, pl.ds(jv * SUB, SUB), :]
            acc = -term if acc is None else acc - term
        w_ref[t, ib, pl.ds(jv * SUB, SUB), :] = acc

    corners = [corner(t, 0) for t in range(sets)]
    for kb in range(groups):
        panels = [panel(t, kb, *corners[t]) for t in range(sets)]
        ahead = []
        if kb + 1 < groups:
            for t in range(sets):
                found = weights(t, kb, kb + 1, panels[t][0], corners[t][1])
                for jv in [kb + 1] + [jv for jv in range(groups) if jv != kb + 1]:
                    trail(t, kb, kb + 1, jv, found)
            ahead = [corner(t, kb + 1) for t in range(sets)]
        for t in range(sets):
            for ib in range(kb + 2, groups):
                found = weights(t, kb, ib, panels[t][0], corners[t][1])
                for jv in range(groups):
                    trail(t, kb, ib, jv, found)
            store(t, kb, panels[t][1])
        corners = ahead


def gram_kernel(
    steps,
    basis_hbm,
    trans_hbm,
    dev_ref,
    basis_ref,
    trans_ref,
    grams_ref,
    own_ref,
    lift_ref,
    basis_sem,
    trans_sem,
):
    leaves, rank = basis_ref.shape[0], basis_ref.shape[1]
    chunk = leaves // steps
    copies = []
    for step in range(steps):
        span = pl.ds(step * chunk, chunk)
        copies.append(
            (
                pltpu.make_async_copy(basis_hbm.at[span], basis_ref.at[span], basis_sem.at[step]),
                pltpu.make_async_copy(trans_hbm.at[span], trans_ref.at[span], trans_sem.at[step]),
            )
        )
        for copy in copies[-1]:
            copy.start()
    total = jnp.zeros((2 * rank, 2 * rank), F32)
    for step in range(steps):
        for copy in copies[step]:
            copy.wait()
        left, right = [], []
        for n in range(step * chunk, (step + 1) * chunk):
            basis = basis_ref[n]
            high, rest = halves(basis)
            middle, low = halves(rest)
            three = jnp.concatenate([high, middle, low], axis=0).astype(B16)
            product = mm_nt(three, three)
            rows = product[:rank] + product[rank : 2 * rank] + product[2 * rank :]
            gram = fold(rows[:, : 2 * rank]) + rows[:, 2 * rank :]
            grams_ref[n] = gram
            trans = pair(trans_ref[n])
            high, low = halves(gram)
            parts = mm(jnp.concatenate([high, low], axis=0).astype(B16), trans)
            left.append(trans)
            right.append(pair(fold(parts[:rank] + parts[rank:])))
        total = total + mm_tn(jnp.concatenate(left, axis=0), jnp.concatenate(right, axis=0))
    gram = fold(total[:rank] + total[rank:])
    own_ref[...] = gram
    lift_ref[...] = lift(gram, dev_ref[0])


def factor_kernel(grams_ref, out_ref, w_ref, g_ref):
    count, rank = grams_ref.shape[0], grams_ref.shape[1]
    load_sets(grams_ref.reshape(count * rank, rank), w_ref)
    eliminate(w_ref, g_ref, out_ref.reshape(count * rank, 2 * rank))


def branch_kernel(n_rows, n_leaf, *refs):
    own_ref, lift_ref = refs[:2]
    got = refs[2 : n_rows + 1]
    upper_ref, send_ref, path_ref = refs[n_rows + 1 :]
    branch, row = lax.axis_index("leaf"), lax.axis_index("rows")
    lifted = [lift_ref[...]] + [ref[...] for ref in got]
    level = (n_rows * n_leaf).bit_length() - 1
    node = branch * n_rows + row
    step = 0
    while len(lifted) > 1:
        grams = [lifted[2 * n] + lifted[2 * n + 1] for n in range(len(lifted) // 2)]
        level -= 1
        node = node >> 1
        path_ref[step] = grams[0]
        step += 1
        lifted = [
            lift(gram, upper_ref[2**level - 2 + (node ^ n)]) for n, gram in enumerate(grams)
        ]
    packed = jnp.concatenate([own_ref[...], lifted[0]], axis=1)
    for n in range(n_leaf):
        send_ref[n] = packed


def leaf_kernel(
    steps,
    basis_ref,
    trans_ref,
    coup_ref,
    factor_ref,
    orth_hbm,
    moved_ref,
    split_ref,
    orth_ref,
    orth_sem,
):
    leaves, rank = basis_ref.shape[0], basis_ref.shape[1]
    chunk = leaves // steps
    lane = lax.broadcasted_iota(jnp.int32, (rank, 2 * rank), 1)
    copies = []
    for step in range(steps):
        for n in range(step * chunk, (step + 1) * chunk):
            high, low = halves(factor_ref[n])
            low = jnp.concatenate([low[:, rank:], low[:, :rank]], axis=1)
            upper = jnp.where(lane < rank, high, low).astype(B16)
            inverse = jnp.where(lane < rank, low, high).astype(B16)
            orth_ref[n] = mm(twice(inverse), tall(basis_ref[n]))
            moved_ref[n] = pair(mm(twice(upper), tall(trans_ref[n])))
            split_ref[n] = pair(coup_ref[n])
        span = pl.ds(step * chunk, chunk)
        copy = pltpu.make_async_copy(orth_ref.at[span], orth_hbm.at[span], orth_sem.at[step])
        copy.start()
        copies.append(copy)
    for copy in copies:
        copy.wait()


def top_kernel(
    n_rows,
    n_leaf,
    steps,
    got_ref,
    upper_ref,
    dev_ref,
    path_ref,
    moved_ref,
    split_ref,
    offset_ref,
    fresh_ref,
    bridge_hbm,
    coupled_hbm,
    grams_ref,
    factor_ref,
    cols_ref,
    bridge_ref,
    coupled_ref,
    bridge_sem,
    coupled_sem,
    w_ref,
    g_ref,
):
    rank = got_ref.shape[1]
    row_bits = n_rows.bit_length() - 1
    leaf_bits = n_leaf.bit_length() - 1
    levels = row_bits + leaf_bits
    branch, row = lax.axis_index("leaf"), lax.axis_index("rows")
    myself = branch * n_rows + row
    for n in range(n_leaf):
        grams_ref[levels + n] = got_ref[n, :, :rank]
    for n in range(row_bits):
        grams_ref[n] = path_ref[n]
    lifted = [got_ref[branch ^ n, :, rank:] for n in range(n_leaf)]
    level, node, step = leaf_bits, branch, row_bits
    while len(lifted) > 1:
        grams = [lifted[2 * n] + lifted[2 * n + 1] for n in range(len(lifted) // 2)]
        level -= 1
        node = node >> 1
        grams_ref[step] = grams[0]
        step += 1
        if level == 0:
            break
        lifted = [
            lift(gram, upper_ref[2**level - 2 + (node ^ n)]) for n, gram in enumerate(grams)
        ]
    count = grams_ref.shape[0]
    load_sets(grams_ref.reshape(count * rank, rank), w_ref)
    eliminate(w_ref, g_ref, factor_ref.reshape(count * rank, 2 * rank))
    own = factor_ref[levels + branch]
    own_upper = twice(pair(own[:, :rank]))
    own_inverse = broad(own[:, rank:])
    for n in range(n_leaf):
        cols_ref[n] = broad(factor_ref[levels + n, :, :rank])
    copies = []
    leaves = moved_ref.shape[0]
    chunk = leaves // steps
    for step in range(steps):
        span = pl.ds(step * chunk, chunk)
        moved = twice(moved_ref[span].reshape(chunk * rank, 2 * rank))
        bridge_ref[span] = mm_nt(moved, own_inverse).reshape(chunk, rank, rank)
        copy = pltpu.make_async_copy(
            bridge_ref.at[span], bridge_hbm.at[span], bridge_sem.at[step]
        )
        copy.start()
        copies.append(copy)
    blocks = split_ref.shape[0]
    chunk = blocks // steps
    for step in range(steps):
        for b in range(step * chunk, (step + 1) * chunk):
            target = lax.rem(myself + offset_ref[b], n_rows * n_leaf)
            inner = mm_nt(twice(split_ref[b]), cols_ref[target // n_rows])
            coupled_ref[b] = mm(own_upper, tall(inner))
        span = pl.ds(step * chunk, chunk)
        copy = pltpu.make_async_copy(
            coupled_ref.at[span], coupled_hbm.at[span], coupled_sem.at[step]
        )
        copy.start()
        copies.append(copy)
    for k in range(levels):
        if k == 0:
            edge, low = dev_ref[0], own[:, :rank]
        else:
            edge = upper_ref[2 ** (levels - k) - 2 + (myself >> k)]
            low = factor_ref[k - 1, :, :rank]
        inner = mm(low, edge, precision=HIGH)
        fresh_ref[0, k] = mm_nt(inner, factor_ref[k, :, rank:], HIGH)
    for copy in copies:
        copy.wait()


def swaps(value, axis):
    size = lax.axis_size(axis)
    return [
        lax.ppermute(value, axis, [(source, source ^ mask) for source in range(size)])
        for mask in range(1, size)
    ]


def cost(flops, moved):
    return pl.CostEstimate(flops=flops, bytes_accessed=moved, transcendentals=0)


def per_device(
    leaf_basis, leaf_transfer, device_transfer, upper_transfer, couplings, couple_offset
):
    n_rows = lax.axis_size("rows")
    n_leaf = lax.axis_size("leaf")
    row_bits = n_rows.bit_length() - 1
    levels = row_bits + n_leaf.bit_length() - 1
    leaves, rank, _ = leaf_basis.shape
    blocks = couplings.shape[0]
    groups = rank // SUB
    params = pltpu.CompilerParams(vmem_limit_bytes=40 * 1024 * 1024)
    vmem = pl.BlockSpec(memory_space=pltpu.VMEM)
    smem = pl.BlockSpec(memory_space=pltpu.SMEM)
    hbm = pl.BlockSpec(memory_space=pltpu.HBM)
    steps = 4

    def like(array, kind=F32):
        return jax.ShapeDtypeStruct(array.shape, kind)

    def shape(*sizes, kind=F32):
        return jax.ShapeDtypeStruct(sizes, kind)

    def scratch(sets):
        return [
            pltpu.VMEM((sets, groups, rank, LANES), F32),
            pltpu.VMEM((sets, SUB, rank, LANES), F32),
        ]

    basis, trans, grams, own_gram, own_lift = pl.pallas_call(
        functools.partial(gram_kernel, steps),
        in_specs=[hbm, hbm, vmem],
        out_specs=[vmem] * 5,
        out_shape=[
            like(leaf_basis),
            like(leaf_transfer),
            shape(leaves, rank, rank),
            shape(rank, rank),
            shape(rank, rank),
        ],
        scratch_shapes=[pltpu.SemaphoreType.DMA((steps,)), pltpu.SemaphoreType.DMA((steps,))],
        compiler_params=params,
        cost_estimate=cost(10**9, 4 * 10**6),
        name="gram",
    )(leaf_basis, leaf_transfer, device_transfer)
    row_lifts = swaps(own_lift, "rows")
    factors = pl.pallas_call(
        factor_kernel,
        in_specs=[vmem],
        out_specs=vmem,
        out_shape=shape(leaves, rank, 2 * rank),
        scratch_shapes=scratch(leaves // SET),
        compiler_params=params,
        cost_estimate=cost(5 * 10**9, 8 * 10**6),
        name="factor",
    )(grams)
    sent, path = pl.pallas_call(
        functools.partial(branch_kernel, n_rows, n_leaf),
        in_specs=[vmem] * (n_rows + 2),
        out_specs=[vmem, vmem],
        out_shape=[shape(n_leaf, rank, 2 * rank), shape(row_bits, rank, rank)],
        compiler_params=params,
        name="branch",
    )(own_gram, own_lift, *row_lifts, upper_transfer)
    others = lax.all_to_all(sent, "leaf", split_axis=0, concat_axis=0, tiled=True)
    leaf_orth, moved, split = pl.pallas_call(
        functools.partial(leaf_kernel, steps),
        in_specs=[vmem] * 4,
        out_specs=[hbm, vmem, vmem],
        out_shape=[
            like(leaf_basis),
            shape(leaves, rank, 2 * rank, kind=B16),
            shape(blocks, rank, 2 * rank, kind=B16),
        ],
        scratch_shapes=[pltpu.VMEM(leaf_basis.shape, F32), pltpu.SemaphoreType.DMA((steps,))],
        compiler_params=params,
        cost_estimate=cost(5 * 10**9, 8 * 10**6),
        name="leaf",
    )(basis, trans, couplings, factors)
    sets = -(-(levels + n_leaf) // SET)
    new_transfers, leaf_bridge, coupled = pl.pallas_call(
        functools.partial(top_kernel, n_rows, n_leaf, steps),
        in_specs=[vmem] * 6 + [smem],
        out_specs=[vmem, hbm, hbm],
        out_shape=[
            shape(1, levels, rank, rank),
            like(leaf_transfer),
            like(couplings),
        ],
        scratch_shapes=[
            pltpu.VMEM((sets * SET, rank, rank), F32),
            pltpu.VMEM((sets * SET, rank, 2 * rank), F32),
            pltpu.VMEM((n_leaf, rank, 4 * rank), B16),
            pltpu.VMEM(leaf_transfer.shape, F32),
            pltpu.VMEM(couplings.shape, F32),
            pltpu.SemaphoreType.DMA((steps,)),
            pltpu.SemaphoreType.DMA((steps,)),
        ]
        + scratch(sets),
        compiler_params=params,
        name="top",
    )(others, upper_transfer, device_transfer, path, moved, split, couple_offset)
    return (leaf_orth, leaf_bridge, new_transfers, coupled)


def solution(mesh):
    in_specs = (
        P(("leaf", "rows"), None, None),
        P(("leaf", "rows"), None, None),
        P(("leaf", "rows"), None, None),
        P(),
        P(("leaf", "rows"), None, None),
        P(("leaf", "rows")),
    )
    out_specs = (
        P(("leaf", "rows"), None, None),
        P(("leaf", "rows"), None, None),
        P(("leaf", "rows"), None, None, None),
        P(("leaf", "rows"), None, None),
    )
    return jax.shard_map(
        per_device, mesh=mesh, in_specs=in_specs, out_specs=out_specs, check_vma=False
    )
```

time: 717 us -> 46.2 us (0.06)
  other arithmetic: 594 us -> 0 us
  blocking collectives: 45.2 us -> 0 us
  matrix products: 32.6 us -> 0 us
  Pallas kernels: 0 us -> 24.8 us
  local copies, waits for them, and re-layouts: 31.6 us -> 7.64 us
  starting transfers between devices: 2 us -> 9.2 us
    another operation x18 -> x0, other arithmetic: 587 us -> none  [the longest x3 191 us: per_device(): column_low = jnp.linalg.cholesky(column_grams)]
    all_gather x3 -> x0, blocking collectives: 45.2 us -> none  [the longest x1 33.3 us: per_device(): piece = lax.all_gather(row_grams, 'leaf', axis=0, tiled=True)]
    pallas_call x0 -> x5, Pallas kernels: none -> 24.8 us  [the longest x1 8.25 us: per_device(): pl.pallas_call(functools.partial(gram_kernel, steps), in_specs=[hbm, hbm,...]
    dot_general x18 -> x0, matrix products: 24.4 us -> none  [the longest x6 6.31 us: lift(): inner = jnp.einsum('nkl,nlj->nkj', grams, trans, precision=HIGH)]
    another operation x5 -> x0, local copies, waits for them, and re-layouts: 8.99 us -> none  [the longest x2 6.87 us: lower_solve(): return lax.linalg.triangular_solve(low, right, left_side=True, lower=True)]
    another operation x3 -> x0, matrix products: 8.16 us -> none  [lower_solve(): return lax.linalg.triangular_solve(low, right, left_side=True, lower=True)]
    ppermute x3, waiting for transfers between devices: 7.91 us -> 0.01 us  [swaps(): lax.ppermute(value, axis, [(source, source ^ mask) for source in range(si...]
  transfers between devices with their start and end apart: 3 -> 4, of which waited for: 2 -> 1; matrix products, arithmetic and copies ran while one was open for 69% -> 0% of each run, Pallas kernels for 0% -> 17%
where the time goes in v2:
time: 46.2 us; the launch traced here: 45.7 us
  Pallas kernels  24.8 us (54%)
  starting transfers between devices  9.2 us (20%)
  local copies, waits for them, and re-layouts  7.64 us (17%)
  waiting for transfers between devices  3.21 us (7%)
  between operations  0.92 us (2%)
    pallas_call x1, Pallas kernels, per_device(): pl.pallas_call(functools.partial(gram_kernel, steps), in_specs=[hbm, hbm,...  8.25 us
    unnamed x26, local copies, waits for them, and re-layouts  7.64 us
    pallas_call x1, Pallas kernels, per_device(): pl.pallas_call(functools.partial(top_kernel, n_rows, n_leaf, steps), in_s...  7.44 us
    all_to_all x1, starting transfers between devices, per_device(): lax.all_to_all(sent, 'leaf', split_axis=0, concat_axis=0, tiled=True)  6.02 us
    pallas_call x1, Pallas kernels, per_device(): pl.pallas_call(factor_kernel, in_specs=[vmem], out_specs=vmem, out_shape=...  5.39 us
    all_to_all x1, waiting for transfers between devices, per_device(): lax.all_to_all(sent, 'leaf', split_axis=0, concat_axis=0, tiled=True)  3.2 us
    ppermute x3, starting transfers between devices, swaps(): lax.ppermute(value, axis, [(source, source ^ mask) for source in range(si...  3.18 us
    pallas_call x1, Pallas kernels, per_device(): pl.pallas_call(functools.partial(leaf_kernel, steps), in_specs=[vmem] * 4...  2.16 us
  transfers between devices with their start and end apart: 4, of which 1 were waited for; matrix products, arithmetic and copies ran while one was open for 0% of the time, Pallas kernels for 17%

profile of v2, /device:TPU:0, one launch (start us, length us, event | category | flops | bytes accessed | tf_op | source)
XLA Modules:
  0.0 45.7 jit_solution(16790403207744920022)
XLA Ops:
  0.6 0.0 copy-start.1
  0.6 0.7 %copy-done.1 = f32[1,64,64]{2,1,0:T(8,128)S(1)} copy-done((f32[1,64,64]{2,1,0:T(8,128)S(1)}, f32[1,64,64]{2,1,0:T(8,128)}, u32[]{:S(2)}) %copy-start.1) | copy-done | bytes 16408
  1.4 1.6 %copy-done.4 = f32[32,64,256]{2,1,0:T(8,128)S(1)} copy-done((f32[32,64,256]{2,1,0:T(8,128)S(1)}, f32[32,64,256]{2,1,0:T(8,128)}, u32[]{:S(2)}) %copy-start.4) | copy-done | bytes 2097176
  3.0 1.2 %copy-done.5 = f32[32,64,64]{2,1,0:T(8,128)S(1)} copy-done((f32[32,64,64]{2,1,0:T(8,128)S(1)}, f32[32,64,64]{2,1,0:T(8,128)}, u32[]{:S(2)}) %copy-start.5) | copy-done | bytes 524312
  4.2 8.2 %gram.1 = (f32[32,64,256]{2,1,0:T(8,128)S(1)}, f32[32,64,64]{2,1,0:T(8,128)S(1)}, f32[32,64,64]{2,1,0:T(8,128)S(1)}, f32[64,64]{1,0:T(8,128)S(1)}, f32[64,64]{1,0:T(8,128)S(1)}) custom-call(f32[32,64,256]{2,1,0:T(8,128)S(1)} %copy-done.4, f32[32,64,64]{2,1,0:T(8,128)S(1)} %copy-done.5, f32[1,64,64]{2,1,0:T(8,128)S(1)} %copy-done.1), custom_call_target="tpu_custom_call" | custom-call | flops 1000000000 | bytes 4000000 | tf_op jit(solution)/shard_map/gram/pallas_call | solution.py:434
  12.5 0.0 copy-start.7
  12.5 0.0 copy-start.9
  12.5 0.5 %collective-permute-start = (f32[64,64]{1,0:T(8,128)S(1)}, f32[64,64]{1,0:T(8,128)S(1)}, u32[]{:S(2)}, u32[]{:S(2)}) collective-permute-start(f32[64,64]{1,0:T(8,128)S(1)} %get-tuple-element.22.refs_1_), channel_id=1, source_target_pairs={{0,1},{1,0},{2,3},{3,2},{4,5},{5,4},{6,7},{7,6},{8,9},{9,8},{10,11... | collective-permute-start | bytes 49160 | tf_op jit(solution)/shard_map/ppermute | solution.py:397
  13.0 2.6 %collective-permute-start.1 = (f32[64,64]{1,0:T(8,128)S(1)}, f32[64,64]{1,0:T(8,128)S(1)}, u32[]{:S(2)}, u32[]{:S(2)}) collective-permute-start(f32[64,64]{1,0:T(8,128)S(1)} %get-tuple-element.22.refs_1_), channel_id=1, source_target_pairs={{0,2},{1,3},{2,0},{3,1},{4,6},{5,7},{6,4},{7,5},{8,10},{9,11},{10,... | collective-permute-start | bytes 49160 | tf_op jit(solution)/shard_map/ppermute | solution.py:397
  15.6 0.1 collective-permute-start.2
  15.7 5.4 %factor.1.factor_ref = f32[32,64,128]{2,1,0:T(8,128)S(1)} custom-call(f32[32,64,64]{2,1,0:T(8,128)S(1)} %get-tuple-element.19.grams_ref), custom_call_target="tpu_custom_call" | custom-call | flops 5000000000 | bytes 8000000 | tf_op jit(solution)/shard_map/factor/pallas_call | solution.py:451
  21.1 0.0 copy-start.11
  21.1 0.0 collective-permute-done.refs_2_
  21.1 0.0 collective-permute-done.1.refs_3_
  21.1 0.0 collective-permute-done.2.refs_4_
  21.1 1.5 %branch.1 = (f32[8,64,128]{2,1,0:T(8,128)}, f32[2,64,64]{2,1,0:T(8,128)S(1)}) custom-call(f32[64,64]{1,0:T(8,128)S(1)} %get-tuple-element.21.refs_0_, f32[64,64]{1,0:T(8,128)S(1)} %get-tuple-element.22.refs_1_, f32[64,64]{1,0:T(8,128)S(1)} %collective-permute-done.refs_2_, f32[64,64]{1,0:T(8,128)S(1)} %collective-permute-done.1.refs_3_, ...), custom_call_target="tpu_custom_call" | custom-call | tf_op jit(solution)/shard_map/branch/pallas_call | solution.py:461
  22.7 6.0 %all-to-all-start = ((f32[8,64,128]{2,1,0:T(8,128)}), f32[8,64,128]{2,1,0:T(8,128)S(1)}, u32[]{:S(2)}, u32[]{:S(2)}) async-start(f32[8,64,128]{2,1,0:T(8,128)} %get-tuple-element.23), calls=%async_computation | async-start | bytes 524288 | tf_op jit(solution)/shard_map/all_to_all | solution.py:469
  28.7 0.0 copy-start.8
  28.7 1.6 %copy-done.8 = f32[32,64,256]{2,1,0:T(8,128)S(1)} copy-done((f32[32,64,256]{2,1,0:T(8,128)S(1)}, f32[32,64,256]{2,1,0:T(8,128)}, u32[]{:S(2)}) %copy-start.8) | copy-done | bytes 2097176
  30.3 1.2 %copy-done.10 = f32[32,64,64]{2,1,0:T(8,128)S(1)} copy-done((f32[32,64,64]{2,1,0:T(8,128)S(1)}, f32[32,64,64]{2,1,0:T(8,128)}, u32[]{:S(2)}) %copy-start.10) | copy-done | bytes 524312
  31.5 1.2 %copy-done.12 = f32[32,64,128]{2,1,0:T(8,128)S(1)} copy-done((f32[32,64,128]{2,1,0:T(8,128)S(1)}, f32[32,64,128]{2,1,0:T(8,128)}, u32[]{:S(2)}) %copy-start.12) | copy-done | bytes 1048600
  32.7 2.2 %leaf.1 = (f32[32,64,256]{2,1,0:T(8,128)}, bf16[32,64,128]{2,1,0:T(8,128)(2,1)S(1)}, bf16[32,64,128]{2,1,0:T(8,128)(2,1)S(1)}) custom-call(f32[32,64,256]{2,1,0:T(8,128)S(1)} %copy-done.8, f32[32,64,64]{2,1,0:T(8,128)S(1)} %copy-done.10, f32[32,64,64]{2,1,0:T(8,128)S(1)} %copy-done.6, f32[32,64,128]{2,1,0:T(8,128)S(1)} %copy-done.12), custom_call_target="tpu_custom_call" | custom-call | flops 5000000000 | bytes 8000000 | tf_op jit(solution)/shard_map/leaf/pallas_call | solution.py:470
  34.9 3.2 %all-to-all-done.got_ref = f32[8,64,128]{2,1,0:T(8,128)S(1)} async-done(((f32[8,64,128]{2,1,0:T(8,128)}), f32[8,64,128]{2,1,0:T(8,128)S(1)}, u32[]{:S(2)}, u32[]{:S(2)}) %all-to-all-start) | async-done | bytes 262176 | tf_op jit(solution)/shard_map/all_to_all | solution.py:469
  38.1 7.4 %top.1 = (f32[1,5,64,64]{3,2,1,0:T(8,128)}, f32[32,64,64]{2,1,0:T(8,128)}, f32[32,64,64]{2,1,0:T(8,128)}) custom-call(f32[8,64,128]{2,1,0:T(8,128)S(1)} %all-to-all-done.got_ref, f32[30,64,64]{2,1,0:T(8,128)S(1)} %copy-done, f32[1,64,64]{2,1,0:T(8,128)S(1)} %copy-done.2, f32[2,64,64]{2,1,0:T(8,128)S(1)} %get-tuple-element.24.path_ref, ...), custom_call_target="tpu_custom_call" | custom-call | tf_op jit(solution)/shard_map/top/pallas_call | solution.py:485
  (15 shorter events, 0.0 us)
Async XLA Ops:
  0.6 0.8 %copy-start.1 = (f32[1,64,64]{2,1,0:T(8,128)S(1)}, f32[1,64,64]{2,1,0:T(8,128)}, u32[]{:S(2)}) copy-start(f32[1,64,64]{2,1,0:T(8,128)} %dev_ref.3) | copy-start | bytes 49156
  1.4 1.6 %copy-start.4 = (f32[32,64,256]{2,1,0:T(8,128)S(1)}, f32[32,64,256]{2,1,0:T(8,128)}, u32[]{:S(2)}) copy-start(f32[32,64,256]{2,1,0:T(8,128)} %basis_hbm.1) | copy-start | bytes 6291460
  3.0 1.2 %copy-start.5 = (f32[32,64,64]{2,1,0:T(8,128)S(1)}, f32[32,64,64]{2,1,0:T(8,128)}, u32[]{:S(2)}) copy-start(f32[32,64,64]{2,1,0:T(8,128)} %trans_hbm.1) | copy-start | bytes 1572868
  12.5 8.6 %copy-start.7 = (f32[32,64,256]{2,1,0:T(8,128)}, f32[32,64,256]{2,1,0:T(8,128)S(1)}, u32[]{:S(2)}) copy-start(f32[32,64,256]{2,1,0:T(8,128)S(1)} %get-tuple-element.17.basis_ref) | copy-start | bytes 6291460
  12.5 8.6 %copy-start.9 = (f32[32,64,64]{2,1,0:T(8,128)}, f32[32,64,64]{2,1,0:T(8,128)S(1)}, u32[]{:S(2)}) copy-start(f32[32,64,64]{2,1,0:T(8,128)S(1)} %get-tuple-element.18.trans_ref) | copy-start | bytes 1572868
  12.5 8.6 %collective-permute-start = (f32[64,64]{1,0:T(8,128)S(1)}, f32[64,64]{1,0:T(8,128)S(1)}, u32[]{:S(2)}, u32[]{:S(2)}) collective-permute-start(f32[64,64]{1,0:T(8,128)S(1)} %get-tuple-element.22.refs_1_), channel_id=1, source_target_pairs={{0,1},{1,0},{2,3},{3,2},{4,5},{5,4},{6,7},{7,6},{8,9},{9,8},{10,11... | collective-permute-start | bytes 49160 | tf_op jit(solution)/shard_map/ppermute | solution.py:397
  13.0 8.1 %collective-permute-start.1 = (f32[64,64]{1,0:T(8,128)S(1)}, f32[64,64]{1,0:T(8,128)S(1)}, u32[]{:S(2)}, u32[]{:S(2)}) collective-permute-start(f32[64,64]{1,0:T(8,128)S(1)} %get-tuple-element.22.refs_1_), channel_id=1, source_target_pairs={{0,2},{1,3},{2,0},{3,1},{4,6},{5,7},{6,4},{7,5},{8,10},{9,11},{10,... | collective-permute-start | bytes 49160 | tf_op jit(solution)/shard_map/ppermute | solution.py:397
  15.6 5.5 %collective-permute-start.2 = (f32[64,64]{1,0:T(8,128)S(1)}, f32[64,64]{1,0:T(8,128)S(1)}, u32[]{:S(2)}, u32[]{:S(2)}) collective-permute-start(f32[64,64]{1,0:T(8,128)S(1)} %get-tuple-element.22.refs_1_), channel_id=1, source_target_pairs={{0,3},{1,2},{2,1},{3,0},{4,7},{5,6},{6,5},{7,4},{8,11},{9,10},{10,... | collective-permute-start | bytes 49160 | tf_op jit(solution)/shard_map/ppermute | solution.py:397
  15.7 5.5 %copy-start = (f32[30,64,64]{2,1,0:T(8,128)S(1)}, f32[30,64,64]{2,1,0:T(8,128)}, u32[]{:S(2)}) copy-start(f32[30,64,64]{2,1,0:T(8,128)} %upper_ref.1) | copy-start | bytes 1474564
  15.7 13.0 %copy-start.6 = (f32[32,64,64]{2,1,0:T(8,128)S(1)}, f32[32,64,64]{2,1,0:T(8,128)}, u32[]{:S(2)}) copy-start(f32[32,64,64]{2,1,0:T(8,128)} %coup_ref.1) | copy-start | bytes 1572868
  21.1 1.6 %copy-start.11 = (f32[32,64,128]{2,1,0:T(8,128)}, f32[32,64,128]{2,1,0:T(8,128)S(1)}, u32[]{:S(2)}) copy-start(f32[32,64,128]{2,1,0:T(8,128)S(1)} %factor.1.factor_ref) | copy-start | bytes 3145732
  22.7 15.4 %all-to-all-start = ((f32[8,64,128]{2,1,0:T(8,128)}), f32[8,64,128]{2,1,0:T(8,128)S(1)}, u32[]{:S(2)}, u32[]{:S(2)}) async-start(f32[8,64,128]{2,1,0:T(8,128)} %get-tuple-element.23), calls=%async_computation | async-start | bytes 524288 | tf_op jit(solution)/shard_map/all_to_all | solution.py:469
  28.7 1.6 %copy-start.8 = (f32[32,64,256]{2,1,0:T(8,128)S(1)}, f32[32,64,256]{2,1,0:T(8,128)}, u32[]{:S(2)}) copy-start(f32[32,64,256]{2,1,0:T(8,128)} %copy-done.7) | copy-start | bytes 6291460
  30.3 1.2 %copy-start.10 = (f32[32,64,64]{2,1,0:T(8,128)S(1)}, f32[32,64,64]{2,1,0:T(8,128)}, u32[]{:S(2)}) copy-start(f32[32,64,64]{2,1,0:T(8,128)} %copy-done.9) | copy-start | bytes 1572868
  31.5 1.2 %copy-start.12 = (f32[32,64,128]{2,1,0:T(8,128)S(1)}, f32[32,64,128]{2,1,0:T(8,128)}, u32[]{:S(2)}) copy-start(f32[32,64,128]{2,1,0:T(8,128)} %copy-done.11) | copy-start | bytes 3145732
  32.7 5.4 %copy-start.2 = (f32[1,64,64]{2,1,0:T(8,128)S(1)}, f32[1,64,64]{2,1,0:T(8,128)}, u32[]{:S(2)}) copy-start(f32[1,64,64]{2,1,0:T(8,128)} %dev_ref.3) | copy-start | bytes 49156
  32.7 5.4 %copy-start.3 = (s32[32]{0:T(128)S(1)}, s32[32]{0:T(128)}, u32[]{:S(2)}) copy-start(s32[32]{0:T(128)} %offset_ref.1) | copy-start | bytes 388

commit v3 on v2

--- a/solution.py
+++ b/solution.py
@@ -186,19 +186,19 @@
         corners = ahead
 
 
-def gram_kernel(
-    steps,
-    basis_hbm,
-    trans_hbm,
-    dev_ref,
-    basis_ref,
-    trans_ref,
-    grams_ref,
-    own_ref,
-    lift_ref,
-    basis_sem,
-    trans_sem,
-):
+def pack(x):
+    half = x.shape[0] // 2
+    return jnp.concatenate([x[:half], x[half:]], axis=1)
+
+
+def unpack(x):
+    half = x.shape[1] // 2
+    return jnp.concatenate([x[:, :half], x[:, half:]], axis=0)
+
+
+def gram_kernel(steps, sets, basis_hbm, trans_hbm, dev_ref, *refs):
+    grams_refs = refs[:sets]
+    own_ref, lift_ref, basis_ref, trans_ref, basis_sem, trans_sem = refs[sets:]
     leaves, rank = basis_ref.shape[0], basis_ref.shape[1]
     chunk = leaves // steps
     copies = []
@@ -225,7 +225,7 @@
             product = mm_nt(three, three)
             rows = product[:rank] + product[rank : 2 * rank] + product[2 * rank :]
             gram = fold(rows[:, : 2 * rank]) + rows[:, 2 * rank :]
-            grams_ref[n] = gram
+            grams_refs[n // SET][n % SET] = gram
             trans = pair(trans_ref[n])
             high, low = halves(gram)
             parts = mm(jnp.concatenate([high, low], axis=0).astype(B16), trans)
@@ -233,58 +233,55 @@
             right.append(pair(fold(parts[:rank] + parts[rank:])))
         total = total + mm_tn(jnp.concatenate(left, axis=0), jnp.concatenate(right, axis=0))
     gram = fold(total[:rank] + total[rank:])
-    own_ref[...] = gram
-    lift_ref[...] = lift(gram, dev_ref[0])
-
-
-def factor_kernel(grams_ref, out_ref, w_ref, g_ref):
+    own_ref[...] = pack(gram)
+    lift_ref[...] = pack(lift(gram, dev_ref[0]))
+
+
+def factor_kernel(grams_ref, after_ref, out_ref, token_ref, w_ref, g_ref):
+    del after_ref
     count, rank = grams_ref.shape[0], grams_ref.shape[1]
     load_sets(grams_ref.reshape(count * rank, rank), w_ref)
     eliminate(w_ref, g_ref, out_ref.reshape(count * rank, 2 * rank))
-
-
-def branch_kernel(n_rows, n_leaf, *refs):
-    own_ref, lift_ref = refs[:2]
-    got = refs[2 : n_rows + 1]
-    upper_ref, send_ref, path_ref = refs[n_rows + 1 :]
-    branch, row = lax.axis_index("leaf"), lax.axis_index("rows")
-    lifted = [lift_ref[...]] + [ref[...] for ref in got]
-    level = (n_rows * n_leaf).bit_length() - 1
-    node = branch * n_rows + row
-    step = 0
-    while len(lifted) > 1:
-        grams = [lifted[2 * n] + lifted[2 * n + 1] for n in range(len(lifted) // 2)]
-        level -= 1
-        node = node >> 1
-        path_ref[step] = grams[0]
-        step += 1
-        lifted = [
-            lift(gram, upper_ref[2**level - 2 + (node ^ n)]) for n, gram in enumerate(grams)
-        ]
-    packed = jnp.concatenate([own_ref[...], lifted[0]], axis=1)
-    for n in range(n_leaf):
-        send_ref[n] = packed
-
-
-def leaf_kernel(
-    steps,
-    basis_ref,
-    trans_ref,
-    coup_ref,
-    factor_ref,
-    orth_hbm,
-    moved_ref,
-    split_ref,
-    orth_ref,
-    orth_sem,
-):
+    token_ref[...] = jnp.zeros(token_ref.shape, F32)
+
+
+def row_hop_kernel(bit, last, mine_ref, got_ref, own_ref, upper_ref, path_ref, next_ref):
+    n_rows, n_leaf = lax.axis_size("rows"), lax.axis_size("leaf")
+    level = (n_rows * n_leaf).bit_length() - 2 - bit
+    myself = lax.axis_index("leaf") * n_rows + lax.axis_index("rows")
+    packed = mine_ref[...] + got_ref[...]
+    path_ref[...] = packed
+    lifted = pack(lift(unpack(packed), upper_ref[2**level - 2 + (myself >> (bit + 1))]))
+    if last:
+        next_ref[0] = lifted
+        next_ref[1] = own_ref[...]
+    else:
+        next_ref[...] = lifted
+
+
+def leaf_hop_kernel(bit, mine_ref, got_ref, upper_ref, after_ref, path_ref, next_ref):
+    del after_ref
+    level = lax.axis_size("leaf").bit_length() - 2 - bit
+    packed = mine_ref[0] + got_ref[0]
+    path_ref[...] = packed
+    node = lax.axis_index("leaf") >> (bit + 1)
+    next_ref[0] = pack(lift(unpack(packed), upper_ref[2**level - 2 + node]))
+    count = 2**bit
+    next_ref[1 : 1 + count] = mine_ref[1:]
+    next_ref[1 + count :] = got_ref[1:]
+
+
+def leaf_kernel(steps, sets, basis_ref, trans_ref, coup_ref, after_ref, *refs):
+    del after_ref
+    factor_refs = refs[:sets]
+    orth_hbm, moved_ref, split_ref, orth_ref, orth_sem = refs[sets:]
     leaves, rank = basis_ref.shape[0], basis_ref.shape[1]
     chunk = leaves // steps
     lane = lax.broadcasted_iota(jnp.int32, (rank, 2 * rank), 1)
     copies = []
     for step in range(steps):
         for n in range(step * chunk, (step + 1) * chunk):
-            high, low = halves(factor_ref[n])
+            high, low = halves(factor_refs[n // SET][n % SET])
             low = jnp.concatenate([low[:, rank:], low[:, :rank]], axis=1)
             upper = jnp.where(lane < rank, high, low).astype(B16)
             inverse = jnp.where(lane < rank, low, high).astype(B16)
@@ -299,57 +296,41 @@
         copy.wait()
 
 
-def top_kernel(
-    n_rows,
-    n_leaf,
-    steps,
-    got_ref,
-    upper_ref,
-    dev_ref,
-    path_ref,
-    moved_ref,
-    split_ref,
-    offset_ref,
-    fresh_ref,
-    bridge_hbm,
-    coupled_hbm,
-    grams_ref,
-    factor_ref,
-    cols_ref,
-    bridge_ref,
-    coupled_ref,
-    bridge_sem,
-    coupled_sem,
-    w_ref,
-    g_ref,
-):
-    rank = got_ref.shape[1]
-    row_bits = n_rows.bit_length() - 1
-    leaf_bits = n_leaf.bit_length() - 1
-    levels = row_bits + leaf_bits
+def top_kernel(n_rows, n_leaf, steps, mine_ref, got_ref, *refs):
+    levels = (n_rows * n_leaf).bit_length() - 1
+    path_refs = refs[: levels - 1]
+    (
+        upper_ref,
+        dev_ref,
+        moved_ref,
+        split_ref,
+        offset_ref,
+        fresh_ref,
+        bridge_hbm,
+        coupled_hbm,
+        grams_ref,
+        factor_ref,
+        cols_ref,
+        bridge_ref,
+        coupled_ref,
+        bridge_sem,
+        coupled_sem,
+        w_ref,
+        g_ref,
+    ) = refs[levels - 1 :]
+    rank = grams_ref.shape[1]
     branch, row = lax.axis_index("leaf"), lax.axis_index("rows")
     myself = branch * n_rows + row
-    for n in range(n_leaf):
-        grams_ref[levels + n] = got_ref[n, :, :rank]
-    for n in range(row_bits):
-        grams_ref[n] = path_ref[n]
-    lifted = [got_ref[branch ^ n, :, rank:] for n in range(n_leaf)]
-    level, node, step = leaf_bits, branch, row_bits
-    while len(lifted) > 1:
-        grams = [lifted[2 * n] + lifted[2 * n + 1] for n in range(len(lifted) // 2)]
-        level -= 1
-        node = node >> 1
-        grams_ref[step] = grams[0]
-        step += 1
-        if level == 0:
-            break
-        lifted = [
-            lift(gram, upper_ref[2**level - 2 + (node ^ n)]) for n, gram in enumerate(grams)
-        ]
+    for n in range(levels - 1):
+        grams_ref[n] = unpack(path_refs[n][...])
+    grams_ref[levels - 1] = unpack(mine_ref[0] + got_ref[0])
+    for n in range(n_leaf // 2):
+        grams_ref[levels + n] = unpack(mine_ref[1 + n])
+        grams_ref[levels + n_leaf // 2 + n] = unpack(got_ref[1 + n])
     count = grams_ref.shape[0]
     load_sets(grams_ref.reshape(count * rank, rank), w_ref)
     eliminate(w_ref, g_ref, factor_ref.reshape(count * rank, 2 * rank))
-    own = factor_ref[levels + branch]
+    own = factor_ref[levels]
     own_upper = twice(pair(own[:, :rank]))
     own_inverse = broad(own[:, rank:])
     for n in range(n_leaf):
@@ -371,7 +352,7 @@
     for step in range(steps):
         for b in range(step * chunk, (step + 1) * chunk):
             target = lax.rem(myself + offset_ref[b], n_rows * n_leaf)
-            inner = mm_nt(twice(split_ref[b]), cols_ref[target // n_rows])
+            inner = mm_nt(twice(split_ref[b]), cols_ref[(target // n_rows) ^ branch])
             coupled_ref[b] = mm(own_upper, tall(inner))
         span = pl.ds(step * chunk, chunk)
         copy = pltpu.make_async_copy(
@@ -391,12 +372,9 @@
         copy.wait()
 
 
-def swaps(value, axis):
-    size = lax.axis_size(axis)
-    return [
-        lax.ppermute(value, axis, [(source, source ^ mask) for source in range(size)])
-        for mask in range(1, size)
-    ]
+def swap(value, axis, bit):
+    pairs = [(source, source ^ 2**bit) for source in range(lax.axis_size(axis))]
+    return lax.ppermute(value, axis, pairs)
 
 
 def cost(flops, moved):
@@ -409,7 +387,8 @@
     n_rows = lax.axis_size("rows")
     n_leaf = lax.axis_size("leaf")
     row_bits = n_rows.bit_length() - 1
-    levels = row_bits + n_leaf.bit_length() - 1
+    leaf_bits = n_leaf.bit_length() - 1
+    levels = row_bits + leaf_bits
     leaves, rank, _ = leaf_basis.shape
     blocks = couplings.shape[0]
     groups = rank // SUB
@@ -431,45 +410,66 @@
             pltpu.VMEM((sets, SUB, rank, LANES), F32),
         ]
 
-    basis, trans, grams, own_gram, own_lift = pl.pallas_call(
-        functools.partial(gram_kernel, steps),
+    sets = leaves // SET
+    half = rank // 2
+    any_place = pl.BlockSpec(memory_space=pl.ANY)
+    *grams, own_gram, own_lift = pl.pallas_call(
+        functools.partial(gram_kernel, steps, sets),
         in_specs=[hbm, hbm, vmem],
-        out_specs=[vmem] * 5,
-        out_shape=[
-            like(leaf_basis),
-            like(leaf_transfer),
-            shape(leaves, rank, rank),
-            shape(rank, rank),
-            shape(rank, rank),
+        out_specs=[vmem] * (sets + 2),
+        out_shape=[shape(SET, rank, rank)] * sets + [shape(half, 2 * rank)] * 2,
+        scratch_shapes=[
+            pltpu.VMEM(leaf_basis.shape, F32),
+            pltpu.VMEM(leaf_transfer.shape, F32),
+            pltpu.SemaphoreType.DMA((steps,)),
+            pltpu.SemaphoreType.DMA((steps,)),
         ],
-        scratch_shapes=[pltpu.SemaphoreType.DMA((steps,)), pltpu.SemaphoreType.DMA((steps,))],
-        compiler_params=params,
+        compiler_params=pltpu.CompilerParams(vmem_limit_bytes=52 * 1024 * 1024),
         cost_estimate=cost(10**9, 4 * 10**6),
         name="gram",
     )(leaf_basis, leaf_transfer, device_transfer)
-    row_lifts = swaps(own_lift, "rows")
-    factors = pl.pallas_call(
-        factor_kernel,
-        in_specs=[vmem],
-        out_specs=vmem,
-        out_shape=shape(leaves, rank, 2 * rank),
-        scratch_shapes=scratch(leaves // SET),
-        compiler_params=params,
-        cost_estimate=cost(5 * 10**9, 8 * 10**6),
-        name="factor",
-    )(grams)
-    sent, path = pl.pallas_call(
-        functools.partial(branch_kernel, n_rows, n_leaf),
-        in_specs=[vmem] * (n_rows + 2),
-        out_specs=[vmem, vmem],
-        out_shape=[shape(n_leaf, rank, 2 * rank), shape(row_bits, rank, rank)],
-        compiler_params=params,
-        name="branch",
-    )(own_gram, own_lift, *row_lifts, upper_transfer)
-    others = lax.all_to_all(sent, "leaf", split_axis=0, concat_axis=0, tiled=True)
+    path = []
+    carry = own_lift
+    for bit in range(row_bits):
+        got = swap(carry, "rows", bit)
+        last = bit == row_bits - 1
+        gram, carry = pl.pallas_call(
+            functools.partial(row_hop_kernel, bit, last),
+            in_specs=[vmem] * 4,
+            out_specs=[vmem, vmem],
+            out_shape=[shape(half, 2 * rank), shape(*((2,) if last else ()), half, 2 * rank)],
+            compiler_params=params,
+            name="row_hop",
+        )(carry, got, own_gram, upper_transfer)
+        path.append(gram)
+    factors = []
+    for bit in range(leaf_bits - 1):
+        got = swap(carry, "leaf", bit)
+        if len(factors) < sets:
+            factor, token = pl.pallas_call(
+                factor_kernel,
+                in_specs=[vmem, any_place],
+                out_specs=[vmem, vmem],
+                out_shape=[shape(SET, rank, 2 * rank), shape(SUB, LANES)],
+                scratch_shapes=scratch(1),
+                compiler_params=params,
+                cost_estimate=cost(5 * 10**9, 8 * 10**6),
+                name="factor",
+            )(grams[len(factors)], carry)
+            factors.append(factor)
+        gram, carry = pl.pallas_call(
+            functools.partial(leaf_hop_kernel, bit),
+            in_specs=[vmem] * 3 + [any_place],
+            out_specs=[vmem, vmem],
+            out_shape=[shape(half, 2 * rank), shape(1 + 2 ** (bit + 1), half, 2 * rank)],
+            compiler_params=params,
+            name="leaf_hop",
+        )(carry, got, upper_transfer, token)
+        path.append(gram)
+    got = swap(carry, "leaf", leaf_bits - 1)
     leaf_orth, moved, split = pl.pallas_call(
-        functools.partial(leaf_kernel, steps),
-        in_specs=[vmem] * 4,
+        functools.partial(leaf_kernel, steps, sets),
+        in_specs=[vmem] * 3 + [any_place] + [vmem] * sets,
         out_specs=[hbm, vmem, vmem],
         out_shape=[
             like(leaf_basis),
@@ -480,11 +480,11 @@
         compiler_params=params,
         cost_estimate=cost(5 * 10**9, 8 * 10**6),
         name="leaf",
-    )(basis, trans, couplings, factors)
+    )(leaf_basis, leaf_transfer, couplings, carry, *factors)
     sets = -(-(levels + n_leaf) // SET)
     new_transfers, leaf_bridge, coupled = pl.pallas_call(
         functools.partial(top_kernel, n_rows, n_leaf, steps),
-        in_specs=[vmem] * 6 + [smem],
+        in_specs=[vmem] * (levels + 5) + [smem],
         out_specs=[vmem, hbm, hbm],
         out_shape=[
             shape(1, levels, rank, rank),
@@ -503,7 +503,7 @@
         + scratch(sets),
         compiler_params=params,
         name="top",
-    )(others, upper_transfer, device_transfer, path, moved, split, couple_offset)
+    )(carry, got, *path, upper_transfer, device_transfer, moved, split, couple_offset)
     return (leaf_orth, leaf_bridge, new_transfers, coupled)
 
 

time: 46.2 us -> 39.6 us (0.86)
  local copies, waits for them, and re-layouts: 7.64 us -> 0.85 us
  starting transfers between devices: 9.2 us -> 9.79 us
    unnamed x26 -> x12, local copies, waits for them, and re-layouts: 7.64 us -> 0.85 us
    ppermute x3 -> x5, starting transfers between devices: 3.18 us -> 9.79 us  [swap(): return lax.ppermute(value, axis, pairs)]
    all_to_all x1 -> x0, starting transfers between devices: 6.02 us -> none  [per_device(): lax.all_to_all(sent, 'leaf', split_axis=0, concat_axis=0, tiled=True)]
    all_to_all x1 -> x0, waiting for transfers between devices: 3.2 us -> none  [per_device(): lax.all_to_all(sent, 'leaf', split_axis=0, concat_axis=0, tiled=True)]
    ppermute x3 -> x5, waiting for transfers between devices: 0.01 us -> 3.13 us  [swap(): return lax.ppermute(value, axis, pairs)]
    pallas_call x4 -> x8, Pallas kernels: 17.3 us -> 18.3 us  [the longest x1 9.2 us: per_device(): pl.pallas_call(functools.partial(gram_kernel, steps, sets), in_specs=[hbm...]
    pallas_call x1, Pallas kernels: 7.44 us -> 6.48 us  [per_device(): pl.pallas_call(functools.partial(top_kernel, n_rows, n_leaf, steps), in_s...]
  transfers between devices with their start and end apart: 4 -> 5, of which waited for: 1 -> 3; matrix products, arithmetic and copies ran while one was open for 0% -> 0% of each run, Pallas kernels for 17% -> 19%
where the time goes in v3:
time: 39.6 us; the launch traced here: 39.5 us
  Pallas kernels  24.8 us (63%)
  starting transfers between devices  9.79 us (25%)
  waiting for transfers between devices  3.13 us (8%)
  between operations  0.9 us (2%)
  local copies, waits for them, and re-layouts  0.85 us (2%)
    ppermute x5, starting transfers between devices, swap(): return lax.ppermute(value, axis, pairs)  9.79 us
    pallas_call x1, Pallas kernels, per_device(): pl.pallas_call(functools.partial(gram_kernel, steps, sets), in_specs=[hbm...  9.2 us
    pallas_call x1, Pallas kernels, per_device(): pl.pallas_call(functools.partial(top_kernel, n_rows, n_leaf, steps), in_s...  6.48 us
    pallas_call x2, Pallas kernels, per_device(): pl.pallas_call(factor_kernel, in_specs=[vmem, any_place], out_specs=[vmem...  5.31 us
    ppermute x5, waiting for transfers between devices, swap(): return lax.ppermute(value, axis, pairs)  3.13 us
    pallas_call x1, Pallas kernels, per_device(): pl.pallas_call(functools.partial(leaf_kernel, steps, sets), in_specs=[vme...  2.17 us
    unnamed x12, local copies, waits for them, and re-layouts  0.85 us
    pallas_call x2, Pallas kernels, per_device(): pl.pallas_call(functools.partial(leaf_hop_kernel, bit), in_specs=[vmem] *...  0.82 us
  transfers between devices with their start and end apart: 5, of which 3 were waited for; matrix products, arithmetic and copies ran while one was open for 0% of the time, Pallas kernels for 19%

profile of v3, /device:TPU:0, one launch (start us, length us, event | category | flops | bytes accessed | tf_op | source)
XLA Modules:
  0.0 39.5 jit_solution(11231869334147683158)
XLA Ops:
  0.6 0.0 copy-start
  0.7 0.8 %copy-done.1 = f32[1,64,64]{2,1,0:T(8,128)S(1)} copy-done((f32[1,64,64]{2,1,0:T(8,128)S(1)}, f32[1,64,64]{2,1,0:T(8,128)}, u32[]{:S(2)}) %copy-start.1) | copy-done | bytes 16408
  1.5 9.2 %gram.1 = (f32[16,64,64]{2,1,0:T(8,128)S(1)}, f32[16,64,64]{2,1,0:T(8,128)S(1)}, f32[32,128]{1,0:T(8,128)S(1)}, f32[32,128]{1,0:T(8,128)S(1)}) custom-call(f32[32,64,256]{2,1,0:T(8,128)} %basis_ref.1, f32[32,64,64]{2,1,0:T(8,128)} %trans_ref.1, f32[1,64,64]{2,1,0:T(8,128)S(1)} %copy-done.1), custom_call_target="tpu_custom_call" | custom-call | flops 1000000000 | bytes 4000000 | tf_op jit(solution)/shard_map/gram/pallas_call | solution.py:416
  10.7 0.5 %collective-permute-start = (f32[32,128]{1,0:T(8,128)S(1)}, f32[32,128]{1,0:T(8,128)S(1)}, u32[]{:S(2)}, u32[]{:S(2)}) collective-permute-start(f32[32,128]{1,0:T(8,128)S(1)} %get-tuple-element.26.mine_ref), channel_id=1, source_target_pairs={{0,1},{1,0},{2,3},{3,2},{4,5},{5,4},{6,7},{7,6},{8,9},{9,8},{10,11... | collective-permute-start | bytes 49160 | tf_op jit(solution)/shard_map/ppermute | solution.py:377
  11.2 0.8 %collective-permute-done.got_ref = f32[32,128]{1,0:T(8,128)S(1)} collective-permute-done((f32[32,128]{1,0:T(8,128)S(1)}, f32[32,128]{1,0:T(8,128)S(1)}, u32[]{:S(2)}, u32[]{:S(2)}) %collective-permute-start) | collective-permute-done | bytes 16416 | tf_op jit(solution)/shard_map/ppermute | solution.py:377
  12.1 0.4 %row_hop.2 = (f32[32,128]{1,0:T(8,128)S(1)}, f32[32,128]{1,0:T(8,128)S(1)}) custom-call(f32[32,128]{1,0:T(8,128)S(1)} %get-tuple-element.26.mine_ref, f32[32,128]{1,0:T(8,128)S(1)} %collective-permute-done.got_ref, f32[32,128]{1,0:T(8,128)S(1)} %get-tuple-element.27.own_ref, f32[30,64,64]{2,1,0:T(8,128)S(1)} %copy-done), custom_call_target="tpu_custom_call" | custom-call | tf_op jit(solution)/shard_map/row_hop/pallas_call | solution.py:436
  12.5 2.9 %collective-permute-start.1 = (f32[32,128]{1,0:T(8,128)S(1)}, f32[32,128]{1,0:T(8,128)S(1)}, u32[]{:S(2)}, u32[]{:S(2)}) collective-permute-start(f32[32,128]{1,0:T(8,128)S(1)} %get-tuple-element.28.mine_ref), channel_id=1, source_target_pairs={{0,2},{1,3},{2,0},{3,1},{4,6},{5,7},{6,4},{7,5},{8,10},{9,11},{10,... | collective-permute-start | bytes 49160 | tf_op jit(solution)/shard_map/ppermute | solution.py:377
  15.4 1.7 %collective-permute-done.1.got_ref = f32[32,128]{1,0:T(8,128)S(1)} collective-permute-done((f32[32,128]{1,0:T(8,128)S(1)}, f32[32,128]{1,0:T(8,128)S(1)}, u32[]{:S(2)}, u32[]{:S(2)}) %collective-permute-start.1) | collective-permute-done | bytes 16416 | tf_op jit(solution)/shard_map/ppermute | solution.py:377
  17.1 0.4 %row_hop.3 = (f32[32,128]{1,0:T(8,128)S(1)}, f32[2,32,128]{2,1,0:T(8,128)S(1)}) custom-call(f32[32,128]{1,0:T(8,128)S(1)} %get-tuple-element.28.mine_ref, f32[32,128]{1,0:T(8,128)S(1)} %collective-permute-done.1.got_ref, f32[32,128]{1,0:T(8,128)S(1)} %get-tuple-element.27.own_ref, f32[30,64,64]{2,1,0:T(8,128)S(1)} %copy-done), custom_call_target="tpu_custom_call" | custom-call | tf_op jit(solution)/shard_map/row_hop/pallas_call | solution.py:436
  17.5 2.1 %collective-permute-start.2 = (f32[2,32,128]{2,1,0:T(8,128)S(1)}, f32[2,32,128]{2,1,0:T(8,128)S(1)}, u32[]{:S(2)}, u32[]{:S(2)}) collective-permute-start(f32[2,32,128]{2,1,0:T(8,128)S(1)} %get-tuple-element.29.after_ref.mine_ref), channel_id=1, source_target_pairs={{0,4},{4,0},{8,12},{12,8},{16,20},{20,16},{24,28},{28,24},{1,5},{5... | collective-permute-start | bytes 98312 | tf_op jit(solution)/shard_map/ppermute | solution.py:377
  19.6 2.7 %factor.2 = (f32[16,64,128]{2,1,0:T(8,128)S(1)}, f32[8,128]{1,0:T(8,128)S(1)}) custom-call(f32[16,64,64]{2,1,0:T(8,128)S(1)} %get-tuple-element.30.grams_ref, f32[2,32,128]{2,1,0:T(8,128)S(1)} %get-tuple-element.29.after_ref.mine_ref), custom_call_target="tpu_custom_call" | custom-call | flops 5000000000 | bytes 8000000 | tf_op jit(solution)/shard_map/factor/pallas_call | solution.py:449
  22.2 0.0 collective-permute-done.2.got_ref
  22.3 0.4 %leaf_hop.2 = (f32[32,128]{1,0:T(8,128)S(1)}, f32[3,32,128]{2,1,0:T(8,128)S(1)}) custom-call(f32[2,32,128]{2,1,0:T(8,128)S(1)} %get-tuple-element.29.after_ref.mine_ref, f32[2,32,128]{2,1,0:T(8,128)S(1)} %collective-permute-done.2.got_ref, f32[30,64,64]{2,1,0:T(8,128)S(1)} %copy-done, f32[8,128]{1,0:T(8,128)S(1)} %get-tuple-element.31.after_ref), custom_call_target="tpu_custom_call" | custom-call | tf_op jit(solution)/shard_map/leaf_hop/pallas_call | solution.py:460
  22.7 1.6 %collective-permute-start.3 = (f32[3,32,128]{2,1,0:T(8,128)S(1)}, f32[3,32,128]{2,1,0:T(8,128)S(1)}, u32[]{:S(2)}, u32[]{:S(2)}) collective-permute-start(f32[3,32,128]{2,1,0:T(8,128)S(1)} %get-tuple-element.32.after_ref.mine_ref), channel_id=1, source_target_pairs={{0,8},{4,12},{8,0},{12,4},{16,24},{20,28},{24,16},{28,20},{1,9},{5... | collective-permute-start | bytes 147464 | tf_op jit(solution)/shard_map/ppermute | solution.py:377
  24.3 2.7 %factor.3 = (f32[16,64,128]{2,1,0:T(8,128)S(1)}, f32[8,128]{1,0:T(8,128)S(1)}) custom-call(f32[16,64,64]{2,1,0:T(8,128)S(1)} %get-tuple-element.33.grams_ref, f32[3,32,128]{2,1,0:T(8,128)S(1)} %get-tuple-element.32.after_ref.mine_ref), custom_call_target="tpu_custom_call" | custom-call | flops 5000000000 | bytes 8000000 | tf_op jit(solution)/shard_map/factor/pallas_call | solution.py:449
  27.0 0.0 collective-permute-done.3.got_ref
  27.0 0.4 %leaf_hop.3 = (f32[32,128]{1,0:T(8,128)S(1)}, f32[5,32,128]{2,1,0:T(8,128)S(1)}) custom-call(f32[3,32,128]{2,1,0:T(8,128)S(1)} %get-tuple-element.32.after_ref.mine_ref, f32[3,32,128]{2,1,0:T(8,128)S(1)} %collective-permute-done.3.got_ref, f32[30,64,64]{2,1,0:T(8,128)S(1)} %copy-done, f32[8,128]{1,0:T(8,128)S(1)} %get-tuple-element.34.after_ref), custom_call_target="tpu_custom_call" | custom-call | tf_op jit(solution)/shard_map/leaf_hop/pallas_call | solution.py:460
  27.4 2.7 %collective-permute-start.4 = (f32[5,32,128]{2,1,0:T(8,128)S(1)}, f32[5,32,128]{2,1,0:T(8,128)S(1)}, u32[]{:S(2)}, u32[]{:S(2)}) collective-permute-start(f32[5,32,128]{2,1,0:T(8,128)S(1)} %get-tuple-element.35.after_ref.mine_ref), channel_id=1, source_target_pairs={{0,16},{4,20},{8,24},{12,28},{16,0},{20,4},{24,8},{28,12},{1,17},{... | collective-permute-start | bytes 245768 | tf_op jit(solution)/shard_map/ppermute | solution.py:377
  30.1 0.0 copy-done.3
  30.1 0.0 copy-done.5
  30.1 2.2 %leaf.1 = (f32[32,64,256]{2,1,0:T(8,128)}, bf16[32,64,128]{2,1,0:T(8,128)(2,1)S(1)}, bf16[32,64,128]{2,1,0:T(8,128)(2,1)S(1)}) custom-call(f32[32,64,256]{2,1,0:T(8,128)S(1)} %copy-done.3, f32[32,64,64]{2,1,0:T(8,128)S(1)} %copy-done.4, f32[32,64,64]{2,1,0:T(8,128)S(1)} %copy-done.5, f32[5,32,128]{2,1,0:T(8,128)S(1)} %get-tuple-element.35.after_ref.mine_ref, ...), custom_call_target="tpu_custom_call" | custom-call | flops 5000000000 | bytes 8000000 | tf_op jit(solution)/shard_map/leaf/pallas_call | solution.py:470
  32.3 0.6 %collective-permute-done.4.got_ref = f32[5,32,128]{2,1,0:T(8,128)S(1)} collective-permute-done((f32[5,32,128]{2,1,0:T(8,128)S(1)}, f32[5,32,128]{2,1,0:T(8,128)S(1)}, u32[]{:S(2)}, u32[]{:S(2)}) %collective-permute-start.4) | collective-permute-done | bytes 81952 | tf_op jit(solution)/shard_map/ppermute | solution.py:377
  32.8 0.0 copy-done.2
  32.8 6.5 %top.1 = (f32[1,5,64,64]{3,2,1,0:T(8,128)}, f32[32,64,64]{2,1,0:T(8,128)}, f32[32,64,64]{2,1,0:T(8,128)}) custom-call(f32[5,32,128]{2,1,0:T(8,128)S(1)} %get-tuple-element.35.after_ref.mine_ref, f32[5,32,128]{2,1,0:T(8,128)S(1)} %collective-permute-done.4.got_ref, f32[32,128]{1,0:T(8,128)S(1)} %get-tuple-element.39.refs_0_, ...), custom_call_target="tpu_custom_call" | custom-call | tf_op jit(solution)/shard_map/top/pallas_call | solution.py:485
  (7 shorter events, 0.0 us)
Async XLA Ops:
  0.6 11.4 %copy-start = (f32[30,64,64]{2,1,0:T(8,128)S(1)}, f32[30,64,64]{2,1,0:T(8,128)}, u32[]{:S(2)}) copy-start(f32[30,64,64]{2,1,0:T(8,128)} %refs_4_.1) | copy-start | bytes 1474564
  0.6 0.8 %copy-start.1 = (f32[1,64,64]{2,1,0:T(8,128)S(1)}, f32[1,64,64]{2,1,0:T(8,128)}, u32[]{:S(2)}) copy-start(f32[1,64,64]{2,1,0:T(8,128)} %refs_5_.1) | copy-start | bytes 49156
  10.7 1.4 %collective-permute-start = (f32[32,128]{1,0:T(8,128)S(1)}, f32[32,128]{1,0:T(8,128)S(1)}, u32[]{:S(2)}, u32[]{:S(2)}) collective-permute-start(f32[32,128]{1,0:T(8,128)S(1)} %get-tuple-element.26.mine_ref), channel_id=1, source_target_pairs={{0,1},{1,0},{2,3},{3,2},{4,5},{5,4},{6,7},{7,6},{8,9},{9,8},{10,11... | collective-permute-start | bytes 49160 | tf_op jit(solution)/shard_map/ppermute | solution.py:377
  12.5 4.6 %collective-permute-start.1 = (f32[32,128]{1,0:T(8,128)S(1)}, f32[32,128]{1,0:T(8,128)S(1)}, u32[]{:S(2)}, u32[]{:S(2)}) collective-permute-start(f32[32,128]{1,0:T(8,128)S(1)} %get-tuple-element.28.mine_ref), channel_id=1, source_target_pairs={{0,2},{1,3},{2,0},{3,1},{4,6},{5,7},{6,4},{7,5},{8,10},{9,11},{10,... | collective-permute-start | bytes 49160 | tf_op jit(solution)/shard_map/ppermute | solution.py:377
  17.5 4.7 %collective-permute-start.2 = (f32[2,32,128]{2,1,0:T(8,128)S(1)}, f32[2,32,128]{2,1,0:T(8,128)S(1)}, u32[]{:S(2)}, u32[]{:S(2)}) collective-permute-start(f32[2,32,128]{2,1,0:T(8,128)S(1)} %get-tuple-element.29.after_ref.mine_ref), channel_id=1, source_target_pairs={{0,4},{4,0},{8,12},{12,8},{16,20},{20,16},{24,28},{28,24},{1,5},{5... | collective-permute-start | bytes 98312 | tf_op jit(solution)/shard_map/ppermute | solution.py:377
  22.7 4.3 %collective-permute-start.3 = (f32[3,32,128]{2,1,0:T(8,128)S(1)}, f32[3,32,128]{2,1,0:T(8,128)S(1)}, u32[]{:S(2)}, u32[]{:S(2)}) collective-permute-start(f32[3,32,128]{2,1,0:T(8,128)S(1)} %get-tuple-element.32.after_ref.mine_ref), channel_id=1, source_target_pairs={{0,8},{4,12},{8,0},{12,4},{16,24},{20,28},{24,16},{28,20},{1,9},{5... | collective-permute-start | bytes 147464 | tf_op jit(solution)/shard_map/ppermute | solution.py:377
  24.3 5.8 %copy-start.3 = (f32[32,64,256]{2,1,0:T(8,128)S(1)}, f32[32,64,256]{2,1,0:T(8,128)}, u32[]{:S(2)}) copy-start(f32[32,64,256]{2,1,0:T(8,128)} %basis_ref.1) | copy-start | bytes 6291460
  24.3 5.8 %copy-start.4 = (f32[32,64,64]{2,1,0:T(8,128)S(1)}, f32[32,64,64]{2,1,0:T(8,128)}, u32[]{:S(2)}) copy-start(f32[32,64,64]{2,1,0:T(8,128)} %trans_ref.1) | copy-start | bytes 1572868
  24.3 5.8 %copy-start.5 = (f32[32,64,64]{2,1,0:T(8,128)S(1)}, f32[32,64,64]{2,1,0:T(8,128)}, u32[]{:S(2)}) copy-start(f32[32,64,64]{2,1,0:T(8,128)} %coup_ref.1) | copy-start | bytes 1572868
  27.4 5.4 %collective-permute-start.4 = (f32[5,32,128]{2,1,0:T(8,128)S(1)}, f32[5,32,128]{2,1,0:T(8,128)S(1)}, u32[]{:S(2)}, u32[]{:S(2)}) collective-permute-start(f32[5,32,128]{2,1,0:T(8,128)S(1)} %get-tuple-element.35.after_ref.mine_ref), channel_id=1, source_target_pairs={{0,16},{4,20},{8,24},{12,28},{16,0},{20,4},{24,8},{28,12},{1,17},{... | collective-permute-start | bytes 245768 | tf_op jit(solution)/shard_map/ppermute | solution.py:377
  30.1 2.8 %copy-start.2 = (s32[32]{0:T(128)S(1)}, s32[32]{0:T(128)}, u32[]{:S(2)}) copy-start(s32[32]{0:T(128)} %refs_8_.1) | copy-start | bytes 388

commit v4 on v3

--- a/solution.py
+++ b/solution.py
@@ -11,6 +11,7 @@
 SUB = 8
 LANES = 128
 SET = LANES // SUB
+GROUP = 4
 F32 = jnp.float32
 B16 = jnp.bfloat16
 
@@ -217,20 +218,24 @@
         for copy in copies[step]:
             copy.wait()
         left, right = [], []
-        for n in range(step * chunk, (step + 1) * chunk):
-            basis = basis_ref[n]
-            high, rest = halves(basis)
-            middle, low = halves(rest)
-            three = jnp.concatenate([high, middle, low], axis=0).astype(B16)
-            product = mm_nt(three, three)
-            rows = product[:rank] + product[rank : 2 * rank] + product[2 * rank :]
-            gram = fold(rows[:, : 2 * rank]) + rows[:, 2 * rank :]
-            grams_refs[n // SET][n % SET] = gram
-            trans = pair(trans_ref[n])
-            high, low = halves(gram)
-            parts = mm(jnp.concatenate([high, low], axis=0).astype(B16), trans)
-            left.append(trans)
-            right.append(pair(fold(parts[:rank] + parts[rank:])))
+        for first in range(step * chunk, (step + 1) * chunk, GROUP):
+            span = range(first, first + GROUP)
+            threes = []
+            for n in span:
+                high, rest = halves(basis_ref[n])
+                middle, low = halves(rest)
+                threes.append(jnp.concatenate([high, middle, low], axis=0).astype(B16))
+            products = [mm_nt(three, three) for three in threes]
+            grams = []
+            for n, product in zip(span, products):
+                rows = product[:rank] + product[rank : 2 * rank] + product[2 * rank :]
+                gram = fold(rows[:, : 2 * rank]) + rows[:, 2 * rank :]
+                grams_refs[n // SET][n % SET] = gram
+                grams.append(jnp.concatenate(halves(gram), axis=0).astype(B16))
+            trans = [pair(trans_ref[n]) for n in span]
+            parts = [mm(gram, edge) for gram, edge in zip(grams, trans)]
+            left += trans
+            right += [pair(fold(part[:rank] + part[rank:])) for part in parts]
         total = total + mm_tn(jnp.concatenate(left, axis=0), jnp.concatenate(right, axis=0))
     gram = fold(total[:rank] + total[rank:])
     own_ref[...] = pack(gram)
@@ -253,22 +258,52 @@
     path_ref[...] = packed
     lifted = pack(lift(unpack(packed), upper_ref[2**level - 2 + (myself >> (bit + 1))]))
     if last:
-        next_ref[0] = lifted
-        next_ref[1] = own_ref[...]
+        half = lifted.shape[0]
+        next_ref[:half] = lifted
+        next_ref[half:] = own_ref[...]
     else:
         next_ref[...] = lifted
 
 
+def packed_places(half):
+    row = lax.broadcasted_iota(jnp.int32, (half, 4 * half), 0)
+    lane = lax.broadcasted_iota(jnp.int32, (half, 4 * half), 1)
+    return jnp.where(lane < 2 * half, row, row + half), lane % (2 * half)
+
+
+def join(a, b):
+    half = a.shape[0]
+    row, column = packed_places(half)
+    diagonal = jnp.sum(jnp.where(row == column, a, 0.0), axis=0, keepdims=True)
+    joint = jnp.where(row > column, a, b)
+    return jnp.concatenate([joint, jnp.broadcast_to(diagonal, (SUB, 4 * half))], axis=0)
+
+
+def part(x):
+    half = x.shape[0] - SUB
+    joint = unpack(x[:half])
+    turned = joint.T
+    row = lax.broadcasted_iota(jnp.int32, joint.shape, 0)
+    column = lax.broadcasted_iota(jnp.int32, joint.shape, 1)
+    diagonal = jnp.broadcast_to(fold(x[half : half + 1]), joint.shape)
+    first = jnp.where(row > column, joint, jnp.where(row == column, diagonal, turned))
+    return first, jnp.where(row <= column, joint, turned)
+
+
 def leaf_hop_kernel(bit, mine_ref, got_ref, upper_ref, after_ref, path_ref, next_ref):
     del after_ref
+    half = path_ref.shape[0]
     level = lax.axis_size("leaf").bit_length() - 2 - bit
-    packed = mine_ref[0] + got_ref[0]
+    packed = mine_ref[:half] + got_ref[:half]
     path_ref[...] = packed
     node = lax.axis_index("leaf") >> (bit + 1)
-    next_ref[0] = pack(lift(unpack(packed), upper_ref[2**level - 2 + node]))
-    count = 2**bit
-    next_ref[1 : 1 + count] = mine_ref[1:]
-    next_ref[1 + count :] = got_ref[1:]
+    next_ref[:half] = pack(lift(unpack(packed), upper_ref[2**level - 2 + node]))
+    if bit == 0:
+        next_ref[half:] = join(mine_ref[half:], got_ref[half:])
+    else:
+        size = mine_ref.shape[0] - half
+        next_ref[half : half + size] = mine_ref[half:]
+        next_ref[half + size :] = got_ref[half:]
 
 
 def leaf_kernel(steps, sets, basis_ref, trans_ref, coup_ref, after_ref, *refs):
@@ -305,14 +340,16 @@
         moved_ref,
         split_ref,
         offset_ref,
-        fresh_ref,
+        fresh_hbm,
         bridge_hbm,
         coupled_hbm,
         grams_ref,
         factor_ref,
         cols_ref,
+        fresh_ref,
         bridge_ref,
         coupled_ref,
+        fresh_sem,
         bridge_sem,
         coupled_sem,
         w_ref,
@@ -323,10 +360,14 @@
     myself = branch * n_rows + row
     for n in range(levels - 1):
         grams_ref[n] = unpack(path_refs[n][...])
-    grams_ref[levels - 1] = unpack(mine_ref[0] + got_ref[0])
-    for n in range(n_leaf // 2):
-        grams_ref[levels + n] = unpack(mine_ref[1 + n])
-        grams_ref[levels + n_leaf // 2 + n] = unpack(got_ref[1 + n])
+    half = rank // 2
+    grams_ref[levels - 1] = unpack(mine_ref[:half] + got_ref[:half])
+    pairs = n_leaf // 4
+    for n in range(pairs):
+        for place, ref in ((0, mine_ref), (pairs, got_ref)):
+            joint = ref[pl.ds(half + n * (half + SUB), half + SUB), :]
+            at = levels + 2 * (place + n)
+            grams_ref[at], grams_ref[at + 1] = part(joint)
     count = grams_ref.shape[0]
     load_sets(grams_ref.reshape(count * rank, rank), w_ref)
     eliminate(w_ref, g_ref, factor_ref.reshape(count * rank, 2 * rank))
@@ -336,38 +377,42 @@
     for n in range(n_leaf):
         cols_ref[n] = broad(factor_ref[levels + n, :, :rank])
     copies = []
+
+    def send(source, target, sem):
+        copies.append(pltpu.make_async_copy(source, target, sem))
+        copies[-1].start()
+
+    lows, edges, inverses = [own_upper], [tall(dev_ref[0])], []
+    for k in range(levels):
+        inverses.append(broad(factor_ref[k, :, rank:]))
+        if k:
+            lows.append(twice(pair(factor_ref[k - 1, :, :rank])))
+            edges.append(tall(upper_ref[2 ** (levels - k) - 2 + (myself >> k)]))
+    inner = [mm(low, edge) for low, edge in zip(lows, edges)]
+    inner = [twice(pair(value)) for value in inner]
+    for k in range(levels):
+        fresh_ref[0, k] = mm_nt(inner[k], inverses[k])
+    send(fresh_ref, fresh_hbm, fresh_sem)
     leaves = moved_ref.shape[0]
     chunk = leaves // steps
     for step in range(steps):
         span = pl.ds(step * chunk, chunk)
         moved = twice(moved_ref[span].reshape(chunk * rank, 2 * rank))
         bridge_ref[span] = mm_nt(moved, own_inverse).reshape(chunk, rank, rank)
-        copy = pltpu.make_async_copy(
-            bridge_ref.at[span], bridge_hbm.at[span], bridge_sem.at[step]
-        )
-        copy.start()
-        copies.append(copy)
+        send(bridge_ref.at[span], bridge_hbm.at[span], bridge_sem.at[step])
     blocks = split_ref.shape[0]
     chunk = blocks // steps
     for step in range(steps):
+        inner = []
         for b in range(step * chunk, (step + 1) * chunk):
             target = lax.rem(myself + offset_ref[b], n_rows * n_leaf)
-            inner = mm_nt(twice(split_ref[b]), cols_ref[(target // n_rows) ^ branch])
-            coupled_ref[b] = mm(own_upper, tall(inner))
+            column = cols_ref[(target // n_rows) ^ branch]
+            inner.append(mm_nt(twice(split_ref[b]), column))
+        inner = [tall(value) for value in inner]
+        for n in range(chunk):
+            coupled_ref[step * chunk + n] = mm(own_upper, inner[n])
         span = pl.ds(step * chunk, chunk)
-        copy = pltpu.make_async_copy(
-            coupled_ref.at[span], coupled_hbm.at[span], coupled_sem.at[step]
-        )
-        copy.start()
-        copies.append(copy)
-    for k in range(levels):
-        if k == 0:
-            edge, low = dev_ref[0], own[:, :rank]
-        else:
-            edge = upper_ref[2 ** (levels - k) - 2 + (myself >> k)]
-            low = factor_ref[k - 1, :, :rank]
-        inner = mm(low, edge, precision=HIGH)
-        fresh_ref[0, k] = mm_nt(inner, factor_ref[k, :, rank:], HIGH)
+        send(coupled_ref.at[span], coupled_hbm.at[span], coupled_sem.at[step])
     for copy in copies:
         copy.wait()
 
@@ -437,7 +482,7 @@
             functools.partial(row_hop_kernel, bit, last),
             in_specs=[vmem] * 4,
             out_specs=[vmem, vmem],
-            out_shape=[shape(half, 2 * rank), shape(*((2,) if last else ()), half, 2 * rank)],
+            out_shape=[shape(half, 2 * rank), shape(rank if last else half, 2 * rank)],
             compiler_params=params,
             name="row_hop",
         )(carry, got, own_gram, upper_transfer)
@@ -461,7 +506,7 @@
             functools.partial(leaf_hop_kernel, bit),
             in_specs=[vmem] * 3 + [any_place],
             out_specs=[vmem, vmem],
-            out_shape=[shape(half, 2 * rank), shape(1 + 2 ** (bit + 1), half, 2 * rank)],
+            out_shape=[shape(half, 2 * rank), shape(half + (half + SUB) * 2**bit, 2 * rank)],
             compiler_params=params,
             name="leaf_hop",
         )(carry, got, upper_transfer, token)
@@ -485,7 +530,7 @@
     new_transfers, leaf_bridge, coupled = pl.pallas_call(
         functools.partial(top_kernel, n_rows, n_leaf, steps),
         in_specs=[vmem] * (levels + 5) + [smem],
-        out_specs=[vmem, hbm, hbm],
+        out_specs=[hbm, hbm, hbm],
         out_shape=[
             shape(1, levels, rank, rank),
             like(leaf_transfer),
@@ -495,8 +540,10 @@
             pltpu.VMEM((sets * SET, rank, rank), F32),
             pltpu.VMEM((sets * SET, rank, 2 * rank), F32),
             pltpu.VMEM((n_leaf, rank, 4 * rank), B16),
+            pltpu.VMEM((1, levels, rank, rank), F32),
             pltpu.VMEM(leaf_transfer.shape, F32),
             pltpu.VMEM(couplings.shape, F32),
+            pltpu.SemaphoreType.DMA(()),
             pltpu.SemaphoreType.DMA((steps,)),
             pltpu.SemaphoreType.DMA((steps,)),
         ]

time: 39.6 us -> 36 us (0.909)
  Pallas kernels: 24.8 us -> 21.7 us
    pallas_call x1, Pallas kernels: 9.2 us -> 6.5 us  [per_device(): pl.pallas_call(functools.partial(gram_kernel, steps, sets), in_specs=[hbm...]
    pallas_call x1, Pallas kernels: 6.48 us -> 6.03 us  [per_device(): pl.pallas_call(functools.partial(top_kernel, n_rows, n_leaf, steps), in_s...]
  transfers between devices with their start and end apart: 5 -> 5, of which waited for: 3 -> 3; matrix products, arithmetic and copies ran while one was open for 0% -> 0% of each run, Pallas kernels for 19% -> 21%
where the time goes in v4:
time: 36 us; the launch traced here: 35.9 us
  Pallas kernels  21.7 us (60%)
  starting transfers between devices  9.8 us (27%)
  waiting for transfers between devices  2.81 us (8%)
  local copies, waits for them, and re-layouts  0.85 us (2%)
  between operations  0.74 us (2%)
    ppermute x5, starting transfers between devices, swap(): return lax.ppermute(value, axis, pairs)  9.8 us
    pallas_call x1, Pallas kernels, per_device(): pl.pallas_call(functools.partial(gram_kernel, steps, sets), in_specs=[hbm...  6.5 us
    pallas_call x1, Pallas kernels, per_device(): pl.pallas_call(functools.partial(top_kernel, n_rows, n_leaf, steps), in_s...  6.03 us
    pallas_call x2, Pallas kernels, per_device(): pl.pallas_call(factor_kernel, in_specs=[vmem, any_place], out_specs=[vmem...  5.3 us
    ppermute x5, waiting for transfers between devices, swap(): return lax.ppermute(value, axis, pairs)  2.81 us
    pallas_call x1, Pallas kernels, per_device(): pl.pallas_call(functools.partial(leaf_kernel, steps, sets), in_specs=[vme...  2.21 us
    unnamed x12, local copies, waits for them, and re-layouts  0.85 us
    pallas_call x2, Pallas kernels, per_device(): pl.pallas_call(functools.partial(leaf_hop_kernel, bit), in_specs=[vmem] *...  0.82 us
  transfers between devices with their start and end apart: 5, of which 3 were waited for; matrix products, arithmetic and copies ran while one was open for 0% of the time, Pallas kernels for 21%

profile of v4, /device:TPU:0, one launch (start us, length us, event | category | flops | bytes accessed | tf_op | source)
XLA Modules:
  0.0 35.9 jit_solution(14600526071158166045)
XLA Ops:
  0.6 0.0 copy-start
  0.6 0.0 copy-start.1
  0.7 0.8 %copy-done.1 = f32[1,64,64]{2,1,0:T(8,128)S(1)} copy-done((f32[1,64,64]{2,1,0:T(8,128)S(1)}, f32[1,64,64]{2,1,0:T(8,128)}, u32[]{:S(2)}) %copy-start.1) | copy-done | bytes 16408
  1.5 6.5 %gram.1 = (f32[16,64,64]{2,1,0:T(8,128)S(1)}, f32[16,64,64]{2,1,0:T(8,128)S(1)}, f32[32,128]{1,0:T(8,128)S(1)}, f32[32,128]{1,0:T(8,128)S(1)}) custom-call(f32[32,64,256]{2,1,0:T(8,128)} %basis_ref.1, f32[32,64,64]{2,1,0:T(8,128)} %trans_ref.1, f32[1,64,64]{2,1,0:T(8,128)S(1)} %copy-done.1), custom_call_target="tpu_custom_call" | custom-call | flops 1000000000 | bytes 4000000 | tf_op jit(solution)/shard_map/gram/pallas_call | solution.py:461
  8.0 0.5 %collective-permute-start = (f32[32,128]{1,0:T(8,128)S(1)}, f32[32,128]{1,0:T(8,128)S(1)}, u32[]{:S(2)}, u32[]{:S(2)}) collective-permute-start(f32[32,128]{1,0:T(8,128)S(1)} %get-tuple-element.26.mine_ref), channel_id=1, source_target_pairs={{0,1},{1,0},{2,3},{3,2},{4,5},{5,4},{6,7},{7,6},{8,9},{9,8},{10,11... | collective-permute-start | bytes 49160 | tf_op jit(solution)/shard_map/ppermute | solution.py:422
  8.5 0.8 %collective-permute-done.got_ref = f32[32,128]{1,0:T(8,128)S(1)} collective-permute-done((f32[32,128]{1,0:T(8,128)S(1)}, f32[32,128]{1,0:T(8,128)S(1)}, u32[]{:S(2)}, u32[]{:S(2)}) %collective-permute-start) | collective-permute-done | bytes 16416 | tf_op jit(solution)/shard_map/ppermute | solution.py:422
  9.4 0.0 copy-done
  9.4 0.4 %row_hop.2 = (f32[32,128]{1,0:T(8,128)S(1)}, f32[32,128]{1,0:T(8,128)S(1)}) custom-call(f32[32,128]{1,0:T(8,128)S(1)} %get-tuple-element.26.mine_ref, f32[32,128]{1,0:T(8,128)S(1)} %collective-permute-done.got_ref, f32[32,128]{1,0:T(8,128)S(1)} %get-tuple-element.27.own_ref, f32[30,64,64]{2,1,0:T(8,128)S(1)} %copy-done), custom_call_target="tpu_custom_call" | custom-call | tf_op jit(solution)/shard_map/row_hop/pallas_call | solution.py:481
  9.8 2.9 %collective-permute-start.1 = (f32[32,128]{1,0:T(8,128)S(1)}, f32[32,128]{1,0:T(8,128)S(1)}, u32[]{:S(2)}, u32[]{:S(2)}) collective-permute-start(f32[32,128]{1,0:T(8,128)S(1)} %get-tuple-element.28.mine_ref), channel_id=1, source_target_pairs={{0,2},{1,3},{2,0},{3,1},{4,6},{5,7},{6,4},{7,5},{8,10},{9,11},{10,... | collective-permute-start | bytes 49160 | tf_op jit(solution)/shard_map/ppermute | solution.py:422
  12.7 1.7 %collective-permute-done.1.got_ref = f32[32,128]{1,0:T(8,128)S(1)} collective-permute-done((f32[32,128]{1,0:T(8,128)S(1)}, f32[32,128]{1,0:T(8,128)S(1)}, u32[]{:S(2)}, u32[]{:S(2)}) %collective-permute-start.1) | collective-permute-done | bytes 16416 | tf_op jit(solution)/shard_map/ppermute | solution.py:422
  14.4 0.4 %row_hop.3 = (f32[32,128]{1,0:T(8,128)S(1)}, f32[64,128]{1,0:T(8,128)S(1)}) custom-call(f32[32,128]{1,0:T(8,128)S(1)} %get-tuple-element.28.mine_ref, f32[32,128]{1,0:T(8,128)S(1)} %collective-permute-done.1.got_ref, f32[32,128]{1,0:T(8,128)S(1)} %get-tuple-element.27.own_ref, f32[30,64,64]{2,1,0:T(8,128)S(1)} %copy-done), custom_call_target="tpu_custom_call" | custom-call | tf_op jit(solution)/shard_map/row_hop/pallas_call | solution.py:481
  14.8 2.1 %collective-permute-start.2 = (f32[64,128]{1,0:T(8,128)S(1)}, f32[64,128]{1,0:T(8,128)S(1)}, u32[]{:S(2)}, u32[]{:S(2)}) collective-permute-start(f32[64,128]{1,0:T(8,128)S(1)} %get-tuple-element.29.after_ref.mine_ref), channel_id=1, source_target_pairs={{0,4},{4,0},{8,12},{12,8},{16,20},{20,16},{24,28},{28,24},{1,5},{5... | collective-permute-start | bytes 98312 | tf_op jit(solution)/shard_map/ppermute | solution.py:422
  16.9 2.7 %factor.2 = (f32[16,64,128]{2,1,0:T(8,128)S(1)}, f32[8,128]{1,0:T(8,128)S(1)}) custom-call(f32[16,64,64]{2,1,0:T(8,128)S(1)} %get-tuple-element.30.grams_ref, f32[64,128]{1,0:T(8,128)S(1)} %get-tuple-element.29.after_ref.mine_ref), custom_call_target="tpu_custom_call" | custom-call | flops 5000000000 | bytes 8000000 | tf_op jit(solution)/shard_map/factor/pallas_call | solution.py:494
  19.5 0.0 collective-permute-done.2.got_ref
  19.5 0.4 %leaf_hop.2 = (f32[32,128]{1,0:T(8,128)S(1)}, f32[72,128]{1,0:T(8,128)S(1)}) custom-call(f32[64,128]{1,0:T(8,128)S(1)} %get-tuple-element.29.after_ref.mine_ref, f32[64,128]{1,0:T(8,128)S(1)} %collective-permute-done.2.got_ref, f32[30,64,64]{2,1,0:T(8,128)S(1)} %copy-done, f32[8,128]{1,0:T(8,128)S(1)} %get-tuple-element.31.after_ref), custom_call_target="tpu_custom_call" | custom-call | tf_op jit(solution)/shard_map/leaf_hop/pallas_call | solution.py:505
  20.0 1.6 %collective-permute-start.3 = (f32[72,128]{1,0:T(8,128)S(1)}, f32[72,128]{1,0:T(8,128)S(1)}, u32[]{:S(2)}, u32[]{:S(2)}) collective-permute-start(f32[72,128]{1,0:T(8,128)S(1)} %get-tuple-element.32.after_ref.mine_ref), channel_id=1, source_target_pairs={{0,8},{4,12},{8,0},{12,4},{16,24},{20,28},{24,16},{28,20},{1,9},{5... | collective-permute-start | bytes 110600 | tf_op jit(solution)/shard_map/ppermute | solution.py:422
  21.6 2.7 %factor.3 = (f32[16,64,128]{2,1,0:T(8,128)S(1)}, f32[8,128]{1,0:T(8,128)S(1)}) custom-call(f32[16,64,64]{2,1,0:T(8,128)S(1)} %get-tuple-element.33.grams_ref, f32[72,128]{1,0:T(8,128)S(1)} %get-tuple-element.32.after_ref.mine_ref), custom_call_target="tpu_custom_call" | custom-call | flops 5000000000 | bytes 8000000 | tf_op jit(solution)/shard_map/factor/pallas_call | solution.py:494
  24.3 0.0 collective-permute-done.3.got_ref
  24.3 0.4 %leaf_hop.3 = (f32[32,128]{1,0:T(8,128)S(1)}, f32[112,128]{1,0:T(8,128)S(1)}) custom-call(f32[72,128]{1,0:T(8,128)S(1)} %get-tuple-element.32.after_ref.mine_ref, f32[72,128]{1,0:T(8,128)S(1)} %collective-permute-done.3.got_ref, f32[30,64,64]{2,1,0:T(8,128)S(1)} %copy-done, f32[8,128]{1,0:T(8,128)S(1)} %get-tuple-element.34.after_ref), custom_call_target="tpu_custom_call" | custom-call | tf_op jit(solution)/shard_map/leaf_hop/pallas_call | solution.py:505
  24.7 2.7 %collective-permute-start.4 = (f32[112,128]{1,0:T(8,128)S(1)}, f32[112,128]{1,0:T(8,128)S(1)}, u32[]{:S(2)}, u32[]{:S(2)}) collective-permute-start(f32[112,128]{1,0:T(8,128)S(1)} %get-tuple-element.35.after_ref.mine_ref), channel_id=1, source_target_pairs={{0,16},{4,20},{8,24},{12,28},{16,0},{20,4},{24,8},{28,12},{1,17},{... | collective-permute-start | bytes 172040 | tf_op jit(solution)/shard_map/ppermute | solution.py:422
  27.4 0.0 copy-done.3
  27.4 2.2 %leaf.1 = (f32[32,64,256]{2,1,0:T(8,128)}, bf16[32,64,128]{2,1,0:T(8,128)(2,1)S(1)}, bf16[32,64,128]{2,1,0:T(8,128)(2,1)S(1)}) custom-call(f32[32,64,256]{2,1,0:T(8,128)S(1)} %copy-done.3, f32[32,64,64]{2,1,0:T(8,128)S(1)} %copy-done.4, f32[32,64,64]{2,1,0:T(8,128)S(1)} %copy-done.5, f32[112,128]{1,0:T(8,128)S(1)} %get-tuple-element.35.after_ref.mine_ref, ...), custom_call_target="tpu_custom_call" | custom-call | flops 5000000000 | bytes 8000000 | tf_op jit(solution)/shard_map/leaf/pallas_call | solution.py:515
  29.6 0.2 collective-permute-done.4.got_ref
  29.8 6.0 %top.1 = (f32[1,5,64,64]{3,2,1,0:T(8,128)}, f32[32,64,64]{2,1,0:T(8,128)}, f32[32,64,64]{2,1,0:T(8,128)}) custom-call(f32[112,128]{1,0:T(8,128)S(1)} %get-tuple-element.35.after_ref.mine_ref, f32[112,128]{1,0:T(8,128)S(1)} %collective-permute-done.4.got_ref, f32[32,128]{1,0:T(8,128)S(1)} %get-tuple-element.39.refs_0_, ...), custom_call_target="tpu_custom_call" | custom-call | tf_op jit(solution)/shard_map/top/pallas_call | solution.py:530
  (7 shorter events, 0.0 us)
Async XLA Ops:
  0.6 8.7 %copy-start = (f32[30,64,64]{2,1,0:T(8,128)S(1)}, f32[30,64,64]{2,1,0:T(8,128)}, u32[]{:S(2)}) copy-start(f32[30,64,64]{2,1,0:T(8,128)} %refs_4_.1) | copy-start | bytes 1474564
  0.6 0.8 %copy-start.1 = (f32[1,64,64]{2,1,0:T(8,128)S(1)}, f32[1,64,64]{2,1,0:T(8,128)}, u32[]{:S(2)}) copy-start(f32[1,64,64]{2,1,0:T(8,128)} %refs_5_.1) | copy-start | bytes 49156
  8.0 1.4 %collective-permute-start = (f32[32,128]{1,0:T(8,128)S(1)}, f32[32,128]{1,0:T(8,128)S(1)}, u32[]{:S(2)}, u32[]{:S(2)}) collective-permute-start(f32[32,128]{1,0:T(8,128)S(1)} %get-tuple-element.26.mine_ref), channel_id=1, source_target_pairs={{0,1},{1,0},{2,3},{3,2},{4,5},{5,4},{6,7},{7,6},{8,9},{9,8},{10,11... | collective-permute-start | bytes 49160 | tf_op jit(solution)/shard_map/ppermute | solution.py:422
  9.8 4.6 %collective-permute-start.1 = (f32[32,128]{1,0:T(8,128)S(1)}, f32[32,128]{1,0:T(8,128)S(1)}, u32[]{:S(2)}, u32[]{:S(2)}) collective-permute-start(f32[32,128]{1,0:T(8,128)S(1)} %get-tuple-element.28.mine_ref), channel_id=1, source_target_pairs={{0,2},{1,3},{2,0},{3,1},{4,6},{5,7},{6,4},{7,5},{8,10},{9,11},{10,... | collective-permute-start | bytes 49160 | tf_op jit(solution)/shard_map/ppermute | solution.py:422
  14.8 4.7 %collective-permute-start.2 = (f32[64,128]{1,0:T(8,128)S(1)}, f32[64,128]{1,0:T(8,128)S(1)}, u32[]{:S(2)}, u32[]{:S(2)}) collective-permute-start(f32[64,128]{1,0:T(8,128)S(1)} %get-tuple-element.29.after_ref.mine_ref), channel_id=1, source_target_pairs={{0,4},{4,0},{8,12},{12,8},{16,20},{20,16},{24,28},{28,24},{1,5},{5... | collective-permute-start | bytes 98312 | tf_op jit(solution)/shard_map/ppermute | solution.py:422
  20.0 4.3 %collective-permute-start.3 = (f32[72,128]{1,0:T(8,128)S(1)}, f32[72,128]{1,0:T(8,128)S(1)}, u32[]{:S(2)}, u32[]{:S(2)}) collective-permute-start(f32[72,128]{1,0:T(8,128)S(1)} %get-tuple-element.32.after_ref.mine_ref), channel_id=1, source_target_pairs={{0,8},{4,12},{8,0},{12,4},{16,24},{20,28},{24,16},{28,20},{1,9},{5... | collective-permute-start | bytes 110600 | tf_op jit(solution)/shard_map/ppermute | solution.py:422
  21.6 5.8 %copy-start.3 = (f32[32,64,256]{2,1,0:T(8,128)S(1)}, f32[32,64,256]{2,1,0:T(8,128)}, u32[]{:S(2)}) copy-start(f32[32,64,256]{2,1,0:T(8,128)} %basis_ref.1) | copy-start | bytes 6291460
  21.6 5.8 %copy-start.4 = (f32[32,64,64]{2,1,0:T(8,128)S(1)}, f32[32,64,64]{2,1,0:T(8,128)}, u32[]{:S(2)}) copy-start(f32[32,64,64]{2,1,0:T(8,128)} %trans_ref.1) | copy-start | bytes 1572868
  21.6 5.8 %copy-start.5 = (f32[32,64,64]{2,1,0:T(8,128)S(1)}, f32[32,64,64]{2,1,0:T(8,128)}, u32[]{:S(2)}) copy-start(f32[32,64,64]{2,1,0:T(8,128)} %coup_ref.1) | copy-start | bytes 1572868
  24.7 5.1 %collective-permute-start.4 = (f32[112,128]{1,0:T(8,128)S(1)}, f32[112,128]{1,0:T(8,128)S(1)}, u32[]{:S(2)}, u32[]{:S(2)}) collective-permute-start(f32[112,128]{1,0:T(8,128)S(1)} %get-tuple-element.35.after_ref.mine_ref), channel_id=1, source_target_pairs={{0,16},{4,20},{8,24},{12,28},{16,0},{20,4},{24,8},{28,12},{1,17},{... | collective-permute-start | bytes 172040 | tf_op jit(solution)/shard_map/ppermute | solution.py:422
  27.4 2.5 %copy-start.2 = (s32[32]{0:T(128)S(1)}, s32[32]{0:T(128)}, u32[]{:S(2)}) copy-start(s32[32]{0:T(128)} %refs_8_.1) | copy-start | bytes 388

commit v5 on v4

--- a/solution.py
+++ b/solution.py
@@ -65,6 +65,12 @@
 
 def spread(value, at):
     return jnp.broadcast_to(value[at : at + 1, :], (SUB, LANES))
+
+
+def added(terms):
+    while len(terms) > 1:
+        terms = [sum(terms[n : n + 2][1:], terms[n]) for n in range(0, len(terms), 2)]
+    return terms[0]
 
 
 def load_sets(flat, w_ref):
@@ -94,18 +100,19 @@
     def corner(t, kb):
         diagonal = tile(t, kb, kb)
         rows = [picked(diagonal, p) for p in range(SUB)]
+        pivot = spread(rows[0], 0)
         inverses, roots = [], []
         for q in range(SUB):
-            pivot = spread(rows[q], q)
-            inverse = 1.0 / pivot
-            root = lax.rsqrt(pivot)
-            roots.append(root * (1.5 - 0.5 * pivot * root * root))
+            unit = jnp.where(place == q, 1.0, rows[q])
+            sides = {p: spread(rows[q], p) for p in range(q + 1, SUB)}
+            inverse = pl.reciprocal(pivot, approx=True)
             inverses.append(inverse)
-            scaled = rows[q] * inverse
-            unit = jnp.where(place == q, 1.0, rows[q])
+            roots.append(lax.rsqrt(pivot))
+            if q + 1 < SUB:
+                pivot = spread(rows[q + 1], q + 1) - sides[q + 1] * sides[q + 1] * inverse
             for p in range(q + 1, SUB):
                 kept = jnp.where(place == q, 0.0, rows[p])
-                rows[p] = kept - spread(scaled, p) * unit
+                rows[p] = kept - (sides[p] * unit) * inverse
         return rows, inverses, roots
 
     def merged(parts):
@@ -132,9 +139,7 @@
             old = [picked(value, p) for p in range(SUB)]
             new = []
             for p in range(SUB):
-                term = old[p]
-                for q in range(p):
-                    term = term + mult[p, q] * old[q]
+                term = added([old[p]] + [mult[p, q] * old[q] for q in range(p)])
                 g_ref[t, p, pl.ds(jv * SUB, SUB), :] = term
                 new.append(term)
             final = merged(new) * root
@@ -155,17 +160,13 @@
         columns = [spread(value, q) for q in range(SUB)]
         found = []
         for q in range(SUB):
-            term = columns[q]
-            for r in range(q):
-                term = term + mult[q, r] * columns[r]
+            term = added([columns[q]] + [mult[q, r] * columns[r] for r in range(q)])
             found.append(term * inverses[q])
         return found
 
     def trail(t, kb, ib, jv, found):
-        acc = None if jv == kb else tile(t, ib, jv)
-        for q in range(SUB):
-            term = found[q] * g_ref[t, q, pl.ds(jv * SUB, SUB), :]
-            acc = -term if acc is None else acc - term
+        terms = [found[q] * g_ref[t, q, pl.ds(jv * SUB, SUB), :] for q in range(SUB)]
+        acc = -added(terms) if jv == kb else tile(t, ib, jv) - added(terms)
         w_ref[t, ib, pl.ds(jv * SUB, SUB), :] = acc
 
     corners = [corner(t, 0) for t in range(sets)]
@@ -213,30 +214,42 @@
         )
         for copy in copies[-1]:
             copy.start()
-    total = jnp.zeros((2 * rank, 2 * rank), F32)
-    for step in range(steps):
-        for copy in copies[step]:
-            copy.wait()
-        left, right = [], []
-        for first in range(step * chunk, (step + 1) * chunk, GROUP):
-            span = range(first, first + GROUP)
+    groups = leaves // GROUP
+    products, parts, edges, rights = {}, {}, {}, {}
+    total = None
+    for stage in range(groups + 3):
+        if stage < groups:
+            if stage * GROUP % chunk == 0:
+                for copy in copies[stage * GROUP // chunk]:
+                    copy.wait()
             threes = []
-            for n in span:
+            for n in range(stage * GROUP, (stage + 1) * GROUP):
                 high, rest = halves(basis_ref[n])
                 middle, low = halves(rest)
                 threes.append(jnp.concatenate([high, middle, low], axis=0).astype(B16))
-            products = [mm_nt(three, three) for three in threes]
-            grams = []
-            for n, product in zip(span, products):
+            products[stage] = [mm_nt(three, three) for three in threes]
+        group = stage - 1
+        if 0 <= group < groups:
+            edges[group] = [
+                pair(trans_ref[n]) for n in range(group * GROUP, (group + 1) * GROUP)
+            ]
+            parts[group] = []
+            for n, product in enumerate(products.pop(group)):
                 rows = product[:rank] + product[rank : 2 * rank] + product[2 * rank :]
                 gram = fold(rows[:, : 2 * rank]) + rows[:, 2 * rank :]
-                grams_refs[n // SET][n % SET] = gram
-                grams.append(jnp.concatenate(halves(gram), axis=0).astype(B16))
-            trans = [pair(trans_ref[n]) for n in span]
-            parts = [mm(gram, edge) for gram, edge in zip(grams, trans)]
-            left += trans
-            right += [pair(fold(part[:rank] + part[rank:])) for part in parts]
-        total = total + mm_tn(jnp.concatenate(left, axis=0), jnp.concatenate(right, axis=0))
+                at = group * GROUP + n
+                grams_refs[at // SET][at % SET] = gram
+                both = jnp.concatenate(halves(gram), axis=0).astype(B16)
+                parts[group].append(mm(both, edges[group][n]))
+        group = stage - 2
+        if 0 <= group < groups:
+            rights[group] = [pair(fold(part[:rank] + part[rank:])) for part in parts.pop(group)]
+        group = stage - 3
+        if 0 <= group < groups and group % 2:
+            left = jnp.concatenate(edges.pop(group - 1) + edges.pop(group), axis=0)
+            right = jnp.concatenate(rights.pop(group - 1) + rights.pop(group), axis=0)
+            term = mm_tn(left, right)
+            total = term if total is None else total + term
     gram = fold(total[:rank] + total[rank:])
     own_ref[...] = pack(gram)
     lift_ref[...] = pack(lift(gram, dev_ref[0]))

time: 36 us -> 34.6 us (0.961)
  Pallas kernels: 21.7 us -> 20.3 us
    pallas_call x1, Pallas kernels: 6.5 us -> 4.8 us  [per_device(): pl.pallas_call(functools.partial(gram_kernel, steps, sets), in_specs=[hbm...]
  transfers between devices with their start and end apart: 5 -> 5, of which waited for: 3 -> 3; matrix products, arithmetic and copies ran while one was open for 0% -> 0% of each run, Pallas kernels for 21% -> 22%
where the time goes in v5:
time: 34.6 us; the launch traced here: 34.5 us
  Pallas kernels  20.3 us (59%)
  starting transfers between devices  9.79 us (28%)
  waiting for transfers between devices  2.83 us (8%)
  local copies, waits for them, and re-layouts  0.85 us (2%)
  between operations  0.74 us (2%)
    ppermute x5, starting transfers between devices, swap(): return lax.ppermute(value, axis, pairs)  9.79 us
    pallas_call x1, Pallas kernels, per_device(): pl.pallas_call(functools.partial(top_kernel, n_rows, n_leaf, steps), in_s...  6.1 us
    pallas_call x2, Pallas kernels, per_device(): pl.pallas_call(factor_kernel, in_specs=[vmem, any_place], out_specs=[vmem...  5.54 us
    pallas_call x1, Pallas kernels, per_device(): pl.pallas_call(functools.partial(gram_kernel, steps, sets), in_specs=[hbm...  4.8 us
    ppermute x5, waiting for transfers between devices, swap(): return lax.ppermute(value, axis, pairs)  2.83 us
    pallas_call x1, Pallas kernels, per_device(): pl.pallas_call(functools.partial(leaf_kernel, steps, sets), in_specs=[vme...  2.21 us
    unnamed x12, local copies, waits for them, and re-layouts  0.85 us
    pallas_call x2, Pallas kernels, per_device(): pl.pallas_call(functools.partial(leaf_hop_kernel, bit), in_specs=[vmem] *...  0.82 us
  transfers between devices with their start and end apart: 5, of which 3 were waited for; matrix products, arithmetic and copies ran while one was open for 0% of the time, Pallas kernels for 22%

profile of v5, /device:TPU:0, one launch (start us, length us, event | category | flops | bytes accessed | tf_op | source)
XLA Modules:
  0.0 34.5 jit_solution(10296543333378387412)
XLA Ops:
  0.6 0.0 copy-start
  0.6 0.0 copy-start.1
  0.7 0.8 %copy-done.1 = f32[1,64,64]{2,1,0:T(8,128)S(1)} copy-done((f32[1,64,64]{2,1,0:T(8,128)S(1)}, f32[1,64,64]{2,1,0:T(8,128)}, u32[]{:S(2)}) %copy-start.1) | copy-done | bytes 16408
  1.5 4.8 %gram.1 = (f32[16,64,64]{2,1,0:T(8,128)S(1)}, f32[16,64,64]{2,1,0:T(8,128)S(1)}, f32[32,128]{1,0:T(8,128)S(1)}, f32[32,128]{1,0:T(8,128)S(1)}) custom-call(f32[32,64,256]{2,1,0:T(8,128)} %basis_ref.1, f32[32,64,64]{2,1,0:T(8,128)} %trans_ref.1, f32[1,64,64]{2,1,0:T(8,128)S(1)} %copy-done.1), custom_call_target="tpu_custom_call" | custom-call | flops 1000000000 | bytes 4000000 | tf_op jit(solution)/shard_map/gram/pallas_call | solution.py:474
  6.3 0.5 %collective-permute-start = (f32[32,128]{1,0:T(8,128)S(1)}, f32[32,128]{1,0:T(8,128)S(1)}, u32[]{:S(2)}, u32[]{:S(2)}) collective-permute-start(f32[32,128]{1,0:T(8,128)S(1)} %get-tuple-element.26.mine_ref), channel_id=1, source_target_pairs={{0,1},{1,0},{2,3},{3,2},{4,5},{5,4},{6,7},{7,6},{8,9},{9,8},{10,11... | collective-permute-start | bytes 49160 | tf_op jit(solution)/shard_map/ppermute | solution.py:435
  6.8 0.8 %collective-permute-done.got_ref = f32[32,128]{1,0:T(8,128)S(1)} collective-permute-done((f32[32,128]{1,0:T(8,128)S(1)}, f32[32,128]{1,0:T(8,128)S(1)}, u32[]{:S(2)}, u32[]{:S(2)}) %collective-permute-start) | collective-permute-done | bytes 16416 | tf_op jit(solution)/shard_map/ppermute | solution.py:435
  7.7 0.0 copy-done
  7.7 0.4 %row_hop.2 = (f32[32,128]{1,0:T(8,128)S(1)}, f32[32,128]{1,0:T(8,128)S(1)}) custom-call(f32[32,128]{1,0:T(8,128)S(1)} %get-tuple-element.26.mine_ref, f32[32,128]{1,0:T(8,128)S(1)} %collective-permute-done.got_ref, f32[32,128]{1,0:T(8,128)S(1)} %get-tuple-element.27.own_ref, f32[30,64,64]{2,1,0:T(8,128)S(1)} %copy-done), custom_call_target="tpu_custom_call" | custom-call | tf_op jit(solution)/shard_map/row_hop/pallas_call | solution.py:494
  8.1 2.9 %collective-permute-start.1 = (f32[32,128]{1,0:T(8,128)S(1)}, f32[32,128]{1,0:T(8,128)S(1)}, u32[]{:S(2)}, u32[]{:S(2)}) collective-permute-start(f32[32,128]{1,0:T(8,128)S(1)} %get-tuple-element.28.mine_ref), channel_id=1, source_target_pairs={{0,2},{1,3},{2,0},{3,1},{4,6},{5,7},{6,4},{7,5},{8,10},{9,11},{10,... | collective-permute-start | bytes 49160 | tf_op jit(solution)/shard_map/ppermute | solution.py:435
  11.0 1.7 %collective-permute-done.1.got_ref = f32[32,128]{1,0:T(8,128)S(1)} collective-permute-done((f32[32,128]{1,0:T(8,128)S(1)}, f32[32,128]{1,0:T(8,128)S(1)}, u32[]{:S(2)}, u32[]{:S(2)}) %collective-permute-start.1) | collective-permute-done | bytes 16416 | tf_op jit(solution)/shard_map/ppermute | solution.py:435
  12.7 0.4 %row_hop.3 = (f32[32,128]{1,0:T(8,128)S(1)}, f32[64,128]{1,0:T(8,128)S(1)}) custom-call(f32[32,128]{1,0:T(8,128)S(1)} %get-tuple-element.28.mine_ref, f32[32,128]{1,0:T(8,128)S(1)} %collective-permute-done.1.got_ref, f32[32,128]{1,0:T(8,128)S(1)} %get-tuple-element.27.own_ref, f32[30,64,64]{2,1,0:T(8,128)S(1)} %copy-done), custom_call_target="tpu_custom_call" | custom-call | tf_op jit(solution)/shard_map/row_hop/pallas_call | solution.py:494
  13.1 2.1 %collective-permute-start.2 = (f32[64,128]{1,0:T(8,128)S(1)}, f32[64,128]{1,0:T(8,128)S(1)}, u32[]{:S(2)}, u32[]{:S(2)}) collective-permute-start(f32[64,128]{1,0:T(8,128)S(1)} %get-tuple-element.29.after_ref.mine_ref), channel_id=1, source_target_pairs={{0,4},{4,0},{8,12},{12,8},{16,20},{20,16},{24,28},{28,24},{1,5},{5... | collective-permute-start | bytes 98312 | tf_op jit(solution)/shard_map/ppermute | solution.py:435
  15.2 2.8 %factor.2 = (f32[16,64,128]{2,1,0:T(8,128)S(1)}, f32[8,128]{1,0:T(8,128)S(1)}) custom-call(f32[16,64,64]{2,1,0:T(8,128)S(1)} %get-tuple-element.30.grams_ref, f32[64,128]{1,0:T(8,128)S(1)} %get-tuple-element.29.after_ref.mine_ref), custom_call_target="tpu_custom_call" | custom-call | flops 5000000000 | bytes 8000000 | tf_op jit(solution)/shard_map/factor/pallas_call | solution.py:507
  18.0 0.0 collective-permute-done.2.got_ref
  18.0 0.4 %leaf_hop.2 = (f32[32,128]{1,0:T(8,128)S(1)}, f32[72,128]{1,0:T(8,128)S(1)}) custom-call(f32[64,128]{1,0:T(8,128)S(1)} %get-tuple-element.29.after_ref.mine_ref, f32[64,128]{1,0:T(8,128)S(1)} %collective-permute-done.2.got_ref, f32[30,64,64]{2,1,0:T(8,128)S(1)} %copy-done, f32[8,128]{1,0:T(8,128)S(1)} %get-tuple-element.31.after_ref), custom_call_target="tpu_custom_call" | custom-call | tf_op jit(solution)/shard_map/leaf_hop/pallas_call | solution.py:518
  18.4 1.6 %collective-permute-start.3 = (f32[72,128]{1,0:T(8,128)S(1)}, f32[72,128]{1,0:T(8,128)S(1)}, u32[]{:S(2)}, u32[]{:S(2)}) collective-permute-start(f32[72,128]{1,0:T(8,128)S(1)} %get-tuple-element.32.after_ref.mine_ref), channel_id=1, source_target_pairs={{0,8},{4,12},{8,0},{12,4},{16,24},{20,28},{24,16},{28,20},{1,9},{5... | collective-permute-start | bytes 110600 | tf_op jit(solution)/shard_map/ppermute | solution.py:435
  20.0 2.8 %factor.3 = (f32[16,64,128]{2,1,0:T(8,128)S(1)}, f32[8,128]{1,0:T(8,128)S(1)}) custom-call(f32[16,64,64]{2,1,0:T(8,128)S(1)} %get-tuple-element.33.grams_ref, f32[72,128]{1,0:T(8,128)S(1)} %get-tuple-element.32.after_ref.mine_ref), custom_call_target="tpu_custom_call" | custom-call | flops 5000000000 | bytes 8000000 | tf_op jit(solution)/shard_map/factor/pallas_call | solution.py:507
  22.8 0.0 collective-permute-done.3.got_ref
  22.8 0.4 %leaf_hop.3 = (f32[32,128]{1,0:T(8,128)S(1)}, f32[112,128]{1,0:T(8,128)S(1)}) custom-call(f32[72,128]{1,0:T(8,128)S(1)} %get-tuple-element.32.after_ref.mine_ref, f32[72,128]{1,0:T(8,128)S(1)} %collective-permute-done.3.got_ref, f32[30,64,64]{2,1,0:T(8,128)S(1)} %copy-done, f32[8,128]{1,0:T(8,128)S(1)} %get-tuple-element.34.after_ref), custom_call_target="tpu_custom_call" | custom-call | tf_op jit(solution)/shard_map/leaf_hop/pallas_call | solution.py:518
  23.2 2.6 %collective-permute-start.4 = (f32[112,128]{1,0:T(8,128)S(1)}, f32[112,128]{1,0:T(8,128)S(1)}, u32[]{:S(2)}, u32[]{:S(2)}) collective-permute-start(f32[112,128]{1,0:T(8,128)S(1)} %get-tuple-element.35.after_ref.mine_ref), channel_id=1, source_target_pairs={{0,16},{4,20},{8,24},{12,28},{16,0},{20,4},{24,8},{28,12},{1,17},{... | collective-permute-start | bytes 172040 | tf_op jit(solution)/shard_map/ppermute | solution.py:435
  25.9 0.0 copy-done.3
  25.9 2.2 %leaf.1 = (f32[32,64,256]{2,1,0:T(8,128)}, bf16[32,64,128]{2,1,0:T(8,128)(2,1)S(1)}, bf16[32,64,128]{2,1,0:T(8,128)(2,1)S(1)}) custom-call(f32[32,64,256]{2,1,0:T(8,128)S(1)} %copy-done.3, f32[32,64,64]{2,1,0:T(8,128)S(1)} %copy-done.4, f32[32,64,64]{2,1,0:T(8,128)S(1)} %copy-done.5, f32[112,128]{1,0:T(8,128)S(1)} %get-tuple-element.35.after_ref.mine_ref, ...), custom_call_target="tpu_custom_call" | custom-call | flops 5000000000 | bytes 8000000 | tf_op jit(solution)/shard_map/leaf/pallas_call | solution.py:528
  28.1 0.3 collective-permute-done.4.got_ref
  28.4 6.1 %top.1 = (f32[1,5,64,64]{3,2,1,0:T(8,128)}, f32[32,64,64]{2,1,0:T(8,128)}, f32[32,64,64]{2,1,0:T(8,128)}) custom-call(f32[112,128]{1,0:T(8,128)S(1)} %get-tuple-element.35.after_ref.mine_ref, f32[112,128]{1,0:T(8,128)S(1)} %collective-permute-done.4.got_ref, f32[32,128]{1,0:T(8,128)S(1)} %get-tuple-element.39.refs_0_, ...), custom_call_target="tpu_custom_call" | custom-call | tf_op jit(solution)/shard_map/top/pallas_call | solution.py:543
  (7 shorter events, 0.0 us)
Async XLA Ops:
  0.6 7.0 %copy-start = (f32[30,64,64]{2,1,0:T(8,128)S(1)}, f32[30,64,64]{2,1,0:T(8,128)}, u32[]{:S(2)}) copy-start(f32[30,64,64]{2,1,0:T(8,128)} %refs_4_.1) | copy-start | bytes 1474564
  0.6 0.8 %copy-start.1 = (f32[1,64,64]{2,1,0:T(8,128)S(1)}, f32[1,64,64]{2,1,0:T(8,128)}, u32[]{:S(2)}) copy-start(f32[1,64,64]{2,1,0:T(8,128)} %refs_5_.1) | copy-start | bytes 49156
  6.3 1.4 %collective-permute-start = (f32[32,128]{1,0:T(8,128)S(1)}, f32[32,128]{1,0:T(8,128)S(1)}, u32[]{:S(2)}, u32[]{:S(2)}) collective-permute-start(f32[32,128]{1,0:T(8,128)S(1)} %get-tuple-element.26.mine_ref), channel_id=1, source_target_pairs={{0,1},{1,0},{2,3},{3,2},{4,5},{5,4},{6,7},{7,6},{8,9},{9,8},{10,11... | collective-permute-start | bytes 49160 | tf_op jit(solution)/shard_map/ppermute | solution.py:435
  8.1 4.6 %collective-permute-start.1 = (f32[32,128]{1,0:T(8,128)S(1)}, f32[32,128]{1,0:T(8,128)S(1)}, u32[]{:S(2)}, u32[]{:S(2)}) collective-permute-start(f32[32,128]{1,0:T(8,128)S(1)} %get-tuple-element.28.mine_ref), channel_id=1, source_target_pairs={{0,2},{1,3},{2,0},{3,1},{4,6},{5,7},{6,4},{7,5},{8,10},{9,11},{10,... | collective-permute-start | bytes 49160 | tf_op jit(solution)/shard_map/ppermute | solution.py:435
  13.1 4.8 %collective-permute-start.2 = (f32[64,128]{1,0:T(8,128)S(1)}, f32[64,128]{1,0:T(8,128)S(1)}, u32[]{:S(2)}, u32[]{:S(2)}) collective-permute-start(f32[64,128]{1,0:T(8,128)S(1)} %get-tuple-element.29.after_ref.mine_ref), channel_id=1, source_target_pairs={{0,4},{4,0},{8,12},{12,8},{16,20},{20,16},{24,28},{28,24},{1,5},{5... | collective-permute-start | bytes 98312 | tf_op jit(solution)/shard_map/ppermute | solution.py:435
  18.4 4.4 %collective-permute-start.3 = (f32[72,128]{1,0:T(8,128)S(1)}, f32[72,128]{1,0:T(8,128)S(1)}, u32[]{:S(2)}, u32[]{:S(2)}) collective-permute-start(f32[72,128]{1,0:T(8,128)S(1)} %get-tuple-element.32.after_ref.mine_ref), channel_id=1, source_target_pairs={{0,8},{4,12},{8,0},{12,4},{16,24},{20,28},{24,16},{28,20},{1,9},{5... | collective-permute-start | bytes 110600 | tf_op jit(solution)/shard_map/ppermute | solution.py:435
  20.0 5.9 %copy-start.3 = (f32[32,64,256]{2,1,0:T(8,128)S(1)}, f32[32,64,256]{2,1,0:T(8,128)}, u32[]{:S(2)}) copy-start(f32[32,64,256]{2,1,0:T(8,128)} %basis_ref.1) | copy-start | bytes 6291460
  20.0 5.9 %copy-start.4 = (f32[32,64,64]{2,1,0:T(8,128)S(1)}, f32[32,64,64]{2,1,0:T(8,128)}, u32[]{:S(2)}) copy-start(f32[32,64,64]{2,1,0:T(8,128)} %trans_ref.1) | copy-start | bytes 1572868
  20.0 5.9 %copy-start.5 = (f32[32,64,64]{2,1,0:T(8,128)S(1)}, f32[32,64,64]{2,1,0:T(8,128)}, u32[]{:S(2)}) copy-start(f32[32,64,64]{2,1,0:T(8,128)} %coup_ref.1) | copy-start | bytes 1572868
  23.2 5.2 %collective-permute-start.4 = (f32[112,128]{1,0:T(8,128)S(1)}, f32[112,128]{1,0:T(8,128)S(1)}, u32[]{:S(2)}, u32[]{:S(2)}) collective-permute-start(f32[112,128]{1,0:T(8,128)S(1)} %get-tuple-element.35.after_ref.mine_ref), channel_id=1, source_target_pairs={{0,16},{4,20},{8,24},{12,28},{16,0},{20,4},{24,8},{28,12},{1,17},{... | collective-permute-start | bytes 172040 | tf_op jit(solution)/shard_map/ppermute | solution.py:435
  25.9 2.5 %copy-start.2 = (s32[32]{0:T(128)S(1)}, s32[32]{0:T(128)}, u32[]{:S(2)}) copy-start(s32[32]{0:T(128)} %refs_8_.1) | copy-start | bytes 388

commit v6 on v5

--- a/solution.py
+++ b/solution.py
@@ -73,18 +73,18 @@
     return terms[0]
 
 
-def load_sets(flat, w_ref):
+def load_sets(flat, w_ref, alone=False):
     sets, groups, rank = w_ref.shape[0], w_ref.shape[1], w_ref.shape[2]
     for t in range(sets):
         for ib in range(groups):
             rows = [
-                flat[pl.ds(t * SET * rank + ib * SUB + s, SET, stride=rank), :]
+                flat[pl.ds(t * SET * rank + ib * SUB + s, SET, stride=0 if alone else rank), :]
                 for s in range(SUB)
             ]
             w_ref[t, ib] = jnp.concatenate(rows, axis=0).T
 
 
-def eliminate(w_ref, g_ref, out):
+def eliminate(w_ref, g_ref, out, alone=False):
     sets, groups, rank = w_ref.shape[0], w_ref.shape[1], w_ref.shape[2]
     place = lax.broadcasted_iota(jnp.int32, (SUB, LANES), 0)
     lane = lax.broadcasted_iota(jnp.int32, (SUB, LANES), 1)
@@ -121,70 +121,84 @@
             value = jnp.where(group == p, parts[p], value)
         return value
 
-    def panel(t, kb, rows, inverses, roots):
-        mult = {(p, q): spread(rows[p], q) for p in range(SUB) for q in range(p)}
+    def copied(ref, row):
+        return ref[pl.ds(row, SUB, stride=0), :]
+
+    def panel(t, kb, rows):
+        for p in range(SUB):
+            g_ref[t, p, pl.ds(kb * SUB, SUB), :] = rows[p]
+        for jv in [kb + 1 + n for n in range(groups - 1 - kb)] + list(range(kb)):
+            value = tile(t, kb, jv)
+            for p in range(SUB):
+                g_ref[t, p, pl.ds(jv * SUB, SUB), :] = picked(value, p)
+        return {
+            (p, q): copied(g_ref.at[t, p], kb * SUB + q) for p in range(SUB) for q in range(p)
+        }
+
+    def store(t, kb, mult, rows, roots):
         root = merged(roots)
+        zero = jnp.zeros((SUB, LANES), F32)
+        lanes = [
+            merged([mult[p, q] if p > q else zero for p in range(SUB)]) for q in range(SUB - 1)
+        ]
         upper, lower = [], []
         for jv in range(groups):
             if jv == kb:
-                for p in range(SUB):
-                    unit = jnp.where(place == p, 1.0, 0.0)
-                    g_ref[t, p, pl.ds(jv * SUB, SUB), :] = jnp.where(place < p, rows[p], unit)
                 final = merged(rows) * root
                 upper.append(jnp.where(place >= group, final, 0.0))
                 unit = jnp.where(place == group, root, 0.0)
                 lower.append(jnp.where(place < group, final, unit))
                 continue
-            value = tile(t, kb, jv)
-            old = [picked(value, p) for p in range(SUB)]
-            new = []
-            for p in range(SUB):
-                term = added([old[p]] + [mult[p, q] * old[q] for q in range(p)])
-                g_ref[t, p, pl.ds(jv * SUB, SUB), :] = term
-                new.append(term)
-            final = merged(new) * root
-            zero = jnp.zeros((SUB, LANES), F32)
+            terms = [lanes[q] * g_ref[t, q, pl.ds(jv * SUB, SUB), :] for q in range(SUB - 1)]
+            final = added([tile(t, kb, jv)] + terms) * root
             upper.append(final if jv > kb else zero)
             lower.append(final if jv < kb else zero)
-        return mult, jnp.concatenate(upper + lower, axis=0)
-
-    def store(t, kb, factors):
-        turned = factors.T
+        turned = jnp.concatenate(upper + lower, axis=0).T
         for s in range(SUB):
-            out[pl.ds(t * SET * rank + kb * SUB + s, SET, stride=rank), :] = turned[
-                s * SET : (s + 1) * SET
-            ]
+            if alone:
+                out[pl.ds(kb * SUB + s, 1), :] = turned[s * SET : s * SET + 1]
+            else:
+                out[pl.ds(t * SET * rank + kb * SUB + s, SET, stride=rank), :] = turned[
+                    s * SET : (s + 1) * SET
+                ]
 
     def weights(t, kb, ib, mult, inverses):
-        value = tile(t, ib, kb)
-        columns = [spread(value, q) for q in range(SUB)]
+        columns = [copied(w_ref.at[t, ib], kb * SUB + q) for q in range(SUB)]
         found = []
         for q in range(SUB):
             term = added([columns[q]] + [mult[q, r] * columns[r] for r in range(q)])
             found.append(term * inverses[q])
-        return found
+        return [
+            added([found[r]] + [found[q] * mult[q, r] for q in range(r + 1, SUB)])
+            for r in range(SUB)
+        ]
 
     def trail(t, kb, ib, jv, found):
-        terms = [found[q] * g_ref[t, q, pl.ds(jv * SUB, SUB), :] for q in range(SUB)]
-        acc = -added(terms) if jv == kb else tile(t, ib, jv) - added(terms)
-        w_ref[t, ib, pl.ds(jv * SUB, SUB), :] = acc
+        if jv == kb:
+            value = -found[0]
+            for r in range(1, SUB):
+                value = jnp.where(place == r, -found[r], value)
+        else:
+            terms = [found[r] * g_ref[t, r, pl.ds(jv * SUB, SUB), :] for r in range(SUB)]
+            value = tile(t, ib, jv) - added(terms)
+        w_ref[t, ib, pl.ds(jv * SUB, SUB), :] = value
 
     corners = [corner(t, 0) for t in range(sets)]
     for kb in range(groups):
-        panels = [panel(t, kb, *corners[t]) for t in range(sets)]
+        mults = [panel(t, kb, corners[t][0]) for t in range(sets)]
         ahead = []
         if kb + 1 < groups:
             for t in range(sets):
-                found = weights(t, kb, kb + 1, panels[t][0], corners[t][1])
+                found = weights(t, kb, kb + 1, mults[t], corners[t][1])
                 for jv in [kb + 1] + [jv for jv in range(groups) if jv != kb + 1]:
                     trail(t, kb, kb + 1, jv, found)
             ahead = [corner(t, kb + 1) for t in range(sets)]
         for t in range(sets):
             for ib in range(kb + 2, groups):
-                found = weights(t, kb, ib, panels[t][0], corners[t][1])
+                found = weights(t, kb, ib, mults[t], corners[t][1])
                 for jv in range(groups):
                     trail(t, kb, ib, jv, found)
-            store(t, kb, panels[t][1])
+            store(t, kb, mults[t], corners[t][0], corners[t][2])
         corners = ahead
 
 
@@ -263,7 +277,18 @@
     token_ref[...] = jnp.zeros(token_ref.shape, F32)
 
 
-def row_hop_kernel(bit, last, mine_ref, got_ref, own_ref, upper_ref, path_ref, next_ref):
+def own_kernel(own_ref, after_ref, out_ref, token_ref, full_ref, w_ref, g_ref):
+    del after_ref
+    full_ref[...] = unpack(own_ref[...])
+    load_sets(full_ref, w_ref, alone=True)
+    eliminate(w_ref, g_ref, out_ref, alone=True)
+    token_ref[...] = jnp.zeros(token_ref.shape, F32)
+
+
+def row_hop_kernel(
+    bit, last, mine_ref, got_ref, own_ref, upper_ref, after_ref, path_ref, next_ref
+):
+    del after_ref
     n_rows, n_leaf = lax.axis_size("rows"), lax.axis_size("leaf")
     level = (n_rows * n_leaf).bit_length() - 2 - bit
     myself = lax.axis_index("leaf") * n_rows + lax.axis_index("rows")
@@ -319,27 +344,45 @@
         next_ref[half + size :] = got_ref[half:]
 
 
-def leaf_kernel(steps, sets, basis_ref, trans_ref, coup_ref, after_ref, *refs):
+def leaf_kernel(steps, sets, basis_ref, trans_ref, coup_ref, own_ref, after_ref, *refs):
     del after_ref
     factor_refs = refs[:sets]
-    orth_hbm, moved_ref, split_ref, orth_ref, orth_sem = refs[sets:]
+    (
+        orth_hbm,
+        bridge_hbm,
+        split_ref,
+        orth_ref,
+        bridge_ref,
+        orth_sem,
+        bridge_sem,
+    ) = refs[sets:]
     leaves, rank = basis_ref.shape[0], basis_ref.shape[1]
     chunk = leaves // steps
     lane = lax.broadcasted_iota(jnp.int32, (rank, 2 * rank), 1)
+    own_upper = twice(pair(own_ref[:, :rank]))
+    own_inverse = broad(own_ref[:, rank:])
     copies = []
+
+    def send(source, target, sem):
+        copies.append(pltpu.make_async_copy(source, target, sem))
+        copies[-1].start()
+
     for step in range(steps):
+        moved = []
         for n in range(step * chunk, (step + 1) * chunk):
             high, low = halves(factor_refs[n // SET][n % SET])
             low = jnp.concatenate([low[:, rank:], low[:, :rank]], axis=1)
             upper = jnp.where(lane < rank, high, low).astype(B16)
             inverse = jnp.where(lane < rank, low, high).astype(B16)
+            moved.append(mm(twice(upper), tall(trans_ref[n])))
             orth_ref[n] = mm(twice(inverse), tall(basis_ref[n]))
-            moved_ref[n] = pair(mm(twice(upper), tall(trans_ref[n])))
-            split_ref[n] = pair(coup_ref[n])
         span = pl.ds(step * chunk, chunk)
-        copy = pltpu.make_async_copy(orth_ref.at[span], orth_hbm.at[span], orth_sem.at[step])
-        copy.start()
-        copies.append(copy)
+        send(orth_ref.at[span], orth_hbm.at[span], orth_sem.at[step])
+        moved = twice(pair(jnp.concatenate(moved, axis=0)))
+        bridge_ref[span] = mm_nt(moved, own_inverse).reshape(chunk, rank, rank)
+        send(bridge_ref.at[span], bridge_hbm.at[span], bridge_sem.at[step])
+    for b in range(coup_ref.shape[0]):
+        split_ref[b] = pair(mm(own_upper, tall(coup_ref[b])))
     for copy in copies:
         copy.wait()
 
@@ -350,20 +393,17 @@
     (
         upper_ref,
         dev_ref,
-        moved_ref,
+        own_ref,
         split_ref,
         offset_ref,
         fresh_hbm,
-        bridge_hbm,
         coupled_hbm,
         grams_ref,
         factor_ref,
         cols_ref,
         fresh_ref,
-        bridge_ref,
         coupled_ref,
         fresh_sem,
-        bridge_sem,
         coupled_sem,
         w_ref,
         g_ref,
@@ -384,9 +424,6 @@
     count = grams_ref.shape[0]
     load_sets(grams_ref.reshape(count * rank, rank), w_ref)
     eliminate(w_ref, g_ref, factor_ref.reshape(count * rank, 2 * rank))
-    own = factor_ref[levels]
-    own_upper = twice(pair(own[:, :rank]))
-    own_inverse = broad(own[:, rank:])
     for n in range(n_leaf):
         cols_ref[n] = broad(factor_ref[levels + n, :, :rank])
     copies = []
@@ -395,7 +432,7 @@
         copies.append(pltpu.make_async_copy(source, target, sem))
         copies[-1].start()
 
-    lows, edges, inverses = [own_upper], [tall(dev_ref[0])], []
+    lows, edges, inverses = [twice(pair(own_ref[:, :rank]))], [tall(dev_ref[0])], []
     for k in range(levels):
         inverses.append(broad(factor_ref[k, :, rank:]))
         if k:
@@ -406,24 +443,13 @@
     for k in range(levels):
         fresh_ref[0, k] = mm_nt(inner[k], inverses[k])
     send(fresh_ref, fresh_hbm, fresh_sem)
-    leaves = moved_ref.shape[0]
-    chunk = leaves // steps
-    for step in range(steps):
-        span = pl.ds(step * chunk, chunk)
-        moved = twice(moved_ref[span].reshape(chunk * rank, 2 * rank))
-        bridge_ref[span] = mm_nt(moved, own_inverse).reshape(chunk, rank, rank)
-        send(bridge_ref.at[span], bridge_hbm.at[span], bridge_sem.at[step])
     blocks = split_ref.shape[0]
     chunk = blocks // steps
     for step in range(steps):
-        inner = []
         for b in range(step * chunk, (step + 1) * chunk):
             target = lax.rem(myself + offset_ref[b], n_rows * n_leaf)
             column = cols_ref[(target // n_rows) ^ branch]
-            inner.append(mm_nt(twice(split_ref[b]), column))
-        inner = [tall(value) for value in inner]
-        for n in range(chunk):
-            coupled_ref[step * chunk + n] = mm(own_upper, inner[n])
+            coupled_ref[b] = mm_nt(twice(split_ref[b]), column)
         span = pl.ds(step * chunk, chunk)
         send(coupled_ref.at[span], coupled_hbm.at[span], coupled_sem.at[step])
     for copy in copies:
@@ -491,14 +517,25 @@
     for bit in range(row_bits):
         got = swap(carry, "rows", bit)
         last = bit == row_bits - 1
+        if bit == 1:
+            own_factor, token = pl.pallas_call(
+                own_kernel,
+                in_specs=[vmem, any_place],
+                out_specs=[vmem, vmem],
+                out_shape=[shape(rank, 2 * rank), shape(SUB, LANES)],
+                scratch_shapes=[pltpu.VMEM((rank, rank), F32)] + scratch(1),
+                compiler_params=params,
+                cost_estimate=cost(5 * 10**9, 8 * 10**6),
+                name="own",
+            )(own_gram, carry)
         gram, carry = pl.pallas_call(
             functools.partial(row_hop_kernel, bit, last),
-            in_specs=[vmem] * 4,
+            in_specs=[vmem] * 4 + [any_place],
             out_specs=[vmem, vmem],
             out_shape=[shape(half, 2 * rank), shape(rank if last else half, 2 * rank)],
             compiler_params=params,
             name="row_hop",
-        )(carry, got, own_gram, upper_transfer)
+        )(carry, got, own_gram, upper_transfer, token if bit == 1 else own_gram)
         path.append(gram)
     factors = []
     for bit in range(leaf_bits - 1):
@@ -525,45 +562,44 @@
         )(carry, got, upper_transfer, token)
         path.append(gram)
     got = swap(carry, "leaf", leaf_bits - 1)
-    leaf_orth, moved, split = pl.pallas_call(
+    leaf_orth, leaf_bridge, split = pl.pallas_call(
         functools.partial(leaf_kernel, steps, sets),
-        in_specs=[vmem] * 3 + [any_place] + [vmem] * sets,
-        out_specs=[hbm, vmem, vmem],
+        in_specs=[vmem] * 4 + [any_place] + [vmem] * sets,
+        out_specs=[hbm, hbm, vmem],
         out_shape=[
             like(leaf_basis),
-            shape(leaves, rank, 2 * rank, kind=B16),
+            like(leaf_transfer),
             shape(blocks, rank, 2 * rank, kind=B16),
         ],
-        scratch_shapes=[pltpu.VMEM(leaf_basis.shape, F32), pltpu.SemaphoreType.DMA((steps,))],
+        scratch_shapes=[
+            pltpu.VMEM(leaf_basis.shape, F32),
+            pltpu.VMEM(leaf_transfer.shape, F32),
+            pltpu.SemaphoreType.DMA((steps,)),
+            pltpu.SemaphoreType.DMA((steps,)),
+        ],
         compiler_params=params,
         cost_estimate=cost(5 * 10**9, 8 * 10**6),
         name="leaf",
-    )(leaf_basis, leaf_transfer, couplings, carry, *factors)
+    )(leaf_basis, leaf_transfer, couplings, own_factor, carry, *factors)
     sets = -(-(levels + n_leaf) // SET)
-    new_transfers, leaf_bridge, coupled = pl.pallas_call(
+    new_transfers, coupled = pl.pallas_call(
         functools.partial(top_kernel, n_rows, n_leaf, steps),
         in_specs=[vmem] * (levels + 5) + [smem],
-        out_specs=[hbm, hbm, hbm],
-        out_shape=[
-            shape(1, levels, rank, rank),
-            like(leaf_transfer),
-            like(couplings),
-        ],
+        out_specs=[hbm, hbm],
+        out_shape=[shape(1, levels, rank, rank), like(couplings)],
         scratch_shapes=[
             pltpu.VMEM((sets * SET, rank, rank), F32),
             pltpu.VMEM((sets * SET, rank, 2 * rank), F32),
             pltpu.VMEM((n_leaf, rank, 4 * rank), B16),
             pltpu.VMEM((1, levels, rank, rank), F32),
-            pltpu.VMEM(leaf_transfer.shape, F32),
             pltpu.VMEM(couplings.shape, F32),
             pltpu.SemaphoreType.DMA(()),
-            pltpu.SemaphoreType.DMA((steps,)),
             pltpu.SemaphoreType.DMA((steps,)),
         ]
         + scratch(sets),
         compiler_params=params,
         name="top",
-    )(carry, got, *path, upper_transfer, device_transfer, moved, split, couple_offset)
+    )(carry, got, *path, upper_transfer, device_transfer, own_factor, split, couple_offset)
     return (leaf_orth, leaf_bridge, new_transfers, coupled)
 
 

time: 34.6 us -> 34.4 us (level)
  Pallas kernels: 20.3 us -> 22.3 us
  waiting for transfers between devices: 2.83 us -> 0.85 us
  starting transfers between devices: 9.79 us -> 9.31 us
    pallas_call x0 -> x1, Pallas kernels: none -> 2.6 us  [per_device(): pl.pallas_call(own_kernel, in_specs=[vmem, any_place], out_specs=[vmem, v...]
    ppermute x5, waiting for transfers between devices: 2.83 us -> 0.85 us  [swap(): return lax.ppermute(value, axis, pairs)]
    pallas_call x1, Pallas kernels: 6.1 us -> 4.93 us  [per_device(): pl.pallas_call(functools.partial(top_kernel, n_rows, n_leaf, steps), in_s...]
    pallas_call x1, Pallas kernels: 2.21 us -> 2.94 us  [per_device(): pl.pallas_call(functools.partial(leaf_kernel, steps, sets), in_specs=[vme...]
    ppermute x5, starting transfers between devices: 9.79 us -> 9.31 us  [swap(): return lax.ppermute(value, axis, pairs)]
  transfers between devices with their start and end apart: 5 -> 5, of which waited for: 3 -> 1; matrix products, arithmetic and copies ran while one was open for 0% -> 0% of each run, Pallas kernels for 22% -> 32%
where the time goes in v6:
time: 34.4 us; the launch traced here: 34.3 us
  Pallas kernels  22.3 us (65%)
  starting transfers between devices  9.31 us (27%)
  between operations  0.93 us (3%)
  local copies, waits for them, and re-layouts  0.85 us (2%)
  waiting for transfers between devices  0.85 us (2%)
    ppermute x5, starting transfers between devices, swap(): return lax.ppermute(value, axis, pairs)  9.31 us
    pallas_call x2, Pallas kernels, per_device(): pl.pallas_call(factor_kernel, in_specs=[vmem, any_place], out_specs=[vmem...  5.43 us
    pallas_call x1, Pallas kernels, per_device(): pl.pallas_call(functools.partial(top_kernel, n_rows, n_leaf, steps), in_s...  4.93 us
    pallas_call x1, Pallas kernels, per_device(): pl.pallas_call(functools.partial(gram_kernel, steps, sets), in_specs=[hbm...  4.8 us
    pallas_call x1, Pallas kernels, per_device(): pl.pallas_call(functools.partial(leaf_kernel, steps, sets), in_specs=[vme...  2.94 us
    pallas_call x1, Pallas kernels, per_device(): pl.pallas_call(own_kernel, in_specs=[vmem, any_place], out_specs=[vmem, v...  2.6 us
    unnamed x12, local copies, waits for them, and re-layouts  0.85 us
    ppermute x5, waiting for transfers between devices, swap(): return lax.ppermute(value, axis, pairs)  0.85 us
  transfers between devices with their start and end apart: 5, of which 1 were waited for; matrix products, arithmetic and copies ran while one was open for 0% of the time, Pallas kernels for 32%

profile of v6, /device:TPU:0, one launch (start us, length us, event | category | flops | bytes accessed | tf_op | source)
XLA Modules:
  0.0 34.3 jit_solution(5281470279852217214)
XLA Ops:
  0.6 0.0 copy-start
  0.6 0.0 copy-start.1
  0.7 0.8 %copy-done.1 = f32[1,64,64]{2,1,0:T(8,128)S(1)} copy-done((f32[1,64,64]{2,1,0:T(8,128)S(1)}, f32[1,64,64]{2,1,0:T(8,128)}, u32[]{:S(2)}) %copy-start.1) | copy-done | bytes 16408
  1.5 4.8 %gram.1 = (f32[16,64,64]{2,1,0:T(8,128)S(1)}, f32[16,64,64]{2,1,0:T(8,128)S(1)}, f32[32,128]{1,0:T(8,128)S(1)}, f32[32,128]{1,0:T(8,128)S(1)}) custom-call(f32[32,64,256]{2,1,0:T(8,128)} %basis_ref.1, f32[32,64,64]{2,1,0:T(8,128)} %trans_ref.1, f32[1,64,64]{2,1,0:T(8,128)S(1)} %copy-done.1), custom_call_target="tpu_custom_call" | custom-call | flops 1000000000 | bytes 4000000 | tf_op jit(solution)/shard_map/gram/pallas_call | solution.py:500
  6.3 0.5 %collective-permute-start = (f32[32,128]{1,0:T(8,128)S(1)}, f32[32,128]{1,0:T(8,128)S(1)}, u32[]{:S(2)}, u32[]{:S(2)}) collective-permute-start(f32[32,128]{1,0:T(8,128)S(1)} %get-tuple-element.28.mine_ref), channel_id=1, source_target_pairs={{0,1},{1,0},{2,3},{3,2},{4,5},{5,4},{6,7},{7,6},{8,9},{9,8},{10,11... | collective-permute-start | bytes 49160 | tf_op jit(solution)/shard_map/ppermute | solution.py:461
  6.8 0.8 %collective-permute-done.got_ref = f32[32,128]{1,0:T(8,128)S(1)} collective-permute-done((f32[32,128]{1,0:T(8,128)S(1)}, f32[32,128]{1,0:T(8,128)S(1)}, u32[]{:S(2)}, u32[]{:S(2)}) %collective-permute-start) | collective-permute-done | bytes 16416 | tf_op jit(solution)/shard_map/ppermute | solution.py:461
  7.7 0.4 %row_hop.2 = (f32[32,128]{1,0:T(8,128)S(1)}, f32[32,128]{1,0:T(8,128)S(1)}) custom-call(f32[32,128]{1,0:T(8,128)S(1)} %get-tuple-element.28.mine_ref, f32[32,128]{1,0:T(8,128)S(1)} %collective-permute-done.got_ref, f32[32,128]{1,0:T(8,128)S(1)} %get-tuple-element.27.own_ref.after_ref, f32[30,64,64]{2,1,0:T(8,128)S(1)} %copy-done, ...), custom_call_target="tpu_custom_call" | custom-call | tf_op jit(solution)/shard_map/row_hop/pallas_call | solution.py:531
  8.1 2.9 %collective-permute-start.1 = (f32[32,128]{1,0:T(8,128)S(1)}, f32[32,128]{1,0:T(8,128)S(1)}, u32[]{:S(2)}, u32[]{:S(2)}) collective-permute-start(f32[32,128]{1,0:T(8,128)S(1)} %get-tuple-element.29.after_ref.mine_ref), channel_id=1, source_target_pairs={{0,2},{1,3},{2,0},{3,1},{4,6},{5,7},{6,4},{7,5},{8,10},{9,11},{10,... | collective-permute-start | bytes 49160 | tf_op jit(solution)/shard_map/ppermute | solution.py:461
  11.0 2.6 %own.1 = (f32[64,128]{1,0:T(8,128)S(1)}, f32[8,128]{1,0:T(8,128)S(1)}) custom-call(f32[32,128]{1,0:T(8,128)S(1)} %get-tuple-element.27.own_ref.after_ref, f32[32,128]{1,0:T(8,128)S(1)} %get-tuple-element.29.after_ref.mine_ref), custom_call_target="tpu_custom_call" | custom-call | flops 5000000000 | bytes 8000000 | tf_op jit(solution)/shard_map/own/pallas_call | solution.py:521
  13.6 0.0 collective-permute-done.1.got_ref
  13.6 0.4 %row_hop.3 = (f32[32,128]{1,0:T(8,128)S(1)}, f32[64,128]{1,0:T(8,128)S(1)}) custom-call(f32[32,128]{1,0:T(8,128)S(1)} %get-tuple-element.29.after_ref.mine_ref, f32[32,128]{1,0:T(8,128)S(1)} %collective-permute-done.1.got_ref, f32[32,128]{1,0:T(8,128)S(1)} %get-tuple-element.27.own_ref.after_ref, f32[30,64,64]{2,1,0:T(8,128)S(1)} %copy-done, ...), custom_call_target="tpu_custom_call" | custom-call | tf_op jit(solution)/shard_map/row_hop/pallas_call | solution.py:531
  14.0 1.6 %collective-permute-start.2 = (f32[64,128]{1,0:T(8,128)S(1)}, f32[64,128]{1,0:T(8,128)S(1)}, u32[]{:S(2)}, u32[]{:S(2)}) collective-permute-start(f32[64,128]{1,0:T(8,128)S(1)} %get-tuple-element.32.after_ref.mine_ref), channel_id=1, source_target_pairs={{0,4},{4,0},{8,12},{12,8},{16,20},{20,16},{24,28},{28,24},{1,5},{5... | collective-permute-start | bytes 98312 | tf_op jit(solution)/shard_map/ppermute | solution.py:461
  15.6 2.7 %factor.2 = (f32[16,64,128]{2,1,0:T(8,128)S(1)}, f32[8,128]{1,0:T(8,128)S(1)}) custom-call(f32[16,64,64]{2,1,0:T(8,128)S(1)} %get-tuple-element.33.grams_ref, f32[64,128]{1,0:T(8,128)S(1)} %get-tuple-element.32.after_ref.mine_ref), custom_call_target="tpu_custom_call" | custom-call | flops 5000000000 | bytes 8000000 | tf_op jit(solution)/shard_map/factor/pallas_call | solution.py:544
  18.3 0.0 collective-permute-done.2.got_ref
  18.3 0.4 %leaf_hop.2 = (f32[32,128]{1,0:T(8,128)S(1)}, f32[72,128]{1,0:T(8,128)S(1)}) custom-call(f32[64,128]{1,0:T(8,128)S(1)} %get-tuple-element.32.after_ref.mine_ref, f32[64,128]{1,0:T(8,128)S(1)} %collective-permute-done.2.got_ref, f32[30,64,64]{2,1,0:T(8,128)S(1)} %copy-done, f32[8,128]{1,0:T(8,128)S(1)} %get-tuple-element.34.after_ref), custom_call_target="tpu_custom_call" | custom-call | tf_op jit(solution)/shard_map/leaf_hop/pallas_call | solution.py:555
  18.7 1.6 %collective-permute-start.3 = (f32[72,128]{1,0:T(8,128)S(1)}, f32[72,128]{1,0:T(8,128)S(1)}, u32[]{:S(2)}, u32[]{:S(2)}) collective-permute-start(f32[72,128]{1,0:T(8,128)S(1)} %get-tuple-element.35.after_ref.mine_ref), channel_id=1, source_target_pairs={{0,8},{4,12},{8,0},{12,4},{16,24},{20,28},{24,16},{28,20},{1,9},{5... | collective-permute-start | bytes 110600 | tf_op jit(solution)/shard_map/ppermute | solution.py:461
  20.4 2.7 %factor.3 = (f32[16,64,128]{2,1,0:T(8,128)S(1)}, f32[8,128]{1,0:T(8,128)S(1)}) custom-call(f32[16,64,64]{2,1,0:T(8,128)S(1)} %get-tuple-element.36.grams_ref, f32[72,128]{1,0:T(8,128)S(1)} %get-tuple-element.35.after_ref.mine_ref), custom_call_target="tpu_custom_call" | custom-call | flops 5000000000 | bytes 8000000 | tf_op jit(solution)/shard_map/factor/pallas_call | solution.py:544
  23.1 0.0 collective-permute-done.3.got_ref
  23.1 0.4 %leaf_hop.3 = (f32[32,128]{1,0:T(8,128)S(1)}, f32[112,128]{1,0:T(8,128)S(1)}) custom-call(f32[72,128]{1,0:T(8,128)S(1)} %get-tuple-element.35.after_ref.mine_ref, f32[72,128]{1,0:T(8,128)S(1)} %collective-permute-done.3.got_ref, f32[30,64,64]{2,1,0:T(8,128)S(1)} %copy-done, f32[8,128]{1,0:T(8,128)S(1)} %get-tuple-element.37.after_ref), custom_call_target="tpu_custom_call" | custom-call | tf_op jit(solution)/shard_map/leaf_hop/pallas_call | solution.py:555
  23.5 2.7 %collective-permute-start.4 = (f32[112,128]{1,0:T(8,128)S(1)}, f32[112,128]{1,0:T(8,128)S(1)}, u32[]{:S(2)}, u32[]{:S(2)}) collective-permute-start(f32[112,128]{1,0:T(8,128)S(1)} %get-tuple-element.38.after_ref.mine_ref), channel_id=1, source_target_pairs={{0,16},{4,20},{8,24},{12,28},{16,0},{20,4},{24,8},{28,12},{1,17},{... | collective-permute-start | bytes 172040 | tf_op jit(solution)/shard_map/ppermute | solution.py:461
  26.2 0.0 copy-done.4
  26.2 2.9 %leaf.1 = (f32[32,64,256]{2,1,0:T(8,128)}, f32[32,64,64]{2,1,0:T(8,128)}, bf16[32,64,128]{2,1,0:T(8,128)(2,1)S(1)}) custom-call(f32[32,64,256]{2,1,0:T(8,128)S(1)} %copy-done.3, f32[32,64,64]{2,1,0:T(8,128)S(1)} %copy-done.4, f32[32,64,64]{2,1,0:T(8,128)S(1)} %copy-done.5, f32[64,128]{1,0:T(8,128)S(1)} %get-tuple-element.30.own_ref.refs_6_, ...), custom_call_target="tpu_custom_call" | custom-call | flops 5000000000 | bytes 8000000 | tf_op jit(solution)/shard_map/leaf/pallas_call | solution.py:565
  29.2 0.0 collective-permute-done.4.got_ref
  29.2 4.9 %top.1 = (f32[1,5,64,64]{3,2,1,0:T(8,128)}, f32[32,64,64]{2,1,0:T(8,128)}) custom-call(f32[112,128]{1,0:T(8,128)S(1)} %get-tuple-element.38.after_ref.mine_ref, f32[112,128]{1,0:T(8,128)S(1)} %collective-permute-done.4.got_ref, f32[32,128]{1,0:T(8,128)S(1)} %get-tuple-element.43.refs_0_, f32[32,128]{1,0:T(8,128)S(1)} %get-tuple-element.44.refs_1_, ...), custom_call_target="tpu_custom_call" | custom-call | tf_op jit(solution)/shard_map/top/pallas_call | solution.py:585
  (8 shorter events, 0.0 us)
Async XLA Ops:
  0.6 7.0 %copy-start = (f32[30,64,64]{2,1,0:T(8,128)S(1)}, f32[30,64,64]{2,1,0:T(8,128)}, u32[]{:S(2)}) copy-start(f32[30,64,64]{2,1,0:T(8,128)} %refs_4_.1) | copy-start | bytes 1474564
  0.6 0.8 %copy-start.1 = (f32[1,64,64]{2,1,0:T(8,128)S(1)}, f32[1,64,64]{2,1,0:T(8,128)}, u32[]{:S(2)}) copy-start(f32[1,64,64]{2,1,0:T(8,128)} %refs_5_.1) | copy-start | bytes 49156
  6.3 1.4 %collective-permute-start = (f32[32,128]{1,0:T(8,128)S(1)}, f32[32,128]{1,0:T(8,128)S(1)}, u32[]{:S(2)}, u32[]{:S(2)}) collective-permute-start(f32[32,128]{1,0:T(8,128)S(1)} %get-tuple-element.28.mine_ref), channel_id=1, source_target_pairs={{0,1},{1,0},{2,3},{3,2},{4,5},{5,4},{6,7},{7,6},{8,9},{9,8},{10,11... | collective-permute-start | bytes 49160 | tf_op jit(solution)/shard_map/ppermute | solution.py:461
  8.1 5.5 %collective-permute-start.1 = (f32[32,128]{1,0:T(8,128)S(1)}, f32[32,128]{1,0:T(8,128)S(1)}, u32[]{:S(2)}, u32[]{:S(2)}) collective-permute-start(f32[32,128]{1,0:T(8,128)S(1)} %get-tuple-element.29.after_ref.mine_ref), channel_id=1, source_target_pairs={{0,2},{1,3},{2,0},{3,1},{4,6},{5,7},{6,4},{7,5},{8,10},{9,11},{10,... | collective-permute-start | bytes 49160 | tf_op jit(solution)/shard_map/ppermute | solution.py:461
  14.0 4.3 %collective-permute-start.2 = (f32[64,128]{1,0:T(8,128)S(1)}, f32[64,128]{1,0:T(8,128)S(1)}, u32[]{:S(2)}, u32[]{:S(2)}) collective-permute-start(f32[64,128]{1,0:T(8,128)S(1)} %get-tuple-element.32.after_ref.mine_ref), channel_id=1, source_target_pairs={{0,4},{4,0},{8,12},{12,8},{16,20},{20,16},{24,28},{28,24},{1,5},{5... | collective-permute-start | bytes 98312 | tf_op jit(solution)/shard_map/ppermute | solution.py:461
  18.7 4.4 %collective-permute-start.3 = (f32[72,128]{1,0:T(8,128)S(1)}, f32[72,128]{1,0:T(8,128)S(1)}, u32[]{:S(2)}, u32[]{:S(2)}) collective-permute-start(f32[72,128]{1,0:T(8,128)S(1)} %get-tuple-element.35.after_ref.mine_ref), channel_id=1, source_target_pairs={{0,8},{4,12},{8,0},{12,4},{16,24},{20,28},{24,16},{28,20},{1,9},{5... | collective-permute-start | bytes 110600 | tf_op jit(solution)/shard_map/ppermute | solution.py:461
  20.4 5.8 %copy-start.3 = (f32[32,64,256]{2,1,0:T(8,128)S(1)}, f32[32,64,256]{2,1,0:T(8,128)}, u32[]{:S(2)}) copy-start(f32[32,64,256]{2,1,0:T(8,128)} %basis_ref.1) | copy-start | bytes 6291460
  20.4 5.8 %copy-start.4 = (f32[32,64,64]{2,1,0:T(8,128)S(1)}, f32[32,64,64]{2,1,0:T(8,128)}, u32[]{:S(2)}) copy-start(f32[32,64,64]{2,1,0:T(8,128)} %trans_ref.1) | copy-start | bytes 1572868
  20.4 5.8 %copy-start.5 = (f32[32,64,64]{2,1,0:T(8,128)S(1)}, f32[32,64,64]{2,1,0:T(8,128)}, u32[]{:S(2)}) copy-start(f32[32,64,64]{2,1,0:T(8,128)} %coup_ref.1) | copy-start | bytes 1572868
  23.5 5.6 %collective-permute-start.4 = (f32[112,128]{1,0:T(8,128)S(1)}, f32[112,128]{1,0:T(8,128)S(1)}, u32[]{:S(2)}, u32[]{:S(2)}) collective-permute-start(f32[112,128]{1,0:T(8,128)S(1)} %get-tuple-element.38.after_ref.mine_ref), channel_id=1, source_target_pairs={{0,16},{4,20},{8,24},{12,28},{16,0},{20,4},{24,8},{28,12},{1,17},{... | collective-permute-start | bytes 172040 | tf_op jit(solution)/shard_map/ppermute | solution.py:461
  26.2 3.0 %copy-start.2 = (s32[32]{0:T(128)S(1)}, s32[32]{0:T(128)}, u32[]{:S(2)}) copy-start(s32[32]{0:T(128)} %refs_8_.1) | copy-start | bytes 388

commit v7 on v6

--- a/solution.py
+++ b/solution.py
@@ -84,7 +84,7 @@
             w_ref[t, ib] = jnp.concatenate(rows, axis=0).T
 
 
-def eliminate(w_ref, g_ref, out, alone=False):
+def eliminate(w_ref, g_ref, c_ref, out, alone=False):
     sets, groups, rank = w_ref.shape[0], w_ref.shape[1], w_ref.shape[2]
     place = lax.broadcasted_iota(jnp.int32, (SUB, LANES), 0)
     lane = lax.broadcasted_iota(jnp.int32, (SUB, LANES), 1)
@@ -97,23 +97,33 @@
     def picked(value, p):
         return jnp.take_along_axis(value, picks[p], axis=1, mode="promise_in_bounds")
 
+    def copied(ref, row):
+        return ref[pl.ds(row, SUB, stride=0), :]
+
     def corner(t, kb):
         diagonal = tile(t, kb, kb)
-        rows = [picked(diagonal, p) for p in range(SUB)]
-        pivot = spread(rows[0], 0)
-        inverses, roots = [], []
+        for p in range(SUB):
+            c_ref[t, p] = picked(diagonal, p)
+        a = {(p, q): copied(c_ref.at[t, p], q) for p in range(SUB) for q in range(p + 1)}
+        low, inverses, roots = {}, [], []
         for q in range(SUB):
-            unit = jnp.where(place == q, 1.0, rows[q])
-            sides = {p: spread(rows[q], p) for p in range(q + 1, SUB)}
-            inverse = pl.reciprocal(pivot, approx=True)
+            squares = {p: a[p, q] * a[q + 1, q] for p in range(q + 1, SUB)}
+            inverse = pl.reciprocal(a[q, q], approx=True)
             inverses.append(inverse)
-            roots.append(lax.rsqrt(pivot))
-            if q + 1 < SUB:
-                pivot = spread(rows[q + 1], q + 1) - sides[q + 1] * sides[q + 1] * inverse
+            roots.append(lax.rsqrt(a[q, q]))
             for p in range(q + 1, SUB):
-                kept = jnp.where(place == q, 0.0, rows[p])
-                rows[p] = kept - (sides[p] * unit) * inverse
-        return rows, inverses, roots
+                a[p, q + 1] = a[p, q + 1] - squares[p] * inverse
+            for p in range(q + 1, SUB):
+                low[p, q] = a[p, q] * inverse
+            for p in range(q + 2, SUB):
+                for r in range(q + 2, p + 1):
+                    a[p, r] = a[p, r] - low[p, q] * a[r, q]
+        mult = {}
+        for p in range(1, SUB):
+            for q in range(p):
+                terms = [low[p, q]] + [low[p, r] * mult[r, q] for r in range(q + 1, p)]
+                mult[p, q] = -added(terms)
+        return a, mult, inverses, roots
 
     def merged(parts):
         value = parts[0]
@@ -121,33 +131,34 @@
             value = jnp.where(group == p, parts[p], value)
         return value
 
-    def copied(ref, row):
-        return ref[pl.ds(row, SUB, stride=0), :]
-
-    def panel(t, kb, rows):
-        for p in range(SUB):
-            g_ref[t, p, pl.ds(kb * SUB, SUB), :] = rows[p]
+    def panel(t, kb):
         for jv in [kb + 1 + n for n in range(groups - 1 - kb)] + list(range(kb)):
             value = tile(t, kb, jv)
             for p in range(SUB):
                 g_ref[t, p, pl.ds(jv * SUB, SUB), :] = picked(value, p)
-        return {
-            (p, q): copied(g_ref.at[t, p], kb * SUB + q) for p in range(SUB) for q in range(p)
-        }
-
-    def store(t, kb, mult, rows, roots):
+
+    def store(t, kb, a, mult, inverses, roots):
+        del inverses
         root = merged(roots)
         zero = jnp.zeros((SUB, LANES), F32)
         lanes = [
             merged([mult[p, q] if p > q else zero for p in range(SUB)]) for q in range(SUB - 1)
         ]
+        pivots = merged([a[p, p] for p in range(SUB)])
         upper, lower = [], []
         for jv in range(groups):
             if jv == kb:
-                final = merged(rows) * root
-                upper.append(jnp.where(place >= group, final, 0.0))
-                unit = jnp.where(place == group, root, 0.0)
-                lower.append(jnp.where(place < group, final, unit))
+                value = zero
+                for r in range(SUB):
+                    row = lanes[r] if r < SUB - 1 else zero
+                    for p in range(r):
+                        row = jnp.where(group == p, a[r, p], row)
+                    value = jnp.where(place == r, row, value)
+                final = value * root
+                middle = jnp.where(place == group, pivots * root, 0.0)
+                upper.append(jnp.where(place > group, final, middle))
+                middle = jnp.where(place == group, root, 0.0)
+                lower.append(jnp.where(place < group, final, middle))
                 continue
             terms = [lanes[q] * g_ref[t, q, pl.ds(jv * SUB, SUB), :] for q in range(SUB - 1)]
             final = added([tile(t, kb, jv)] + terms) * root
@@ -185,20 +196,21 @@
 
     corners = [corner(t, 0) for t in range(sets)]
     for kb in range(groups):
-        mults = [panel(t, kb, corners[t][0]) for t in range(sets)]
+        for t in range(sets):
+            panel(t, kb)
         ahead = []
         if kb + 1 < groups:
             for t in range(sets):
-                found = weights(t, kb, kb + 1, mults[t], corners[t][1])
+                found = weights(t, kb, kb + 1, *corners[t][1:3])
                 for jv in [kb + 1] + [jv for jv in range(groups) if jv != kb + 1]:
                     trail(t, kb, kb + 1, jv, found)
             ahead = [corner(t, kb + 1) for t in range(sets)]
         for t in range(sets):
             for ib in range(kb + 2, groups):
-                found = weights(t, kb, ib, mults[t], corners[t][1])
+                found = weights(t, kb, ib, *corners[t][1:3])
                 for jv in range(groups):
                     trail(t, kb, ib, jv, found)
-            store(t, kb, mults[t], corners[t][0], corners[t][2])
+            store(t, kb, *corners[t])
         corners = ahead
 
 
@@ -236,12 +248,10 @@
             if stage * GROUP % chunk == 0:
                 for copy in copies[stage * GROUP // chunk]:
                     copy.wait()
-            threes = []
+            twos = []
             for n in range(stage * GROUP, (stage + 1) * GROUP):
-                high, rest = halves(basis_ref[n])
-                middle, low = halves(rest)
-                threes.append(jnp.concatenate([high, middle, low], axis=0).astype(B16))
-            products[stage] = [mm_nt(three, three) for three in threes]
+                twos.append(jnp.concatenate(halves(basis_ref[n]), axis=0).astype(B16))
+            products[stage] = [mm_nt(two, two) for two in twos]
         group = stage - 1
         if 0 <= group < groups:
             edges[group] = [
@@ -249,8 +259,7 @@
             ]
             parts[group] = []
             for n, product in enumerate(products.pop(group)):
-                rows = product[:rank] + product[rank : 2 * rank] + product[2 * rank :]
-                gram = fold(rows[:, : 2 * rank]) + rows[:, 2 * rank :]
+                gram = fold(product[:rank] + product[rank:])
                 at = group * GROUP + n
                 grams_refs[at // SET][at % SET] = gram
                 both = jnp.concatenate(halves(gram), axis=0).astype(B16)
@@ -269,19 +278,19 @@
     lift_ref[...] = pack(lift(gram, dev_ref[0]))
 
 
-def factor_kernel(grams_ref, after_ref, out_ref, token_ref, w_ref, g_ref):
+def factor_kernel(grams_ref, after_ref, out_ref, token_ref, w_ref, g_ref, c_ref):
     del after_ref
     count, rank = grams_ref.shape[0], grams_ref.shape[1]
     load_sets(grams_ref.reshape(count * rank, rank), w_ref)
-    eliminate(w_ref, g_ref, out_ref.reshape(count * rank, 2 * rank))
+    eliminate(w_ref, g_ref, c_ref, out_ref.reshape(count * rank, 2 * rank))
     token_ref[...] = jnp.zeros(token_ref.shape, F32)
 
 
-def own_kernel(own_ref, after_ref, out_ref, token_ref, full_ref, w_ref, g_ref):
+def own_kernel(own_ref, after_ref, out_ref, token_ref, full_ref, w_ref, g_ref, c_ref):
     del after_ref
     full_ref[...] = unpack(own_ref[...])
     load_sets(full_ref, w_ref, alone=True)
-    eliminate(w_ref, g_ref, out_ref, alone=True)
+    eliminate(w_ref, g_ref, c_ref, out_ref, alone=True)
     token_ref[...] = jnp.zeros(token_ref.shape, F32)
 
 
@@ -407,6 +416,7 @@
         coupled_sem,
         w_ref,
         g_ref,
+        c_ref,
     ) = refs[levels - 1 :]
     rank = grams_ref.shape[1]
     branch, row = lax.axis_index("leaf"), lax.axis_index("rows")
@@ -423,7 +433,7 @@
             grams_ref[at], grams_ref[at + 1] = part(joint)
     count = grams_ref.shape[0]
     load_sets(grams_ref.reshape(count * rank, rank), w_ref)
-    eliminate(w_ref, g_ref, factor_ref.reshape(count * rank, 2 * rank))
+    eliminate(w_ref, g_ref, c_ref, factor_ref.reshape(count * rank, 2 * rank))
     for n in range(n_leaf):
         cols_ref[n] = broad(factor_ref[levels + n, :, :rank])
     copies = []
@@ -492,6 +502,7 @@
         return [
             pltpu.VMEM((sets, groups, rank, LANES), F32),
             pltpu.VMEM((sets, SUB, rank, LANES), F32),
+            pltpu.VMEM((sets, SUB, SUB, LANES), F32),
         ]
 
     sets = leaves // SET

time: 34.4 us -> 34.6 us (level)
  transfers between devices with their start and end apart: 5 -> 5, of which waited for: 1 -> 1; matrix products, arithmetic and copies ran while one was open for 0% -> 0% of each run, Pallas kernels for 32% -> 33%
where the time goes in v7:
time: 34.6 us; the launch traced here: 34.5 us
  Pallas kernels  22.6 us (65%)
  starting transfers between devices  9.29 us (27%)
  between operations  0.93 us (3%)
  local copies, waits for them, and re-layouts  0.85 us (2%)
  waiting for transfers between devices  0.85 us (2%)
    ppermute x5, starting transfers between devices, swap(): return lax.ppermute(value, axis, pairs)  9.29 us
    pallas_call x2, Pallas kernels, per_device(): pl.pallas_call(factor_kernel, in_specs=[vmem, any_place], out_specs=[vmem...  5.59 us
    pallas_call x1, Pallas kernels, per_device(): pl.pallas_call(functools.partial(top_kernel, n_rows, n_leaf, steps), in_s...  5.19 us
    pallas_call x1, Pallas kernels, per_device(): pl.pallas_call(functools.partial(gram_kernel, steps, sets), in_specs=[hbm...  4.51 us
    pallas_call x1, Pallas kernels, per_device(): pl.pallas_call(functools.partial(leaf_kernel, steps, sets), in_specs=[vme...  2.95 us
    pallas_call x1, Pallas kernels, per_device(): pl.pallas_call(own_kernel, in_specs=[vmem, any_place], out_specs=[vmem, v...  2.69 us
    unnamed x12, local copies, waits for them, and re-layouts  0.85 us
    ppermute x5, waiting for transfers between devices, swap(): return lax.ppermute(value, axis, pairs)  0.85 us
  transfers between devices with their start and end apart: 5, of which 1 were waited for; matrix products, arithmetic and copies ran while one was open for 0% of the time, Pallas kernels for 33%

profile of v7, /device:TPU:0, one launch (start us, length us, event | category | flops | bytes accessed | tf_op | source)
XLA Modules:
  0.0 34.5 jit_solution(4730384740388597363)
XLA Ops:
  0.6 0.0 copy-start
  0.6 0.0 copy-start.1
  0.7 0.8 %copy-done.1 = f32[1,64,64]{2,1,0:T(8,128)S(1)} copy-done((f32[1,64,64]{2,1,0:T(8,128)S(1)}, f32[1,64,64]{2,1,0:T(8,128)}, u32[]{:S(2)}) %copy-start.1) | copy-done | bytes 16408
  1.5 4.5 %gram.1 = (f32[16,64,64]{2,1,0:T(8,128)S(1)}, f32[16,64,64]{2,1,0:T(8,128)S(1)}, f32[32,128]{1,0:T(8,128)S(1)}, f32[32,128]{1,0:T(8,128)S(1)}) custom-call(f32[32,64,256]{2,1,0:T(8,128)} %basis_ref.1, f32[32,64,64]{2,1,0:T(8,128)} %trans_ref.1, f32[1,64,64]{2,1,0:T(8,128)S(1)} %copy-done.1), custom_call_target="tpu_custom_call" | custom-call | flops 1000000000 | bytes 4000000 | tf_op jit(solution)/shard_map/gram/pallas_call | solution.py:511
  6.0 0.5 %collective-permute-start = (f32[32,128]{1,0:T(8,128)S(1)}, f32[32,128]{1,0:T(8,128)S(1)}, u32[]{:S(2)}, u32[]{:S(2)}) collective-permute-start(f32[32,128]{1,0:T(8,128)S(1)} %get-tuple-element.28.mine_ref), channel_id=1, source_target_pairs={{0,1},{1,0},{2,3},{3,2},{4,5},{5,4},{6,7},{7,6},{8,9},{9,8},{10,11... | collective-permute-start | bytes 49160 | tf_op jit(solution)/shard_map/ppermute | solution.py:471
  6.5 0.8 %collective-permute-done.got_ref = f32[32,128]{1,0:T(8,128)S(1)} collective-permute-done((f32[32,128]{1,0:T(8,128)S(1)}, f32[32,128]{1,0:T(8,128)S(1)}, u32[]{:S(2)}, u32[]{:S(2)}) %collective-permute-start) | collective-permute-done | bytes 16416 | tf_op jit(solution)/shard_map/ppermute | solution.py:471
  7.4 0.0 copy-done
  7.4 0.4 %row_hop.2 = (f32[32,128]{1,0:T(8,128)S(1)}, f32[32,128]{1,0:T(8,128)S(1)}) custom-call(f32[32,128]{1,0:T(8,128)S(1)} %get-tuple-element.28.mine_ref, f32[32,128]{1,0:T(8,128)S(1)} %collective-permute-done.got_ref, f32[32,128]{1,0:T(8,128)S(1)} %get-tuple-element.27.own_ref.after_ref, f32[30,64,64]{2,1,0:T(8,128)S(1)} %copy-done, ...), custom_call_target="tpu_custom_call" | custom-call | tf_op jit(solution)/shard_map/row_hop/pallas_call | solution.py:542
  7.8 2.9 %collective-permute-start.1 = (f32[32,128]{1,0:T(8,128)S(1)}, f32[32,128]{1,0:T(8,128)S(1)}, u32[]{:S(2)}, u32[]{:S(2)}) collective-permute-start(f32[32,128]{1,0:T(8,128)S(1)} %get-tuple-element.29.after_ref.mine_ref), channel_id=1, source_target_pairs={{0,2},{1,3},{2,0},{3,1},{4,6},{5,7},{6,4},{7,5},{8,10},{9,11},{10,... | collective-permute-start | bytes 49160 | tf_op jit(solution)/shard_map/ppermute | solution.py:471
  10.7 2.7 %own.1 = (f32[64,128]{1,0:T(8,128)S(1)}, f32[8,128]{1,0:T(8,128)S(1)}) custom-call(f32[32,128]{1,0:T(8,128)S(1)} %get-tuple-element.27.own_ref.after_ref, f32[32,128]{1,0:T(8,128)S(1)} %get-tuple-element.29.after_ref.mine_ref), custom_call_target="tpu_custom_call" | custom-call | flops 5000000000 | bytes 8000000 | tf_op jit(solution)/shard_map/own/pallas_call | solution.py:532
  13.4 0.0 collective-permute-done.1.got_ref
  13.4 0.4 %row_hop.3 = (f32[32,128]{1,0:T(8,128)S(1)}, f32[64,128]{1,0:T(8,128)S(1)}) custom-call(f32[32,128]{1,0:T(8,128)S(1)} %get-tuple-element.29.after_ref.mine_ref, f32[32,128]{1,0:T(8,128)S(1)} %collective-permute-done.1.got_ref, f32[32,128]{1,0:T(8,128)S(1)} %get-tuple-element.27.own_ref.after_ref, f32[30,64,64]{2,1,0:T(8,128)S(1)} %copy-done, ...), custom_call_target="tpu_custom_call" | custom-call | tf_op jit(solution)/shard_map/row_hop/pallas_call | solution.py:542
  13.8 1.6 %collective-permute-start.2 = (f32[64,128]{1,0:T(8,128)S(1)}, f32[64,128]{1,0:T(8,128)S(1)}, u32[]{:S(2)}, u32[]{:S(2)}) collective-permute-start(f32[64,128]{1,0:T(8,128)S(1)} %get-tuple-element.32.after_ref.mine_ref), channel_id=1, source_target_pairs={{0,4},{4,0},{8,12},{12,8},{16,20},{20,16},{24,28},{28,24},{1,5},{5... | collective-permute-start | bytes 98312 | tf_op jit(solution)/shard_map/ppermute | solution.py:471
  15.4 2.8 %factor.2 = (f32[16,64,128]{2,1,0:T(8,128)S(1)}, f32[8,128]{1,0:T(8,128)S(1)}) custom-call(f32[16,64,64]{2,1,0:T(8,128)S(1)} %get-tuple-element.33.grams_ref, f32[64,128]{1,0:T(8,128)S(1)} %get-tuple-element.32.after_ref.mine_ref), custom_call_target="tpu_custom_call" | custom-call | flops 5000000000 | bytes 8000000 | tf_op jit(solution)/shard_map/factor/pallas_call | solution.py:555
  18.2 0.0 collective-permute-done.2.got_ref
  18.2 0.4 %leaf_hop.2 = (f32[32,128]{1,0:T(8,128)S(1)}, f32[72,128]{1,0:T(8,128)S(1)}) custom-call(f32[64,128]{1,0:T(8,128)S(1)} %get-tuple-element.32.after_ref.mine_ref, f32[64,128]{1,0:T(8,128)S(1)} %collective-permute-done.2.got_ref, f32[30,64,64]{2,1,0:T(8,128)S(1)} %copy-done, f32[8,128]{1,0:T(8,128)S(1)} %get-tuple-element.34.after_ref), custom_call_target="tpu_custom_call" | custom-call | tf_op jit(solution)/shard_map/leaf_hop/pallas_call | solution.py:566
  18.6 1.6 %collective-permute-start.3 = (f32[72,128]{1,0:T(8,128)S(1)}, f32[72,128]{1,0:T(8,128)S(1)}, u32[]{:S(2)}, u32[]{:S(2)}) collective-permute-start(f32[72,128]{1,0:T(8,128)S(1)} %get-tuple-element.35.after_ref.mine_ref), channel_id=1, source_target_pairs={{0,8},{4,12},{8,0},{12,4},{16,24},{20,28},{24,16},{28,20},{1,9},{5... | collective-permute-start | bytes 110600 | tf_op jit(solution)/shard_map/ppermute | solution.py:471
  20.3 2.8 %factor.3 = (f32[16,64,128]{2,1,0:T(8,128)S(1)}, f32[8,128]{1,0:T(8,128)S(1)}) custom-call(f32[16,64,64]{2,1,0:T(8,128)S(1)} %get-tuple-element.36.grams_ref, f32[72,128]{1,0:T(8,128)S(1)} %get-tuple-element.35.after_ref.mine_ref), custom_call_target="tpu_custom_call" | custom-call | flops 5000000000 | bytes 8000000 | tf_op jit(solution)/shard_map/factor/pallas_call | solution.py:555
  23.1 0.0 collective-permute-done.3.got_ref
  23.1 0.4 %leaf_hop.3 = (f32[32,128]{1,0:T(8,128)S(1)}, f32[112,128]{1,0:T(8,128)S(1)}) custom-call(f32[72,128]{1,0:T(8,128)S(1)} %get-tuple-element.35.after_ref.mine_ref, f32[72,128]{1,0:T(8,128)S(1)} %collective-permute-done.3.got_ref, f32[30,64,64]{2,1,0:T(8,128)S(1)} %copy-done, f32[8,128]{1,0:T(8,128)S(1)} %get-tuple-element.37.after_ref), custom_call_target="tpu_custom_call" | custom-call | tf_op jit(solution)/shard_map/leaf_hop/pallas_call | solution.py:566
  23.5 2.6 %collective-permute-start.4 = (f32[112,128]{1,0:T(8,128)S(1)}, f32[112,128]{1,0:T(8,128)S(1)}, u32[]{:S(2)}, u32[]{:S(2)}) collective-permute-start(f32[112,128]{1,0:T(8,128)S(1)} %get-tuple-element.38.after_ref.mine_ref), channel_id=1, source_target_pairs={{0,16},{4,20},{8,24},{12,28},{16,0},{20,4},{24,8},{28,12},{1,17},{... | collective-permute-start | bytes 172040 | tf_op jit(solution)/shard_map/ppermute | solution.py:471
  26.2 2.9 %leaf.1 = (f32[32,64,256]{2,1,0:T(8,128)}, f32[32,64,64]{2,1,0:T(8,128)}, bf16[32,64,128]{2,1,0:T(8,128)(2,1)S(1)}) custom-call(f32[32,64,256]{2,1,0:T(8,128)S(1)} %copy-done.3, f32[32,64,64]{2,1,0:T(8,128)S(1)} %copy-done.4, f32[32,64,64]{2,1,0:T(8,128)S(1)} %copy-done.5, f32[64,128]{1,0:T(8,128)S(1)} %get-tuple-element.30.own_ref.refs_6_, ...), custom_call_target="tpu_custom_call" | custom-call | flops 5000000000 | bytes 8000000 | tf_op jit(solution)/shard_map/leaf/pallas_call | solution.py:576
  29.1 0.0 collective-permute-done.4.got_ref
  29.1 5.2 %top.1 = (f32[1,5,64,64]{3,2,1,0:T(8,128)}, f32[32,64,64]{2,1,0:T(8,128)}) custom-call(f32[112,128]{1,0:T(8,128)S(1)} %get-tuple-element.38.after_ref.mine_ref, f32[112,128]{1,0:T(8,128)S(1)} %collective-permute-done.4.got_ref, f32[32,128]{1,0:T(8,128)S(1)} %get-tuple-element.43.refs_0_, f32[32,128]{1,0:T(8,128)S(1)} %get-tuple-element.44.refs_1_, ...), custom_call_target="tpu_custom_call" | custom-call | tf_op jit(solution)/shard_map/top/pallas_call | solution.py:596
  (8 shorter events, 0.0 us)
Async XLA Ops:
  0.6 6.7 %copy-start = (f32[30,64,64]{2,1,0:T(8,128)S(1)}, f32[30,64,64]{2,1,0:T(8,128)}, u32[]{:S(2)}) copy-start(f32[30,64,64]{2,1,0:T(8,128)} %refs_4_.1) | copy-start | bytes 1474564
  0.6 0.8 %copy-start.1 = (f32[1,64,64]{2,1,0:T(8,128)S(1)}, f32[1,64,64]{2,1,0:T(8,128)}, u32[]{:S(2)}) copy-start(f32[1,64,64]{2,1,0:T(8,128)} %refs_5_.1) | copy-start | bytes 49156
  6.0 1.4 %collective-permute-start = (f32[32,128]{1,0:T(8,128)S(1)}, f32[32,128]{1,0:T(8,128)S(1)}, u32[]{:S(2)}, u32[]{:S(2)}) collective-permute-start(f32[32,128]{1,0:T(8,128)S(1)} %get-tuple-element.28.mine_ref), channel_id=1, source_target_pairs={{0,1},{1,0},{2,3},{3,2},{4,5},{5,4},{6,7},{7,6},{8,9},{9,8},{10,11... | collective-permute-start | bytes 49160 | tf_op jit(solution)/shard_map/ppermute | solution.py:471
  7.8 5.6 %collective-permute-start.1 = (f32[32,128]{1,0:T(8,128)S(1)}, f32[32,128]{1,0:T(8,128)S(1)}, u32[]{:S(2)}, u32[]{:S(2)}) collective-permute-start(f32[32,128]{1,0:T(8,128)S(1)} %get-tuple-element.29.after_ref.mine_ref), channel_id=1, source_target_pairs={{0,2},{1,3},{2,0},{3,1},{4,6},{5,7},{6,4},{7,5},{8,10},{9,11},{10,... | collective-permute-start | bytes 49160 | tf_op jit(solution)/shard_map/ppermute | solution.py:471
  13.8 4.4 %collective-permute-start.2 = (f32[64,128]{1,0:T(8,128)S(1)}, f32[64,128]{1,0:T(8,128)S(1)}, u32[]{:S(2)}, u32[]{:S(2)}) collective-permute-start(f32[64,128]{1,0:T(8,128)S(1)} %get-tuple-element.32.after_ref.mine_ref), channel_id=1, source_target_pairs={{0,4},{4,0},{8,12},{12,8},{16,20},{20,16},{24,28},{28,24},{1,5},{5... | collective-permute-start | bytes 98312 | tf_op jit(solution)/shard_map/ppermute | solution.py:471
  18.6 4.5 %collective-permute-start.3 = (f32[72,128]{1,0:T(8,128)S(1)}, f32[72,128]{1,0:T(8,128)S(1)}, u32[]{:S(2)}, u32[]{:S(2)}) collective-permute-start(f32[72,128]{1,0:T(8,128)S(1)} %get-tuple-element.35.after_ref.mine_ref), channel_id=1, source_target_pairs={{0,8},{4,12},{8,0},{12,4},{16,24},{20,28},{24,16},{28,20},{1,9},{5... | collective-permute-start | bytes 110600 | tf_op jit(solution)/shard_map/ppermute | solution.py:471
  20.3 5.9 %copy-start.3 = (f32[32,64,256]{2,1,0:T(8,128)S(1)}, f32[32,64,256]{2,1,0:T(8,128)}, u32[]{:S(2)}) copy-start(f32[32,64,256]{2,1,0:T(8,128)} %basis_ref.1) | copy-start | bytes 6291460
  20.3 5.9 %copy-start.4 = (f32[32,64,64]{2,1,0:T(8,128)S(1)}, f32[32,64,64]{2,1,0:T(8,128)}, u32[]{:S(2)}) copy-start(f32[32,64,64]{2,1,0:T(8,128)} %trans_ref.1) | copy-start | bytes 1572868
  20.3 5.9 %copy-start.5 = (f32[32,64,64]{2,1,0:T(8,128)S(1)}, f32[32,64,64]{2,1,0:T(8,128)}, u32[]{:S(2)}) copy-start(f32[32,64,64]{2,1,0:T(8,128)} %coup_ref.1) | copy-start | bytes 1572868
  23.5 5.6 %collective-permute-start.4 = (f32[112,128]{1,0:T(8,128)S(1)}, f32[112,128]{1,0:T(8,128)S(1)}, u32[]{:S(2)}, u32[]{:S(2)}) collective-permute-start(f32[112,128]{1,0:T(8,128)S(1)} %get-tuple-element.38.after_ref.mine_ref), channel_id=1, source_target_pairs={{0,16},{4,20},{8,24},{12,28},{16,0},{20,4},{24,8},{28,12},{1,17},{... | collective-permute-start | bytes 172040 | tf_op jit(solution)/shard_map/ppermute | solution.py:471
  26.2 3.0 %copy-start.2 = (s32[32]{0:T(128)S(1)}, s32[32]{0:T(128)}, u32[]{:S(2)}) copy-start(s32[32]{0:T(128)} %refs_8_.1) | copy-start | bytes 388

commit v8 on v7

--- a/solution.py
+++ b/solution.py
@@ -89,21 +89,29 @@
     place = lax.broadcasted_iota(jnp.int32, (SUB, LANES), 0)
     lane = lax.broadcasted_iota(jnp.int32, (SUB, LANES), 1)
     group = lane // SET
-    picks = [p * SET + lane % SET for p in range(SUB)]
 
     def tile(t, ib, jv):
         return w_ref[t, ib, pl.ds(jv * SUB, SUB), :]
 
-    def picked(value, p):
-        return jnp.take_along_axis(value, picks[p], axis=1, mode="promise_in_bounds")
+    def replicated(value):
+        found = [value]
+        for width in (LANES // 2, LANES // 4, LANES // 8):
+            first = lane % (2 * width) < width
+            split = []
+            for part in found:
+                rolled = pltpu.roll(part, width, 1)
+                split.append(jnp.where(first, part, rolled))
+                split.append(jnp.where(first, rolled, part))
+            found = split
+        return found
 
     def copied(ref, row):
         return ref[pl.ds(row, SUB, stride=0), :]
 
     def corner(t, kb):
         diagonal = tile(t, kb, kb)
-        for p in range(SUB):
-            c_ref[t, p] = picked(diagonal, p)
+        for p, row in enumerate(replicated(diagonal)):
+            c_ref[t, p] = row
         a = {(p, q): copied(c_ref.at[t, p], q) for p in range(SUB) for q in range(p + 1)}
         low, inverses, roots = {}, [], []
         for q in range(SUB):
@@ -133,9 +141,8 @@
 
     def panel(t, kb):
         for jv in [kb + 1 + n for n in range(groups - 1 - kb)] + list(range(kb)):
-            value = tile(t, kb, jv)
-            for p in range(SUB):
-                g_ref[t, p, pl.ds(jv * SUB, SUB), :] = picked(value, p)
+            for p, row in enumerate(replicated(tile(t, kb, jv))):
+                g_ref[t, p, pl.ds(jv * SUB, SUB), :] = row
 
     def store(t, kb, a, mult, inverses, roots):
         del inverses
@@ -184,15 +191,21 @@
             for r in range(SUB)
         ]
 
-    def trail(t, kb, ib, jv, found):
+    def trail(t, kb, jv, founds):
         if jv == kb:
-            value = -found[0]
-            for r in range(1, SUB):
-                value = jnp.where(place == r, -found[r], value)
+            values = {}
+            for ib, found in founds.items():
+                values[ib] = -found[0]
+                for r in range(1, SUB):
+                    values[ib] = jnp.where(place == r, -found[r], values[ib])
         else:
-            terms = [found[r] * g_ref[t, r, pl.ds(jv * SUB, SUB), :] for r in range(SUB)]
-            value = tile(t, ib, jv) - added(terms)
-        w_ref[t, ib, pl.ds(jv * SUB, SUB), :] = value
+            source = [g_ref[t, r, pl.ds(jv * SUB, SUB), :] for r in range(SUB)]
+            values = {
+                ib: tile(t, ib, jv) - added([found[r] * source[r] for r in range(SUB)])
+                for ib, found in founds.items()
+            }
+        for ib, value in values.items():
+            w_ref[t, ib, pl.ds(jv * SUB, SUB), :] = value
 
     corners = [corner(t, 0) for t in range(sets)]
     for kb in range(groups):
@@ -201,15 +214,17 @@
         ahead = []
         if kb + 1 < groups:
             for t in range(sets):
-                found = weights(t, kb, kb + 1, *corners[t][1:3])
+                founds = {kb + 1: weights(t, kb, kb + 1, *corners[t][1:3])}
                 for jv in [kb + 1] + [jv for jv in range(groups) if jv != kb + 1]:
-                    trail(t, kb, kb + 1, jv, found)
+                    trail(t, kb, jv, founds)
             ahead = [corner(t, kb + 1) for t in range(sets)]
         for t in range(sets):
-            for ib in range(kb + 2, groups):
-                found = weights(t, kb, ib, *corners[t][1:3])
+            for ib in range(kb + 2, groups, 2):
+                founds = {
+                    n: weights(t, kb, n, *corners[t][1:3]) for n in range(ib, min(ib + 2, groups))
+                }
                 for jv in range(groups):
-                    trail(t, kb, ib, jv, found)
+                    trail(t, kb, jv, founds)
             store(t, kb, *corners[t])
         corners = ahead
 

time: 34.6 us -> 39.5 us (1.14)
  Pallas kernels: 22.6 us -> 27.4 us
    pallas_call x2, Pallas kernels: 5.59 us -> 8.09 us  [per_device(): pl.pallas_call(factor_kernel, in_specs=[vmem, any_place], out_specs=[vmem...]
    pallas_call x1, Pallas kernels: 2.69 us -> 3.9 us  [per_device(): pl.pallas_call(own_kernel, in_specs=[vmem, any_place], out_specs=[vmem, v...]
    pallas_call x1, Pallas kernels: 5.19 us -> 6.29 us  [per_device(): pl.pallas_call(functools.partial(top_kernel, n_rows, n_leaf, steps), in_s...]
  transfers between devices with their start and end apart: 5 -> 5, of which waited for: 1 -> 1; matrix products, arithmetic and copies ran while one was open for 0% -> 0% of each run, Pallas kernels for 33% -> 38%
where the time goes in v8:
time: 39.5 us; the launch traced here: 39.3 us
  Pallas kernels  27.4 us (69%)
  starting transfers between devices  9.29 us (24%)
  between operations  0.91 us (2%)
  waiting for transfers between devices  0.87 us (2%)
  local copies, waits for them, and re-layouts  0.85 us (2%)
    ppermute x5, starting transfers between devices, swap(): return lax.ppermute(value, axis, pairs)  9.29 us
    pallas_call x2, Pallas kernels, per_device(): pl.pallas_call(factor_kernel, in_specs=[vmem, any_place], out_specs=[vmem...  8.09 us
    pallas_call x1, Pallas kernels, per_device(): pl.pallas_call(functools.partial(top_kernel, n_rows, n_leaf, steps), in_s...  6.29 us
    pallas_call x1, Pallas kernels, per_device(): pl.pallas_call(functools.partial(gram_kernel, steps, sets), in_specs=[hbm...  4.51 us
    pallas_call x1, Pallas kernels, per_device(): pl.pallas_call(own_kernel, in_specs=[vmem, any_place], out_specs=[vmem, v...  3.9 us
    pallas_call x1, Pallas kernels, per_device(): pl.pallas_call(functools.partial(leaf_kernel, steps, sets), in_specs=[vme...  2.96 us
    ppermute x5, waiting for transfers between devices, swap(): return lax.ppermute(value, axis, pairs)  0.87 us
    unnamed x12, local copies, waits for them, and re-layouts  0.85 us
  transfers between devices with their start and end apart: 5, of which 1 were waited for; matrix products, arithmetic and copies ran while one was open for 0% of the time, Pallas kernels for 38%

profile of v8, /device:TPU:0, one launch (start us, length us, event | category | flops | bytes accessed | tf_op | source)
XLA Modules:
  0.0 39.3 jit_solution(11691180316396904937)
XLA Ops:
  0.7 0.8 %copy-done.1 = f32[1,64,64]{2,1,0:T(8,128)S(1)} copy-done((f32[1,64,64]{2,1,0:T(8,128)S(1)}, f32[1,64,64]{2,1,0:T(8,128)}, u32[]{:S(2)}) %copy-start.1) | copy-done | bytes 16408
  1.5 4.5 %gram.1 = (f32[16,64,64]{2,1,0:T(8,128)S(1)}, f32[16,64,64]{2,1,0:T(8,128)S(1)}, f32[32,128]{1,0:T(8,128)S(1)}, f32[32,128]{1,0:T(8,128)S(1)}) custom-call(f32[32,64,256]{2,1,0:T(8,128)} %basis_ref.1, f32[32,64,64]{2,1,0:T(8,128)} %trans_ref.1, f32[1,64,64]{2,1,0:T(8,128)S(1)} %copy-done.1), custom_call_target="tpu_custom_call" | custom-call | flops 1000000000 | bytes 4000000 | tf_op jit(solution)/shard_map/gram/pallas_call | solution.py:526
  6.0 0.5 %collective-permute-start = (f32[32,128]{1,0:T(8,128)S(1)}, f32[32,128]{1,0:T(8,128)S(1)}, u32[]{:S(2)}, u32[]{:S(2)}) collective-permute-start(f32[32,128]{1,0:T(8,128)S(1)} %get-tuple-element.28.mine_ref), channel_id=1, source_target_pairs={{0,1},{1,0},{2,3},{3,2},{4,5},{5,4},{6,7},{7,6},{8,9},{9,8},{10,11... | collective-permute-start | bytes 49160 | tf_op jit(solution)/shard_map/ppermute | solution.py:486
  6.5 0.8 %collective-permute-done.got_ref = f32[32,128]{1,0:T(8,128)S(1)} collective-permute-done((f32[32,128]{1,0:T(8,128)S(1)}, f32[32,128]{1,0:T(8,128)S(1)}, u32[]{:S(2)}, u32[]{:S(2)}) %collective-permute-start) | collective-permute-done | bytes 16416 | tf_op jit(solution)/shard_map/ppermute | solution.py:486
  7.4 0.0 copy-done
  7.4 0.4 %row_hop.2 = (f32[32,128]{1,0:T(8,128)S(1)}, f32[32,128]{1,0:T(8,128)S(1)}) custom-call(f32[32,128]{1,0:T(8,128)S(1)} %get-tuple-element.28.mine_ref, f32[32,128]{1,0:T(8,128)S(1)} %collective-permute-done.got_ref, f32[32,128]{1,0:T(8,128)S(1)} %get-tuple-element.27.own_ref.after_ref, f32[30,64,64]{2,1,0:T(8,128)S(1)} %copy-done, ...), custom_call_target="tpu_custom_call" | custom-call | tf_op jit(solution)/shard_map/row_hop/pallas_call | solution.py:557
  7.8 2.9 %collective-permute-start.1 = (f32[32,128]{1,0:T(8,128)S(1)}, f32[32,128]{1,0:T(8,128)S(1)}, u32[]{:S(2)}, u32[]{:S(2)}) collective-permute-start(f32[32,128]{1,0:T(8,128)S(1)} %get-tuple-element.29.after_ref.mine_ref), channel_id=1, source_target_pairs={{0,2},{1,3},{2,0},{3,1},{4,6},{5,7},{6,4},{7,5},{8,10},{9,11},{10,... | collective-permute-start | bytes 49160 | tf_op jit(solution)/shard_map/ppermute | solution.py:486
  10.7 3.9 %own.1 = (f32[64,128]{1,0:T(8,128)S(1)}, f32[8,128]{1,0:T(8,128)S(1)}) custom-call(f32[32,128]{1,0:T(8,128)S(1)} %get-tuple-element.27.own_ref.after_ref, f32[32,128]{1,0:T(8,128)S(1)} %get-tuple-element.29.after_ref.mine_ref), custom_call_target="tpu_custom_call" | custom-call | flops 5000000000 | bytes 8000000 | tf_op jit(solution)/shard_map/own/pallas_call | solution.py:547
  14.6 0.0 collective-permute-done.1.got_ref
  14.6 0.4 %row_hop.3 = (f32[32,128]{1,0:T(8,128)S(1)}, f32[64,128]{1,0:T(8,128)S(1)}) custom-call(f32[32,128]{1,0:T(8,128)S(1)} %get-tuple-element.29.after_ref.mine_ref, f32[32,128]{1,0:T(8,128)S(1)} %collective-permute-done.1.got_ref, f32[32,128]{1,0:T(8,128)S(1)} %get-tuple-element.27.own_ref.after_ref, f32[30,64,64]{2,1,0:T(8,128)S(1)} %copy-done, ...), custom_call_target="tpu_custom_call" | custom-call | tf_op jit(solution)/shard_map/row_hop/pallas_call | solution.py:557
  15.0 1.6 %collective-permute-start.2 = (f32[64,128]{1,0:T(8,128)S(1)}, f32[64,128]{1,0:T(8,128)S(1)}, u32[]{:S(2)}, u32[]{:S(2)}) collective-permute-start(f32[64,128]{1,0:T(8,128)S(1)} %get-tuple-element.32.after_ref.mine_ref), channel_id=1, source_target_pairs={{0,4},{4,0},{8,12},{12,8},{16,20},{20,16},{24,28},{28,24},{1,5},{5... | collective-permute-start | bytes 98312 | tf_op jit(solution)/shard_map/ppermute | solution.py:486
  16.6 4.0 %factor.2 = (f32[16,64,128]{2,1,0:T(8,128)S(1)}, f32[8,128]{1,0:T(8,128)S(1)}) custom-call(f32[16,64,64]{2,1,0:T(8,128)S(1)} %get-tuple-element.33.grams_ref, f32[64,128]{1,0:T(8,128)S(1)} %get-tuple-element.32.after_ref.mine_ref), custom_call_target="tpu_custom_call" | custom-call | flops 5000000000 | bytes 8000000 | tf_op jit(solution)/shard_map/factor/pallas_call | solution.py:570
  20.7 0.0 collective-permute-done.2.got_ref
  20.7 0.4 %leaf_hop.2 = (f32[32,128]{1,0:T(8,128)S(1)}, f32[72,128]{1,0:T(8,128)S(1)}) custom-call(f32[64,128]{1,0:T(8,128)S(1)} %get-tuple-element.32.after_ref.mine_ref, f32[64,128]{1,0:T(8,128)S(1)} %collective-permute-done.2.got_ref, f32[30,64,64]{2,1,0:T(8,128)S(1)} %copy-done, f32[8,128]{1,0:T(8,128)S(1)} %get-tuple-element.34.after_ref), custom_call_target="tpu_custom_call" | custom-call | tf_op jit(solution)/shard_map/leaf_hop/pallas_call | solution.py:581
  21.1 1.6 %collective-permute-start.3 = (f32[72,128]{1,0:T(8,128)S(1)}, f32[72,128]{1,0:T(8,128)S(1)}, u32[]{:S(2)}, u32[]{:S(2)}) collective-permute-start(f32[72,128]{1,0:T(8,128)S(1)} %get-tuple-element.35.after_ref.mine_ref), channel_id=1, source_target_pairs={{0,8},{4,12},{8,0},{12,4},{16,24},{20,28},{24,16},{28,20},{1,9},{5... | collective-permute-start | bytes 110600 | tf_op jit(solution)/shard_map/ppermute | solution.py:486
  22.7 4.0 %factor.3 = (f32[16,64,128]{2,1,0:T(8,128)S(1)}, f32[8,128]{1,0:T(8,128)S(1)}) custom-call(f32[16,64,64]{2,1,0:T(8,128)S(1)} %get-tuple-element.36.grams_ref, f32[72,128]{1,0:T(8,128)S(1)} %get-tuple-element.35.after_ref.mine_ref), custom_call_target="tpu_custom_call" | custom-call | flops 5000000000 | bytes 8000000 | tf_op jit(solution)/shard_map/factor/pallas_call | solution.py:570
  26.8 0.0 collective-permute-done.3.got_ref
  26.8 0.4 %leaf_hop.3 = (f32[32,128]{1,0:T(8,128)S(1)}, f32[112,128]{1,0:T(8,128)S(1)}) custom-call(f32[72,128]{1,0:T(8,128)S(1)} %get-tuple-element.35.after_ref.mine_ref, f32[72,128]{1,0:T(8,128)S(1)} %collective-permute-done.3.got_ref, f32[30,64,64]{2,1,0:T(8,128)S(1)} %copy-done, f32[8,128]{1,0:T(8,128)S(1)} %get-tuple-element.37.after_ref), custom_call_target="tpu_custom_call" | custom-call | tf_op jit(solution)/shard_map/leaf_hop/pallas_call | solution.py:581
  27.2 2.6 %collective-permute-start.4 = (f32[112,128]{1,0:T(8,128)S(1)}, f32[112,128]{1,0:T(8,128)S(1)}, u32[]{:S(2)}, u32[]{:S(2)}) collective-permute-start(f32[112,128]{1,0:T(8,128)S(1)} %get-tuple-element.38.after_ref.mine_ref), channel_id=1, source_target_pairs={{0,16},{4,20},{8,24},{12,28},{16,0},{20,4},{24,8},{28,12},{1,17},{... | collective-permute-start | bytes 172040 | tf_op jit(solution)/shard_map/ppermute | solution.py:486
  29.9 0.0 copy-done.3
  29.9 0.0 copy-done.5
  29.9 3.0 %leaf.1 = (f32[32,64,256]{2,1,0:T(8,128)}, f32[32,64,64]{2,1,0:T(8,128)}, bf16[32,64,128]{2,1,0:T(8,128)(2,1)S(1)}) custom-call(f32[32,64,256]{2,1,0:T(8,128)S(1)} %copy-done.3, f32[32,64,64]{2,1,0:T(8,128)S(1)} %copy-done.4, f32[32,64,64]{2,1,0:T(8,128)S(1)} %copy-done.5, f32[64,128]{1,0:T(8,128)S(1)} %get-tuple-element.30.own_ref.refs_6_, ...), custom_call_target="tpu_custom_call" | custom-call | flops 5000000000 | bytes 8000000 | tf_op jit(solution)/shard_map/leaf/pallas_call | solution.py:591
  32.8 0.0 collective-permute-done.4.got_ref
  32.9 6.3 %top.1 = (f32[1,5,64,64]{3,2,1,0:T(8,128)}, f32[32,64,64]{2,1,0:T(8,128)}) custom-call(f32[112,128]{1,0:T(8,128)S(1)} %get-tuple-element.38.after_ref.mine_ref, f32[112,128]{1,0:T(8,128)S(1)} %collective-permute-done.4.got_ref, f32[32,128]{1,0:T(8,128)S(1)} %get-tuple-element.43.refs_0_, f32[32,128]{1,0:T(8,128)S(1)} %get-tuple-element.44.refs_1_, ...), custom_call_target="tpu_custom_call" | custom-call | tf_op jit(solution)/shard_map/top/pallas_call | solution.py:611
  (8 shorter events, 0.0 us)
Async XLA Ops:
  0.6 6.7 %copy-start = (f32[30,64,64]{2,1,0:T(8,128)S(1)}, f32[30,64,64]{2,1,0:T(8,128)}, u32[]{:S(2)}) copy-start(f32[30,64,64]{2,1,0:T(8,128)} %refs_4_.1) | copy-start | bytes 1474564
  0.6 0.8 %copy-start.1 = (f32[1,64,64]{2,1,0:T(8,128)S(1)}, f32[1,64,64]{2,1,0:T(8,128)}, u32[]{:S(2)}) copy-start(f32[1,64,64]{2,1,0:T(8,128)} %refs_5_.1) | copy-start | bytes 49156
  6.0 1.4 %collective-permute-start = (f32[32,128]{1,0:T(8,128)S(1)}, f32[32,128]{1,0:T(8,128)S(1)}, u32[]{:S(2)}, u32[]{:S(2)}) collective-permute-start(f32[32,128]{1,0:T(8,128)S(1)} %get-tuple-element.28.mine_ref), channel_id=1, source_target_pairs={{0,1},{1,0},{2,3},{3,2},{4,5},{5,4},{6,7},{7,6},{8,9},{9,8},{10,11... | collective-permute-start | bytes 49160 | tf_op jit(solution)/shard_map/ppermute | solution.py:486
  7.8 6.8 %collective-permute-start.1 = (f32[32,128]{1,0:T(8,128)S(1)}, f32[32,128]{1,0:T(8,128)S(1)}, u32[]{:S(2)}, u32[]{:S(2)}) collective-permute-start(f32[32,128]{1,0:T(8,128)S(1)} %get-tuple-element.29.after_ref.mine_ref), channel_id=1, source_target_pairs={{0,2},{1,3},{2,0},{3,1},{4,6},{5,7},{6,4},{7,5},{8,10},{9,11},{10,... | collective-permute-start | bytes 49160 | tf_op jit(solution)/shard_map/ppermute | solution.py:486
  15.0 5.6 %collective-permute-start.2 = (f32[64,128]{1,0:T(8,128)S(1)}, f32[64,128]{1,0:T(8,128)S(1)}, u32[]{:S(2)}, u32[]{:S(2)}) collective-permute-start(f32[64,128]{1,0:T(8,128)S(1)} %get-tuple-element.32.after_ref.mine_ref), channel_id=1, source_target_pairs={{0,4},{4,0},{8,12},{12,8},{16,20},{20,16},{24,28},{28,24},{1,5},{5... | collective-permute-start | bytes 98312 | tf_op jit(solution)/shard_map/ppermute | solution.py:486
  21.1 5.7 %collective-permute-start.3 = (f32[72,128]{1,0:T(8,128)S(1)}, f32[72,128]{1,0:T(8,128)S(1)}, u32[]{:S(2)}, u32[]{:S(2)}) collective-permute-start(f32[72,128]{1,0:T(8,128)S(1)} %get-tuple-element.35.after_ref.mine_ref), channel_id=1, source_target_pairs={{0,8},{4,12},{8,0},{12,4},{16,24},{20,28},{24,16},{28,20},{1,9},{5... | collective-permute-start | bytes 110600 | tf_op jit(solution)/shard_map/ppermute | solution.py:486
  22.7 7.1 %copy-start.3 = (f32[32,64,256]{2,1,0:T(8,128)S(1)}, f32[32,64,256]{2,1,0:T(8,128)}, u32[]{:S(2)}) copy-start(f32[32,64,256]{2,1,0:T(8,128)} %basis_ref.1) | copy-start | bytes 6291460
  22.7 7.1 %copy-start.4 = (f32[32,64,64]{2,1,0:T(8,128)S(1)}, f32[32,64,64]{2,1,0:T(8,128)}, u32[]{:S(2)}) copy-start(f32[32,64,64]{2,1,0:T(8,128)} %trans_ref.1) | copy-start | bytes 1572868
  22.7 7.1 %copy-start.5 = (f32[32,64,64]{2,1,0:T(8,128)S(1)}, f32[32,64,64]{2,1,0:T(8,128)}, u32[]{:S(2)}) copy-start(f32[32,64,64]{2,1,0:T(8,128)} %coup_ref.1) | copy-start | bytes 1572868
  27.2 5.6 %collective-permute-start.4 = (f32[112,128]{1,0:T(8,128)S(1)}, f32[112,128]{1,0:T(8,128)S(1)}, u32[]{:S(2)}, u32[]{:S(2)}) collective-permute-start(f32[112,128]{1,0:T(8,128)S(1)} %get-tuple-element.38.after_ref.mine_ref), channel_id=1, source_target_pairs={{0,16},{4,20},{8,24},{12,28},{16,0},{20,4},{24,8},{28,12},{1,17},{... | collective-permute-start | bytes 172040 | tf_op jit(solution)/shard_map/ppermute | solution.py:486
  29.9 3.0 %copy-start.2 = (s32[32]{0:T(128)S(1)}, s32[32]{0:T(128)}, u32[]{:S(2)}) copy-start(s32[32]{0:T(128)} %refs_8_.1) | copy-start | bytes 388

commit v9 on v7

--- a/solution.py
+++ b/solution.py
@@ -106,11 +106,13 @@
             c_ref[t, p] = picked(diagonal, p)
         a = {(p, q): copied(c_ref.at[t, p], q) for p in range(SUB) for q in range(p + 1)}
         low, inverses, roots = {}, [], []
+        yield None
         for q in range(SUB):
             squares = {p: a[p, q] * a[q + 1, q] for p in range(q + 1, SUB)}
             inverse = pl.reciprocal(a[q, q], approx=True)
             inverses.append(inverse)
             roots.append(lax.rsqrt(a[q, q]))
+            yield None
             for p in range(q + 1, SUB):
                 a[p, q + 1] = a[p, q + 1] - squares[p] * inverse
             for p in range(q + 1, SUB):
@@ -120,10 +122,12 @@
                     a[p, r] = a[p, r] - low[p, q] * a[r, q]
         mult = {}
         for p in range(1, SUB):
+            if p % 2 == 0:
+                yield None
             for q in range(p):
                 terms = [low[p, q]] + [low[p, r] * mult[r, q] for r in range(q + 1, p)]
                 mult[p, q] = -added(terms)
-        return a, mult, inverses, roots
+        yield a, mult, inverses, roots
 
     def merged(parts):
         value = parts[0]
@@ -131,11 +135,10 @@
             value = jnp.where(group == p, parts[p], value)
         return value
 
-    def panel(t, kb):
-        for jv in [kb + 1 + n for n in range(groups - 1 - kb)] + list(range(kb)):
-            value = tile(t, kb, jv)
-            for p in range(SUB):
-                g_ref[t, p, pl.ds(jv * SUB, SUB), :] = picked(value, p)
+    def panel(t, kb, jv):
+        value = tile(t, kb, jv)
+        for p in range(SUB):
+            g_ref[kb % 2, t, p, pl.ds(jv * SUB, SUB), :] = picked(value, p)
 
     def store(t, kb, a, mult, inverses, roots):
         del inverses
@@ -160,7 +163,7 @@
                 middle = jnp.where(place == group, root, 0.0)
                 lower.append(jnp.where(place < group, final, middle))
                 continue
-            terms = [lanes[q] * g_ref[t, q, pl.ds(jv * SUB, SUB), :] for q in range(SUB - 1)]
+            terms = [lanes[q] * g_ref[kb % 2, t, q, pl.ds(jv * SUB, SUB), :] for q in range(SUB - 1)]
             final = added([tile(t, kb, jv)] + terms) * root
             upper.append(final if jv > kb else zero)
             lower.append(final if jv < kb else zero)
@@ -190,28 +193,52 @@
             for r in range(1, SUB):
                 value = jnp.where(place == r, -found[r], value)
         else:
-            terms = [found[r] * g_ref[t, r, pl.ds(jv * SUB, SUB), :] for r in range(SUB)]
+            terms = [found[r] * g_ref[kb % 2, t, r, pl.ds(jv * SUB, SUB), :] for r in range(SUB)]
             value = tile(t, ib, jv) - added(terms)
         w_ref[t, ib, pl.ds(jv * SUB, SUB), :] = value
 
-    corners = [corner(t, 0) for t in range(sets)]
+    def woven(chains, work):
+        results = [None] * len(chains)
+        steps = SUB + 5
+        for step in range(steps):
+            for n, chain in enumerate(chains):
+                results[n] = next(chain)
+            done = len(work) * step // steps
+            for item in work[done : len(work) * (step + 1) // steps]:
+                item()
+        return results
+
+    def gathers(kb):
+        order = list(range(kb + 1, groups)) + list(range(kb))
+        return [functools.partial(panel, t, kb, jv) for jv in order for t in range(sets)]
+
+    def bulk(t, kb, ib, state):
+        founds = {}
+
+        def prepare():
+            founds[ib] = weights(t, kb, ib, *state[1:3])
+
+        def subtract(jv):
+            trail(t, kb, ib, jv, founds[ib])
+
+        return [prepare] + [functools.partial(subtract, jv) for jv in range(groups)]
+
+    states = woven([corner(t, 0) for t in range(sets)], gathers(0))
     for kb in range(groups):
+        if kb + 1 == groups:
+            for t in range(sets):
+                store(t, kb, *states[t])
+            break
         for t in range(sets):
-            panel(t, kb)
-        ahead = []
-        if kb + 1 < groups:
+            found = weights(t, kb, kb + 1, *states[t][1:3])
+            for jv in [kb + 1] + [jv for jv in range(groups) if jv != kb + 1]:
+                trail(t, kb, kb + 1, jv, found)
+        work = gathers(kb + 1)
+        for ib in range(kb + 2, groups):
             for t in range(sets):
-                found = weights(t, kb, kb + 1, *corners[t][1:3])
-                for jv in [kb + 1] + [jv for jv in range(groups) if jv != kb + 1]:
-                    trail(t, kb, kb + 1, jv, found)
-            ahead = [corner(t, kb + 1) for t in range(sets)]
-        for t in range(sets):
-            for ib in range(kb + 2, groups):
-                found = weights(t, kb, ib, *corners[t][1:3])
-                for jv in range(groups):
-                    trail(t, kb, ib, jv, found)
-            store(t, kb, *corners[t])
-        corners = ahead
+                work += bulk(t, kb, ib, states[t])
+        work += [functools.partial(store, t, kb, *states[t]) for t in range(sets)]
+        states = woven([corner(t, kb + 1) for t in range(sets)], work)
 
 
 def pack(x):
@@ -501,7 +528,7 @@
     def scratch(sets):
         return [
             pltpu.VMEM((sets, groups, rank, LANES), F32),
-            pltpu.VMEM((sets, SUB, rank, LANES), F32),
+            pltpu.VMEM((2, sets, SUB, rank, LANES), F32),
             pltpu.VMEM((sets, SUB, SUB, LANES), F32),
         ]
 

time: 34.6 us -> 34.7 us (level)
  transfers between devices with their start and end apart: 5 -> 5, of which waited for: 1 -> 1; matrix products, arithmetic and copies ran while one was open for 0% -> 0% of each run, Pallas kernels for 33% -> 32%
where the time goes in v9:
time: 34.7 us; the launch traced here: 34.6 us
  Pallas kernels  22.6 us (65%)
  starting transfers between devices  9.29 us (27%)
  between operations  0.93 us (3%)
  local copies, waits for them, and re-layouts  0.85 us (2%)
  waiting for transfers between devices  0.85 us (2%)
    ppermute x5, starting transfers between devices, swap(): return lax.ppermute(value, axis, pairs)  9.29 us
    pallas_call x2, Pallas kernels, per_device(): pl.pallas_call(factor_kernel, in_specs=[vmem, any_place], out_specs=[vmem...  5.55 us
    pallas_call x1, Pallas kernels, per_device(): pl.pallas_call(functools.partial(top_kernel, n_rows, n_leaf, steps), in_s...  5.27 us
    pallas_call x1, Pallas kernels, per_device(): pl.pallas_call(functools.partial(gram_kernel, steps, sets), in_specs=[hbm...  4.51 us
    pallas_call x1, Pallas kernels, per_device(): pl.pallas_call(functools.partial(leaf_kernel, steps, sets), in_specs=[vme...  2.95 us
    pallas_call x1, Pallas kernels, per_device(): pl.pallas_call(own_kernel, in_specs=[vmem, any_place], out_specs=[vmem, v...  2.72 us
    unnamed x12, local copies, waits for them, and re-layouts  0.85 us
    ppermute x5, waiting for transfers between devices, swap(): return lax.ppermute(value, axis, pairs)  0.85 us
  transfers between devices with their start and end apart: 5, of which 1 were waited for; matrix products, arithmetic and copies ran while one was open for 0% of the time, Pallas kernels for 32%

profile of v9, /device:TPU:0, one launch (start us, length us, event | category | flops | bytes accessed | tf_op | source)
XLA Modules:
  0.0 34.6 jit_solution(4536156481606462989)
XLA Ops:
  0.6 0.0 copy-start
  0.6 0.0 copy-start.1
  0.7 0.8 %copy-done.1 = f32[1,64,64]{2,1,0:T(8,128)S(1)} copy-done((f32[1,64,64]{2,1,0:T(8,128)S(1)}, f32[1,64,64]{2,1,0:T(8,128)}, u32[]{:S(2)}) %copy-start.1) | copy-done | bytes 16408
  1.5 4.5 %gram.1 = (f32[16,64,64]{2,1,0:T(8,128)S(1)}, f32[16,64,64]{2,1,0:T(8,128)S(1)}, f32[32,128]{1,0:T(8,128)S(1)}, f32[32,128]{1,0:T(8,128)S(1)}) custom-call(f32[32,64,256]{2,1,0:T(8,128)} %basis_ref.1, f32[32,64,64]{2,1,0:T(8,128)} %trans_ref.1, f32[1,64,64]{2,1,0:T(8,128)S(1)} %copy-done.1), custom_call_target="tpu_custom_call" | custom-call | flops 1000000000 | bytes 4000000 | tf_op jit(solution)/shard_map/gram/pallas_call | solution.py:538
  6.0 0.5 %collective-permute-start = (f32[32,128]{1,0:T(8,128)S(1)}, f32[32,128]{1,0:T(8,128)S(1)}, u32[]{:S(2)}, u32[]{:S(2)}) collective-permute-start(f32[32,128]{1,0:T(8,128)S(1)} %get-tuple-element.28.mine_ref), channel_id=1, source_target_pairs={{0,1},{1,0},{2,3},{3,2},{4,5},{5,4},{6,7},{7,6},{8,9},{9,8},{10,11... | collective-permute-start | bytes 49160 | tf_op jit(solution)/shard_map/ppermute | solution.py:498
  6.5 0.8 %collective-permute-done.got_ref = f32[32,128]{1,0:T(8,128)S(1)} collective-permute-done((f32[32,128]{1,0:T(8,128)S(1)}, f32[32,128]{1,0:T(8,128)S(1)}, u32[]{:S(2)}, u32[]{:S(2)}) %collective-permute-start) | collective-permute-done | bytes 16416 | tf_op jit(solution)/shard_map/ppermute | solution.py:498
  7.4 0.4 %row_hop.2 = (f32[32,128]{1,0:T(8,128)S(1)}, f32[32,128]{1,0:T(8,128)S(1)}) custom-call(f32[32,128]{1,0:T(8,128)S(1)} %get-tuple-element.28.mine_ref, f32[32,128]{1,0:T(8,128)S(1)} %collective-permute-done.got_ref, f32[32,128]{1,0:T(8,128)S(1)} %get-tuple-element.27.own_ref.after_ref, f32[30,64,64]{2,1,0:T(8,128)S(1)} %copy-done, ...), custom_call_target="tpu_custom_call" | custom-call | tf_op jit(solution)/shard_map/row_hop/pallas_call | solution.py:569
  7.8 2.9 %collective-permute-start.1 = (f32[32,128]{1,0:T(8,128)S(1)}, f32[32,128]{1,0:T(8,128)S(1)}, u32[]{:S(2)}, u32[]{:S(2)}) collective-permute-start(f32[32,128]{1,0:T(8,128)S(1)} %get-tuple-element.29.after_ref.mine_ref), channel_id=1, source_target_pairs={{0,2},{1,3},{2,0},{3,1},{4,6},{5,7},{6,4},{7,5},{8,10},{9,11},{10,... | collective-permute-start | bytes 49160 | tf_op jit(solution)/shard_map/ppermute | solution.py:498
  10.7 2.7 %own.1 = (f32[64,128]{1,0:T(8,128)S(1)}, f32[8,128]{1,0:T(8,128)S(1)}) custom-call(f32[32,128]{1,0:T(8,128)S(1)} %get-tuple-element.27.own_ref.after_ref, f32[32,128]{1,0:T(8,128)S(1)} %get-tuple-element.29.after_ref.mine_ref), custom_call_target="tpu_custom_call" | custom-call | flops 5000000000 | bytes 8000000 | tf_op jit(solution)/shard_map/own/pallas_call | solution.py:559
  13.4 0.0 collective-permute-done.1.got_ref
  13.4 0.4 %row_hop.3 = (f32[32,128]{1,0:T(8,128)S(1)}, f32[64,128]{1,0:T(8,128)S(1)}) custom-call(f32[32,128]{1,0:T(8,128)S(1)} %get-tuple-element.29.after_ref.mine_ref, f32[32,128]{1,0:T(8,128)S(1)} %collective-permute-done.1.got_ref, f32[32,128]{1,0:T(8,128)S(1)} %get-tuple-element.27.own_ref.after_ref, f32[30,64,64]{2,1,0:T(8,128)S(1)} %copy-done, ...), custom_call_target="tpu_custom_call" | custom-call | tf_op jit(solution)/shard_map/row_hop/pallas_call | solution.py:569
  13.9 1.6 %collective-permute-start.2 = (f32[64,128]{1,0:T(8,128)S(1)}, f32[64,128]{1,0:T(8,128)S(1)}, u32[]{:S(2)}, u32[]{:S(2)}) collective-permute-start(f32[64,128]{1,0:T(8,128)S(1)} %get-tuple-element.32.after_ref.mine_ref), channel_id=1, source_target_pairs={{0,4},{4,0},{8,12},{12,8},{16,20},{20,16},{24,28},{28,24},{1,5},{5... | collective-permute-start | bytes 98312 | tf_op jit(solution)/shard_map/ppermute | solution.py:498
  15.4 2.8 %factor.2 = (f32[16,64,128]{2,1,0:T(8,128)S(1)}, f32[8,128]{1,0:T(8,128)S(1)}) custom-call(f32[16,64,64]{2,1,0:T(8,128)S(1)} %get-tuple-element.33.grams_ref, f32[64,128]{1,0:T(8,128)S(1)} %get-tuple-element.32.after_ref.mine_ref), custom_call_target="tpu_custom_call" | custom-call | flops 5000000000 | bytes 8000000 | tf_op jit(solution)/shard_map/factor/pallas_call | solution.py:582
  18.2 0.0 collective-permute-done.2.got_ref
  18.2 0.4 %leaf_hop.2 = (f32[32,128]{1,0:T(8,128)S(1)}, f32[72,128]{1,0:T(8,128)S(1)}) custom-call(f32[64,128]{1,0:T(8,128)S(1)} %get-tuple-element.32.after_ref.mine_ref, f32[64,128]{1,0:T(8,128)S(1)} %collective-permute-done.2.got_ref, f32[30,64,64]{2,1,0:T(8,128)S(1)} %copy-done, f32[8,128]{1,0:T(8,128)S(1)} %get-tuple-element.34.after_ref), custom_call_target="tpu_custom_call" | custom-call | tf_op jit(solution)/shard_map/leaf_hop/pallas_call | solution.py:593
  18.6 1.6 %collective-permute-start.3 = (f32[72,128]{1,0:T(8,128)S(1)}, f32[72,128]{1,0:T(8,128)S(1)}, u32[]{:S(2)}, u32[]{:S(2)}) collective-permute-start(f32[72,128]{1,0:T(8,128)S(1)} %get-tuple-element.35.after_ref.mine_ref), channel_id=1, source_target_pairs={{0,8},{4,12},{8,0},{12,4},{16,24},{20,28},{24,16},{28,20},{1,9},{5... | collective-permute-start | bytes 110600 | tf_op jit(solution)/shard_map/ppermute | solution.py:498
  20.3 2.8 %factor.3 = (f32[16,64,128]{2,1,0:T(8,128)S(1)}, f32[8,128]{1,0:T(8,128)S(1)}) custom-call(f32[16,64,64]{2,1,0:T(8,128)S(1)} %get-tuple-element.36.grams_ref, f32[72,128]{1,0:T(8,128)S(1)} %get-tuple-element.35.after_ref.mine_ref), custom_call_target="tpu_custom_call" | custom-call | flops 5000000000 | bytes 8000000 | tf_op jit(solution)/shard_map/factor/pallas_call | solution.py:582
  23.1 0.0 collective-permute-done.3.got_ref
  23.1 0.4 %leaf_hop.3 = (f32[32,128]{1,0:T(8,128)S(1)}, f32[112,128]{1,0:T(8,128)S(1)}) custom-call(f32[72,128]{1,0:T(8,128)S(1)} %get-tuple-element.35.after_ref.mine_ref, f32[72,128]{1,0:T(8,128)S(1)} %collective-permute-done.3.got_ref, f32[30,64,64]{2,1,0:T(8,128)S(1)} %copy-done, f32[8,128]{1,0:T(8,128)S(1)} %get-tuple-element.37.after_ref), custom_call_target="tpu_custom_call" | custom-call | tf_op jit(solution)/shard_map/leaf_hop/pallas_call | solution.py:593
  23.5 2.6 %collective-permute-start.4 = (f32[112,128]{1,0:T(8,128)S(1)}, f32[112,128]{1,0:T(8,128)S(1)}, u32[]{:S(2)}, u32[]{:S(2)}) collective-permute-start(f32[112,128]{1,0:T(8,128)S(1)} %get-tuple-element.38.after_ref.mine_ref), channel_id=1, source_target_pairs={{0,16},{4,20},{8,24},{12,28},{16,0},{20,4},{24,8},{28,12},{1,17},{... | collective-permute-start | bytes 172040 | tf_op jit(solution)/shard_map/ppermute | solution.py:498
  26.1 0.0 copy-done.3
  26.1 2.9 %leaf.1 = (f32[32,64,256]{2,1,0:T(8,128)}, f32[32,64,64]{2,1,0:T(8,128)}, bf16[32,64,128]{2,1,0:T(8,128)(2,1)S(1)}) custom-call(f32[32,64,256]{2,1,0:T(8,128)S(1)} %copy-done.3, f32[32,64,64]{2,1,0:T(8,128)S(1)} %copy-done.4, f32[32,64,64]{2,1,0:T(8,128)S(1)} %copy-done.5, f32[64,128]{1,0:T(8,128)S(1)} %get-tuple-element.30.own_ref.refs_6_, ...), custom_call_target="tpu_custom_call" | custom-call | flops 5000000000 | bytes 8000000 | tf_op jit(solution)/shard_map/leaf/pallas_call | solution.py:603
  29.1 0.0 collective-permute-done.4.got_ref
  29.1 5.3 %top.1 = (f32[1,5,64,64]{3,2,1,0:T(8,128)}, f32[32,64,64]{2,1,0:T(8,128)}) custom-call(f32[112,128]{1,0:T(8,128)S(1)} %get-tuple-element.38.after_ref.mine_ref, f32[112,128]{1,0:T(8,128)S(1)} %collective-permute-done.4.got_ref, f32[32,128]{1,0:T(8,128)S(1)} %get-tuple-element.43.refs_0_, f32[32,128]{1,0:T(8,128)S(1)} %get-tuple-element.44.refs_1_, ...), custom_call_target="tpu_custom_call" | custom-call | tf_op jit(solution)/shard_map/top/pallas_call | solution.py:623
  (8 shorter events, 0.0 us)
Async XLA Ops:
  0.6 6.7 %copy-start = (f32[30,64,64]{2,1,0:T(8,128)S(1)}, f32[30,64,64]{2,1,0:T(8,128)}, u32[]{:S(2)}) copy-start(f32[30,64,64]{2,1,0:T(8,128)} %refs_4_.1) | copy-start | bytes 1474564
  0.6 0.8 %copy-start.1 = (f32[1,64,64]{2,1,0:T(8,128)S(1)}, f32[1,64,64]{2,1,0:T(8,128)}, u32[]{:S(2)}) copy-start(f32[1,64,64]{2,1,0:T(8,128)} %refs_5_.1) | copy-start | bytes 49156
  6.0 1.4 %collective-permute-start = (f32[32,128]{1,0:T(8,128)S(1)}, f32[32,128]{1,0:T(8,128)S(1)}, u32[]{:S(2)}, u32[]{:S(2)}) collective-permute-start(f32[32,128]{1,0:T(8,128)S(1)} %get-tuple-element.28.mine_ref), channel_id=1, source_target_pairs={{0,1},{1,0},{2,3},{3,2},{4,5},{5,4},{6,7},{7,6},{8,9},{9,8},{10,11... | collective-permute-start | bytes 49160 | tf_op jit(solution)/shard_map/ppermute | solution.py:498
  7.8 5.6 %collective-permute-start.1 = (f32[32,128]{1,0:T(8,128)S(1)}, f32[32,128]{1,0:T(8,128)S(1)}, u32[]{:S(2)}, u32[]{:S(2)}) collective-permute-start(f32[32,128]{1,0:T(8,128)S(1)} %get-tuple-element.29.after_ref.mine_ref), channel_id=1, source_target_pairs={{0,2},{1,3},{2,0},{3,1},{4,6},{5,7},{6,4},{7,5},{8,10},{9,11},{10,... | collective-permute-start | bytes 49160 | tf_op jit(solution)/shard_map/ppermute | solution.py:498
  13.9 4.4 %collective-permute-start.2 = (f32[64,128]{1,0:T(8,128)S(1)}, f32[64,128]{1,0:T(8,128)S(1)}, u32[]{:S(2)}, u32[]{:S(2)}) collective-permute-start(f32[64,128]{1,0:T(8,128)S(1)} %get-tuple-element.32.after_ref.mine_ref), channel_id=1, source_target_pairs={{0,4},{4,0},{8,12},{12,8},{16,20},{20,16},{24,28},{28,24},{1,5},{5... | collective-permute-start | bytes 98312 | tf_op jit(solution)/shard_map/ppermute | solution.py:498
  18.6 4.4 %collective-permute-start.3 = (f32[72,128]{1,0:T(8,128)S(1)}, f32[72,128]{1,0:T(8,128)S(1)}, u32[]{:S(2)}, u32[]{:S(2)}) collective-permute-start(f32[72,128]{1,0:T(8,128)S(1)} %get-tuple-element.35.after_ref.mine_ref), channel_id=1, source_target_pairs={{0,8},{4,12},{8,0},{12,4},{16,24},{20,28},{24,16},{28,20},{1,9},{5... | collective-permute-start | bytes 110600 | tf_op jit(solution)/shard_map/ppermute | solution.py:498
  20.3 5.9 %copy-start.3 = (f32[32,64,256]{2,1,0:T(8,128)S(1)}, f32[32,64,256]{2,1,0:T(8,128)}, u32[]{:S(2)}) copy-start(f32[32,64,256]{2,1,0:T(8,128)} %basis_ref.1) | copy-start | bytes 6291460
  20.3 5.9 %copy-start.4 = (f32[32,64,64]{2,1,0:T(8,128)S(1)}, f32[32,64,64]{2,1,0:T(8,128)}, u32[]{:S(2)}) copy-start(f32[32,64,64]{2,1,0:T(8,128)} %trans_ref.1) | copy-start | bytes 1572868
  20.3 5.9 %copy-start.5 = (f32[32,64,64]{2,1,0:T(8,128)S(1)}, f32[32,64,64]{2,1,0:T(8,128)}, u32[]{:S(2)}) copy-start(f32[32,64,64]{2,1,0:T(8,128)} %coup_ref.1) | copy-start | bytes 1572868
  23.5 5.6 %collective-permute-start.4 = (f32[112,128]{1,0:T(8,128)S(1)}, f32[112,128]{1,0:T(8,128)S(1)}, u32[]{:S(2)}, u32[]{:S(2)}) collective-permute-start(f32[112,128]{1,0:T(8,128)S(1)} %get-tuple-element.38.after_ref.mine_ref), channel_id=1, source_target_pairs={{0,16},{4,20},{8,24},{12,28},{16,0},{20,4},{24,8},{28,12},{1,17},{... | collective-permute-start | bytes 172040 | tf_op jit(solution)/shard_map/ppermute | solution.py:498
  26.1 3.0 %copy-start.2 = (s32[32]{0:T(128)S(1)}, s32[32]{0:T(128)}, u32[]{:S(2)}) copy-start(s32[32]{0:T(128)} %refs_8_.1) | copy-start | bytes 388

commit v10 on v9

--- a/solution.py
+++ b/solution.py
@@ -84,7 +84,7 @@
             w_ref[t, ib] = jnp.concatenate(rows, axis=0).T
 
 
-def eliminate(w_ref, g_ref, c_ref, out, alone=False):
+def eliminate(w_ref, g_ref, c_ref, pick_ref, out, alone=False):
     sets, groups, rank = w_ref.shape[0], w_ref.shape[1], w_ref.shape[2]
     place = lax.broadcasted_iota(jnp.int32, (SUB, LANES), 0)
     lane = lax.broadcasted_iota(jnp.int32, (SUB, LANES), 1)
@@ -135,10 +135,19 @@
             value = jnp.where(group == p, parts[p], value)
         return value
 
-    def panel(t, kb, jv):
-        value = tile(t, kb, jv)
-        for p in range(SUB):
-            g_ref[kb % 2, t, p, pl.ds(jv * SUB, SUB), :] = picked(value, p)
+    def panel(t, kb):
+        parts = []
+
+        def prepare():
+            high, rest = halves(w_ref[t, kb])
+            parts.append(jnp.concatenate([high, *halves(rest)], axis=1).astype(B16))
+
+        def select(p):
+            found = mm(parts[0], pick_ref[:, pl.ds(p * LANES, 2 * LANES)])
+            g_ref[kb % 2, t, p] = found[:, :LANES]
+            g_ref[kb % 2, t, p + 1] = found[:, LANES:]
+
+        return [prepare] + [functools.partial(select, p) for p in range(0, SUB, 2)]
 
     def store(t, kb, a, mult, inverses, roots):
         del inverses
@@ -209,8 +218,7 @@
         return results
 
     def gathers(kb):
-        order = list(range(kb + 1, groups)) + list(range(kb))
-        return [functools.partial(panel, t, kb, jv) for jv in order for t in range(sets)]
+        return [item for t in range(sets) for item in panel(t, kb)]
 
     def bulk(t, kb, ib, state):
         founds = {}
@@ -223,6 +231,12 @@
 
         return [prepare] + [functools.partial(subtract, jv) for jv in range(groups)]
 
+    row = lax.broadcasted_iota(jnp.int32, (LANES, SUB * LANES), 0)
+    column = lax.broadcasted_iota(jnp.int32, (LANES, SUB * LANES), 1)
+    wanted = column // LANES * SET + column % SET
+    for n in range(3):
+        chosen = jnp.where(row == wanted, 1.0, 0.0).astype(B16)
+        pick_ref[pl.ds(n * LANES, LANES), :] = chosen
     states = woven([corner(t, 0) for t in range(sets)], gathers(0))
     for kb in range(groups):
         if kb + 1 == groups:
@@ -305,19 +319,19 @@
     lift_ref[...] = pack(lift(gram, dev_ref[0]))
 
 
-def factor_kernel(grams_ref, after_ref, out_ref, token_ref, w_ref, g_ref, c_ref):
+def factor_kernel(grams_ref, after_ref, out_ref, token_ref, w_ref, g_ref, c_ref, pick_ref):
     del after_ref
     count, rank = grams_ref.shape[0], grams_ref.shape[1]
     load_sets(grams_ref.reshape(count * rank, rank), w_ref)
-    eliminate(w_ref, g_ref, c_ref, out_ref.reshape(count * rank, 2 * rank))
+    eliminate(w_ref, g_ref, c_ref, pick_ref, out_ref.reshape(count * rank, 2 * rank))
     token_ref[...] = jnp.zeros(token_ref.shape, F32)
 
 
-def own_kernel(own_ref, after_ref, out_ref, token_ref, full_ref, w_ref, g_ref, c_ref):
+def own_kernel(own_ref, after_ref, out_ref, token_ref, full_ref, w_ref, g_ref, c_ref, pick_ref):
     del after_ref
     full_ref[...] = unpack(own_ref[...])
     load_sets(full_ref, w_ref, alone=True)
-    eliminate(w_ref, g_ref, c_ref, out_ref, alone=True)
+    eliminate(w_ref, g_ref, c_ref, pick_ref, out_ref, alone=True)
     token_ref[...] = jnp.zeros(token_ref.shape, F32)
 
 
@@ -444,6 +458,7 @@
         w_ref,
         g_ref,
         c_ref,
+        pick_ref,
     ) = refs[levels - 1 :]
     rank = grams_ref.shape[1]
     branch, row = lax.axis_index("leaf"), lax.axis_index("rows")
@@ -459,8 +474,10 @@
             at = levels + 2 * (place + n)
             grams_ref[at], grams_ref[at + 1] = part(joint)
     count = grams_ref.shape[0]
+    for n in range(levels + n_leaf, count):
+        grams_ref[n] = grams_ref[levels]
     load_sets(grams_ref.reshape(count * rank, rank), w_ref)
-    eliminate(w_ref, g_ref, c_ref, factor_ref.reshape(count * rank, 2 * rank))
+    eliminate(w_ref, g_ref, c_ref, pick_ref, factor_ref.reshape(count * rank, 2 * rank))
     for n in range(n_leaf):
         cols_ref[n] = broad(factor_ref[levels + n, :, :rank])
     copies = []
@@ -530,6 +547,7 @@
             pltpu.VMEM((sets, groups, rank, LANES), F32),
             pltpu.VMEM((2, sets, SUB, rank, LANES), F32),
             pltpu.VMEM((sets, SUB, SUB, LANES), F32),
+            pltpu.VMEM((3 * LANES, SUB * LANES), B16),
         ]
 
     sets = leaves // SET

time: 34.7 us -> 35.6 us (1.026)
  Pallas kernels: 22.6 us -> 23.4 us
    pallas_call x2, Pallas kernels: 5.55 us -> 6.12 us  [per_device(): pl.pallas_call(factor_kernel, in_specs=[vmem, any_place], out_specs=[vmem...]
  transfers between devices with their start and end apart: 5 -> 5, of which waited for: 1 -> 2; matrix products, arithmetic and copies ran while one was open for 0% -> 0% of each run, Pallas kernels for 32% -> 34%
where the time goes in v10:
time: 35.6 us; the launch traced here: 35.5 us
  Pallas kernels  23.4 us (66%)
  starting transfers between devices  9.29 us (26%)
  waiting for transfers between devices  0.99 us (3%)
  between operations  0.91 us (3%)
  local copies, waits for them, and re-layouts  0.85 us (2%)
    ppermute x5, starting transfers between devices, swap(): return lax.ppermute(value, axis, pairs)  9.29 us
    pallas_call x2, Pallas kernels, per_device(): pl.pallas_call(factor_kernel, in_specs=[vmem, any_place], out_specs=[vmem...  6.12 us
    pallas_call x1, Pallas kernels, per_device(): pl.pallas_call(functools.partial(top_kernel, n_rows, n_leaf, steps), in_s...  5.39 us
    pallas_call x1, Pallas kernels, per_device(): pl.pallas_call(functools.partial(gram_kernel, steps, sets), in_specs=[hbm...  4.51 us
    pallas_call x1, Pallas kernels, per_device(): pl.pallas_call(functools.partial(leaf_kernel, steps, sets), in_specs=[vme...  2.96 us
    pallas_call x1, Pallas kernels, per_device(): pl.pallas_call(own_kernel, in_specs=[vmem, any_place], out_specs=[vmem, v...  2.82 us
    ppermute x5, waiting for transfers between devices, swap(): return lax.ppermute(value, axis, pairs)  0.99 us
    unnamed x12, local copies, waits for them, and re-layouts  0.85 us
  transfers between devices with their start and end apart: 5, of which 2 were waited for; matrix products, arithmetic and copies ran while one was open for 0% of the time, Pallas kernels for 34%

profile of v10, /device:TPU:0, one launch (start us, length us, event | category | flops | bytes accessed | tf_op | source)
XLA Modules:
  0.0 35.5 jit_solution(15216514962223654955)
XLA Ops:
  0.6 0.0 copy-start
  0.6 0.0 copy-start.1
  0.7 0.8 %copy-done.1 = f32[1,64,64]{2,1,0:T(8,128)S(1)} copy-done((f32[1,64,64]{2,1,0:T(8,128)S(1)}, f32[1,64,64]{2,1,0:T(8,128)}, u32[]{:S(2)}) %copy-start.1) | copy-done | bytes 16408
  1.5 4.5 %gram.1 = (f32[16,64,64]{2,1,0:T(8,128)S(1)}, f32[16,64,64]{2,1,0:T(8,128)S(1)}, f32[32,128]{1,0:T(8,128)S(1)}, f32[32,128]{1,0:T(8,128)S(1)}) custom-call(f32[32,64,256]{2,1,0:T(8,128)} %basis_ref.1, f32[32,64,64]{2,1,0:T(8,128)} %trans_ref.1, f32[1,64,64]{2,1,0:T(8,128)S(1)} %copy-done.1), custom_call_target="tpu_custom_call" | custom-call | flops 1000000000 | bytes 4000000 | tf_op jit(solution)/shard_map/gram/pallas_call | solution.py:556
  6.0 0.5 %collective-permute-start = (f32[32,128]{1,0:T(8,128)S(1)}, f32[32,128]{1,0:T(8,128)S(1)}, u32[]{:S(2)}, u32[]{:S(2)}) collective-permute-start(f32[32,128]{1,0:T(8,128)S(1)} %get-tuple-element.28.mine_ref), channel_id=1, source_target_pairs={{0,1},{1,0},{2,3},{3,2},{4,5},{5,4},{6,7},{7,6},{8,9},{9,8},{10,11... | collective-permute-start | bytes 49160 | tf_op jit(solution)/shard_map/ppermute | solution.py:515
  6.5 0.8 %collective-permute-done.got_ref = f32[32,128]{1,0:T(8,128)S(1)} collective-permute-done((f32[32,128]{1,0:T(8,128)S(1)}, f32[32,128]{1,0:T(8,128)S(1)}, u32[]{:S(2)}, u32[]{:S(2)}) %collective-permute-start) | collective-permute-done | bytes 16416 | tf_op jit(solution)/shard_map/ppermute | solution.py:515
  7.4 0.4 %row_hop.2 = (f32[32,128]{1,0:T(8,128)S(1)}, f32[32,128]{1,0:T(8,128)S(1)}) custom-call(f32[32,128]{1,0:T(8,128)S(1)} %get-tuple-element.28.mine_ref, f32[32,128]{1,0:T(8,128)S(1)} %collective-permute-done.got_ref, f32[32,128]{1,0:T(8,128)S(1)} %get-tuple-element.27.own_ref.after_ref, f32[30,64,64]{2,1,0:T(8,128)S(1)} %copy-done, ...), custom_call_target="tpu_custom_call" | custom-call | tf_op jit(solution)/shard_map/row_hop/pallas_call | solution.py:587
  7.8 2.9 %collective-permute-start.1 = (f32[32,128]{1,0:T(8,128)S(1)}, f32[32,128]{1,0:T(8,128)S(1)}, u32[]{:S(2)}, u32[]{:S(2)}) collective-permute-start(f32[32,128]{1,0:T(8,128)S(1)} %get-tuple-element.29.after_ref.mine_ref), channel_id=1, source_target_pairs={{0,2},{1,3},{2,0},{3,1},{4,6},{5,7},{6,4},{7,5},{8,10},{9,11},{10,... | collective-permute-start | bytes 49160 | tf_op jit(solution)/shard_map/ppermute | solution.py:515
  10.7 2.8 %own.1 = (f32[64,128]{1,0:T(8,128)S(1)}, f32[8,128]{1,0:T(8,128)S(1)}) custom-call(f32[32,128]{1,0:T(8,128)S(1)} %get-tuple-element.27.own_ref.after_ref, f32[32,128]{1,0:T(8,128)S(1)} %get-tuple-element.29.after_ref.mine_ref), custom_call_target="tpu_custom_call" | custom-call | flops 5000000000 | bytes 8000000 | tf_op jit(solution)/shard_map/own/pallas_call | solution.py:577
  13.5 0.0 collective-permute-done.1.got_ref
  13.5 0.4 %row_hop.3 = (f32[32,128]{1,0:T(8,128)S(1)}, f32[64,128]{1,0:T(8,128)S(1)}) custom-call(f32[32,128]{1,0:T(8,128)S(1)} %get-tuple-element.29.after_ref.mine_ref, f32[32,128]{1,0:T(8,128)S(1)} %collective-permute-done.1.got_ref, f32[32,128]{1,0:T(8,128)S(1)} %get-tuple-element.27.own_ref.after_ref, f32[30,64,64]{2,1,0:T(8,128)S(1)} %copy-done, ...), custom_call_target="tpu_custom_call" | custom-call | tf_op jit(solution)/shard_map/row_hop/pallas_call | solution.py:587
  14.0 1.6 %collective-permute-start.2 = (f32[64,128]{1,0:T(8,128)S(1)}, f32[64,128]{1,0:T(8,128)S(1)}, u32[]{:S(2)}, u32[]{:S(2)}) collective-permute-start(f32[64,128]{1,0:T(8,128)S(1)} %get-tuple-element.32.after_ref.mine_ref), channel_id=1, source_target_pairs={{0,4},{4,0},{8,12},{12,8},{16,20},{20,16},{24,28},{28,24},{1,5},{5... | collective-permute-start | bytes 98312 | tf_op jit(solution)/shard_map/ppermute | solution.py:515
  15.5 3.1 %factor.2 = (f32[16,64,128]{2,1,0:T(8,128)S(1)}, f32[8,128]{1,0:T(8,128)S(1)}) custom-call(f32[16,64,64]{2,1,0:T(8,128)S(1)} %get-tuple-element.33.grams_ref, f32[64,128]{1,0:T(8,128)S(1)} %get-tuple-element.32.after_ref.mine_ref), custom_call_target="tpu_custom_call" | custom-call | flops 5000000000 | bytes 8000000 | tf_op jit(solution)/shard_map/factor/pallas_call | solution.py:600
  18.6 0.0 collective-permute-done.2.got_ref
  18.6 0.4 %leaf_hop.2 = (f32[32,128]{1,0:T(8,128)S(1)}, f32[72,128]{1,0:T(8,128)S(1)}) custom-call(f32[64,128]{1,0:T(8,128)S(1)} %get-tuple-element.32.after_ref.mine_ref, f32[64,128]{1,0:T(8,128)S(1)} %collective-permute-done.2.got_ref, f32[30,64,64]{2,1,0:T(8,128)S(1)} %copy-done, f32[8,128]{1,0:T(8,128)S(1)} %get-tuple-element.34.after_ref), custom_call_target="tpu_custom_call" | custom-call | tf_op jit(solution)/shard_map/leaf_hop/pallas_call | solution.py:611
  19.0 1.6 %collective-permute-start.3 = (f32[72,128]{1,0:T(8,128)S(1)}, f32[72,128]{1,0:T(8,128)S(1)}, u32[]{:S(2)}, u32[]{:S(2)}) collective-permute-start(f32[72,128]{1,0:T(8,128)S(1)} %get-tuple-element.35.after_ref.mine_ref), channel_id=1, source_target_pairs={{0,8},{4,12},{8,0},{12,4},{16,24},{20,28},{24,16},{28,20},{1,9},{5... | collective-permute-start | bytes 110600 | tf_op jit(solution)/shard_map/ppermute | solution.py:515
  20.7 3.1 %factor.3 = (f32[16,64,128]{2,1,0:T(8,128)S(1)}, f32[8,128]{1,0:T(8,128)S(1)}) custom-call(f32[16,64,64]{2,1,0:T(8,128)S(1)} %get-tuple-element.36.grams_ref, f32[72,128]{1,0:T(8,128)S(1)} %get-tuple-element.35.after_ref.mine_ref), custom_call_target="tpu_custom_call" | custom-call | flops 5000000000 | bytes 8000000 | tf_op jit(solution)/shard_map/factor/pallas_call | solution.py:600
  23.7 0.0 collective-permute-done.3.got_ref
  23.7 0.4 %leaf_hop.3 = (f32[32,128]{1,0:T(8,128)S(1)}, f32[112,128]{1,0:T(8,128)S(1)}) custom-call(f32[72,128]{1,0:T(8,128)S(1)} %get-tuple-element.35.after_ref.mine_ref, f32[72,128]{1,0:T(8,128)S(1)} %collective-permute-done.3.got_ref, f32[30,64,64]{2,1,0:T(8,128)S(1)} %copy-done, f32[8,128]{1,0:T(8,128)S(1)} %get-tuple-element.37.after_ref), custom_call_target="tpu_custom_call" | custom-call | tf_op jit(solution)/shard_map/leaf_hop/pallas_call | solution.py:611
  24.2 2.6 %collective-permute-start.4 = (f32[112,128]{1,0:T(8,128)S(1)}, f32[112,128]{1,0:T(8,128)S(1)}, u32[]{:S(2)}, u32[]{:S(2)}) collective-permute-start(f32[112,128]{1,0:T(8,128)S(1)} %get-tuple-element.38.after_ref.mine_ref), channel_id=1, source_target_pairs={{0,16},{4,20},{8,24},{12,28},{16,0},{20,4},{24,8},{28,12},{1,17},{... | collective-permute-start | bytes 172040 | tf_op jit(solution)/shard_map/ppermute | solution.py:515
  26.8 0.0 copy-done.4
  26.8 3.0 %leaf.1 = (f32[32,64,256]{2,1,0:T(8,128)}, f32[32,64,64]{2,1,0:T(8,128)}, bf16[32,64,128]{2,1,0:T(8,128)(2,1)S(1)}) custom-call(f32[32,64,256]{2,1,0:T(8,128)S(1)} %copy-done.3, f32[32,64,64]{2,1,0:T(8,128)S(1)} %copy-done.4, f32[32,64,64]{2,1,0:T(8,128)S(1)} %copy-done.5, f32[64,128]{1,0:T(8,128)S(1)} %get-tuple-element.30.own_ref.refs_6_, ...), custom_call_target="tpu_custom_call" | custom-call | flops 5000000000 | bytes 8000000 | tf_op jit(solution)/shard_map/leaf/pallas_call | solution.py:621
  29.8 0.1 collective-permute-done.4.got_ref
  29.9 5.4 %top.1 = (f32[1,5,64,64]{3,2,1,0:T(8,128)}, f32[32,64,64]{2,1,0:T(8,128)}) custom-call(f32[112,128]{1,0:T(8,128)S(1)} %get-tuple-element.38.after_ref.mine_ref, f32[112,128]{1,0:T(8,128)S(1)} %collective-permute-done.4.got_ref, f32[32,128]{1,0:T(8,128)S(1)} %get-tuple-element.43.refs_0_, f32[32,128]{1,0:T(8,128)S(1)} %get-tuple-element.44.refs_1_, ...), custom_call_target="tpu_custom_call" | custom-call | tf_op jit(solution)/shard_map/top/pallas_call | solution.py:641
  (8 shorter events, 0.0 us)
Async XLA Ops:
  0.6 6.7 %copy-start = (f32[30,64,64]{2,1,0:T(8,128)S(1)}, f32[30,64,64]{2,1,0:T(8,128)}, u32[]{:S(2)}) copy-start(f32[30,64,64]{2,1,0:T(8,128)} %refs_4_.1) | copy-start | bytes 1474564
  0.6 0.8 %copy-start.1 = (f32[1,64,64]{2,1,0:T(8,128)S(1)}, f32[1,64,64]{2,1,0:T(8,128)}, u32[]{:S(2)}) copy-start(f32[1,64,64]{2,1,0:T(8,128)} %refs_5_.1) | copy-start | bytes 49156
  6.0 1.4 %collective-permute-start = (f32[32,128]{1,0:T(8,128)S(1)}, f32[32,128]{1,0:T(8,128)S(1)}, u32[]{:S(2)}, u32[]{:S(2)}) collective-permute-start(f32[32,128]{1,0:T(8,128)S(1)} %get-tuple-element.28.mine_ref), channel_id=1, source_target_pairs={{0,1},{1,0},{2,3},{3,2},{4,5},{5,4},{6,7},{7,6},{8,9},{9,8},{10,11... | collective-permute-start | bytes 49160 | tf_op jit(solution)/shard_map/ppermute | solution.py:515
  7.8 5.7 %collective-permute-start.1 = (f32[32,128]{1,0:T(8,128)S(1)}, f32[32,128]{1,0:T(8,128)S(1)}, u32[]{:S(2)}, u32[]{:S(2)}) collective-permute-start(f32[32,128]{1,0:T(8,128)S(1)} %get-tuple-element.29.after_ref.mine_ref), channel_id=1, source_target_pairs={{0,2},{1,3},{2,0},{3,1},{4,6},{5,7},{6,4},{7,5},{8,10},{9,11},{10,... | collective-permute-start | bytes 49160 | tf_op jit(solution)/shard_map/ppermute | solution.py:515
  14.0 4.6 %collective-permute-start.2 = (f32[64,128]{1,0:T(8,128)S(1)}, f32[64,128]{1,0:T(8,128)S(1)}, u32[]{:S(2)}, u32[]{:S(2)}) collective-permute-start(f32[64,128]{1,0:T(8,128)S(1)} %get-tuple-element.32.after_ref.mine_ref), channel_id=1, source_target_pairs={{0,4},{4,0},{8,12},{12,8},{16,20},{20,16},{24,28},{28,24},{1,5},{5... | collective-permute-start | bytes 98312 | tf_op jit(solution)/shard_map/ppermute | solution.py:515
  19.0 4.7 %collective-permute-start.3 = (f32[72,128]{1,0:T(8,128)S(1)}, f32[72,128]{1,0:T(8,128)S(1)}, u32[]{:S(2)}, u32[]{:S(2)}) collective-permute-start(f32[72,128]{1,0:T(8,128)S(1)} %get-tuple-element.35.after_ref.mine_ref), channel_id=1, source_target_pairs={{0,8},{4,12},{8,0},{12,4},{16,24},{20,28},{24,16},{28,20},{1,9},{5... | collective-permute-start | bytes 110600 | tf_op jit(solution)/shard_map/ppermute | solution.py:515
  20.7 6.1 %copy-start.3 = (f32[32,64,256]{2,1,0:T(8,128)S(1)}, f32[32,64,256]{2,1,0:T(8,128)}, u32[]{:S(2)}) copy-start(f32[32,64,256]{2,1,0:T(8,128)} %basis_ref.1) | copy-start | bytes 6291460
  20.7 6.1 %copy-start.4 = (f32[32,64,64]{2,1,0:T(8,128)S(1)}, f32[32,64,64]{2,1,0:T(8,128)}, u32[]{:S(2)}) copy-start(f32[32,64,64]{2,1,0:T(8,128)} %trans_ref.1) | copy-start | bytes 1572868
  20.7 6.1 %copy-start.5 = (f32[32,64,64]{2,1,0:T(8,128)S(1)}, f32[32,64,64]{2,1,0:T(8,128)}, u32[]{:S(2)}) copy-start(f32[32,64,64]{2,1,0:T(8,128)} %coup_ref.1) | copy-start | bytes 1572868
  24.2 5.8 %collective-permute-start.4 = (f32[112,128]{1,0:T(8,128)S(1)}, f32[112,128]{1,0:T(8,128)S(1)}, u32[]{:S(2)}, u32[]{:S(2)}) collective-permute-start(f32[112,128]{1,0:T(8,128)S(1)} %get-tuple-element.38.after_ref.mine_ref), channel_id=1, source_target_pairs={{0,16},{4,20},{8,24},{12,28},{16,0},{20,4},{24,8},{28,12},{1,17},{... | collective-permute-start | bytes 172040 | tf_op jit(solution)/shard_map/ppermute | solution.py:515
  26.8 3.1 %copy-start.2 = (s32[32]{0:T(128)S(1)}, s32[32]{0:T(128)}, u32[]{:S(2)}) copy-start(s32[32]{0:T(128)} %refs_8_.1) | copy-start | bytes 388

commit v11 on v6

--- a/solution.py
+++ b/solution.py
@@ -236,12 +236,10 @@
             if stage * GROUP % chunk == 0:
                 for copy in copies[stage * GROUP // chunk]:
                     copy.wait()
-            threes = []
+            twos = []
             for n in range(stage * GROUP, (stage + 1) * GROUP):
-                high, rest = halves(basis_ref[n])
-                middle, low = halves(rest)
-                threes.append(jnp.concatenate([high, middle, low], axis=0).astype(B16))
-            products[stage] = [mm_nt(three, three) for three in threes]
+                twos.append(jnp.concatenate(halves(basis_ref[n]), axis=0).astype(B16))
+            products[stage] = [mm_nt(two, two) for two in twos]
         group = stage - 1
         if 0 <= group < groups:
             edges[group] = [
@@ -249,8 +247,7 @@
             ]
             parts[group] = []
             for n, product in enumerate(products.pop(group)):
-                rows = product[:rank] + product[rank : 2 * rank] + product[2 * rank :]
-                gram = fold(rows[:, : 2 * rank]) + rows[:, 2 * rank :]
+                gram = fold(product[:rank] + product[rank:])
                 at = group * GROUP + n
                 grams_refs[at // SET][at % SET] = gram
                 both = jnp.concatenate(halves(gram), axis=0).astype(B16)
@@ -381,8 +378,12 @@
         moved = twice(pair(jnp.concatenate(moved, axis=0)))
         bridge_ref[span] = mm_nt(moved, own_inverse).reshape(chunk, rank, rank)
         send(bridge_ref.at[span], bridge_hbm.at[span], bridge_sem.at[step])
-    for b in range(coup_ref.shape[0]):
-        split_ref[b] = pair(mm(own_upper, tall(coup_ref[b])))
+    chunk = coup_ref.shape[0] // steps
+    for step in range(steps):
+        span = range(step * chunk, (step + 1) * chunk)
+        values = [mm(own_upper, tall(coup_ref[b])) for b in span]
+        for b, value in zip(span, values):
+            split_ref[b] = pair(value)
     for copy in copies:
         copy.wait()
 

time: 34.4 us -> 34.1 us (level)
  no operation moved by 1% of the time
where the time goes in v11:
time: 34.1 us; the launch traced here: 34 us
  Pallas kernels  22.1 us (65%)
  starting transfers between devices  9.29 us (27%)
  between operations  0.93 us (3%)
  local copies, waits for them, and re-layouts  0.85 us (2%)
  waiting for transfers between devices  0.85 us (2%)
    ppermute x5, starting transfers between devices, swap(): return lax.ppermute(value, axis, pairs)  9.29 us
    pallas_call x2, Pallas kernels, per_device(): pl.pallas_call(factor_kernel, in_specs=[vmem, any_place], out_specs=[vmem...  5.43 us
    pallas_call x1, Pallas kernels, per_device(): pl.pallas_call(functools.partial(top_kernel, n_rows, n_leaf, steps), in_s...  5.11 us
    pallas_call x1, Pallas kernels, per_device(): pl.pallas_call(functools.partial(gram_kernel, steps, sets), in_specs=[hbm...  4.51 us
    pallas_call x1, Pallas kernels, per_device(): pl.pallas_call(functools.partial(leaf_kernel, steps, sets), in_specs=[vme...  2.77 us
    pallas_call x1, Pallas kernels, per_device(): pl.pallas_call(own_kernel, in_specs=[vmem, any_place], out_specs=[vmem, v...  2.6 us
    unnamed x12, local copies, waits for them, and re-layouts  0.85 us
    ppermute x5, waiting for transfers between devices, swap(): return lax.ppermute(value, axis, pairs)  0.85 us
  transfers between devices with their start and end apart: 5, of which 1 were waited for; matrix products, arithmetic and copies ran while one was open for 0% of the time, Pallas kernels for 32%

profile of v11, /device:TPU:0, one launch (start us, length us, event | category | flops | bytes accessed | tf_op | source)
XLA Modules:
  0.0 34.0 jit_solution(8239472863295616018)
XLA Ops:
  0.6 0.0 copy-start
  0.6 0.0 copy-start.1
  0.7 0.8 %copy-done.1 = f32[1,64,64]{2,1,0:T(8,128)S(1)} copy-done((f32[1,64,64]{2,1,0:T(8,128)S(1)}, f32[1,64,64]{2,1,0:T(8,128)}, u32[]{:S(2)}) %copy-start.1) | copy-done | bytes 16408
  1.5 4.5 %gram.1 = (f32[16,64,64]{2,1,0:T(8,128)S(1)}, f32[16,64,64]{2,1,0:T(8,128)S(1)}, f32[32,128]{1,0:T(8,128)S(1)}, f32[32,128]{1,0:T(8,128)S(1)}) custom-call(f32[32,64,256]{2,1,0:T(8,128)} %basis_ref.1, f32[32,64,64]{2,1,0:T(8,128)} %trans_ref.1, f32[1,64,64]{2,1,0:T(8,128)S(1)} %copy-done.1), custom_call_target="tpu_custom_call" | custom-call | flops 1000000000 | bytes 4000000 | tf_op jit(solution)/shard_map/gram/pallas_call | solution.py:501
  6.0 0.5 %collective-permute-start = (f32[32,128]{1,0:T(8,128)S(1)}, f32[32,128]{1,0:T(8,128)S(1)}, u32[]{:S(2)}, u32[]{:S(2)}) collective-permute-start(f32[32,128]{1,0:T(8,128)S(1)} %get-tuple-element.28.mine_ref), channel_id=1, source_target_pairs={{0,1},{1,0},{2,3},{3,2},{4,5},{5,4},{6,7},{7,6},{8,9},{9,8},{10,11... | collective-permute-start | bytes 49160 | tf_op jit(solution)/shard_map/ppermute | solution.py:462
  6.5 0.8 %collective-permute-done.got_ref = f32[32,128]{1,0:T(8,128)S(1)} collective-permute-done((f32[32,128]{1,0:T(8,128)S(1)}, f32[32,128]{1,0:T(8,128)S(1)}, u32[]{:S(2)}, u32[]{:S(2)}) %collective-permute-start) | collective-permute-done | bytes 16416 | tf_op jit(solution)/shard_map/ppermute | solution.py:462
  7.4 0.0 copy-done
  7.4 0.4 %row_hop.2 = (f32[32,128]{1,0:T(8,128)S(1)}, f32[32,128]{1,0:T(8,128)S(1)}) custom-call(f32[32,128]{1,0:T(8,128)S(1)} %get-tuple-element.28.mine_ref, f32[32,128]{1,0:T(8,128)S(1)} %collective-permute-done.got_ref, f32[32,128]{1,0:T(8,128)S(1)} %get-tuple-element.27.own_ref.after_ref, f32[30,64,64]{2,1,0:T(8,128)S(1)} %copy-done, ...), custom_call_target="tpu_custom_call" | custom-call | tf_op jit(solution)/shard_map/row_hop/pallas_call | solution.py:532
  7.8 2.9 %collective-permute-start.1 = (f32[32,128]{1,0:T(8,128)S(1)}, f32[32,128]{1,0:T(8,128)S(1)}, u32[]{:S(2)}, u32[]{:S(2)}) collective-permute-start(f32[32,128]{1,0:T(8,128)S(1)} %get-tuple-element.29.after_ref.mine_ref), channel_id=1, source_target_pairs={{0,2},{1,3},{2,0},{3,1},{4,6},{5,7},{6,4},{7,5},{8,10},{9,11},{10,... | collective-permute-start | bytes 49160 | tf_op jit(solution)/shard_map/ppermute | solution.py:462
  10.7 2.6 %own.1 = (f32[64,128]{1,0:T(8,128)S(1)}, f32[8,128]{1,0:T(8,128)S(1)}) custom-call(f32[32,128]{1,0:T(8,128)S(1)} %get-tuple-element.27.own_ref.after_ref, f32[32,128]{1,0:T(8,128)S(1)} %get-tuple-element.29.after_ref.mine_ref), custom_call_target="tpu_custom_call" | custom-call | flops 5000000000 | bytes 8000000 | tf_op jit(solution)/shard_map/own/pallas_call | solution.py:522
  13.3 0.0 collective-permute-done.1.got_ref
  13.3 0.4 %row_hop.3 = (f32[32,128]{1,0:T(8,128)S(1)}, f32[64,128]{1,0:T(8,128)S(1)}) custom-call(f32[32,128]{1,0:T(8,128)S(1)} %get-tuple-element.29.after_ref.mine_ref, f32[32,128]{1,0:T(8,128)S(1)} %collective-permute-done.1.got_ref, f32[32,128]{1,0:T(8,128)S(1)} %get-tuple-element.27.own_ref.after_ref, f32[30,64,64]{2,1,0:T(8,128)S(1)} %copy-done, ...), custom_call_target="tpu_custom_call" | custom-call | tf_op jit(solution)/shard_map/row_hop/pallas_call | solution.py:532
  13.7 1.6 %collective-permute-start.2 = (f32[64,128]{1,0:T(8,128)S(1)}, f32[64,128]{1,0:T(8,128)S(1)}, u32[]{:S(2)}, u32[]{:S(2)}) collective-permute-start(f32[64,128]{1,0:T(8,128)S(1)} %get-tuple-element.32.after_ref.mine_ref), channel_id=1, source_target_pairs={{0,4},{4,0},{8,12},{12,8},{16,20},{20,16},{24,28},{28,24},{1,5},{5... | collective-permute-start | bytes 98312 | tf_op jit(solution)/shard_map/ppermute | solution.py:462
  15.3 2.7 %factor.2 = (f32[16,64,128]{2,1,0:T(8,128)S(1)}, f32[8,128]{1,0:T(8,128)S(1)}) custom-call(f32[16,64,64]{2,1,0:T(8,128)S(1)} %get-tuple-element.33.grams_ref, f32[64,128]{1,0:T(8,128)S(1)} %get-tuple-element.32.after_ref.mine_ref), custom_call_target="tpu_custom_call" | custom-call | flops 5000000000 | bytes 8000000 | tf_op jit(solution)/shard_map/factor/pallas_call | solution.py:545
  18.0 0.0 collective-permute-done.2.got_ref
  18.0 0.4 %leaf_hop.2 = (f32[32,128]{1,0:T(8,128)S(1)}, f32[72,128]{1,0:T(8,128)S(1)}) custom-call(f32[64,128]{1,0:T(8,128)S(1)} %get-tuple-element.32.after_ref.mine_ref, f32[64,128]{1,0:T(8,128)S(1)} %collective-permute-done.2.got_ref, f32[30,64,64]{2,1,0:T(8,128)S(1)} %copy-done, f32[8,128]{1,0:T(8,128)S(1)} %get-tuple-element.34.after_ref), custom_call_target="tpu_custom_call" | custom-call | tf_op jit(solution)/shard_map/leaf_hop/pallas_call | solution.py:556
  18.5 1.6 %collective-permute-start.3 = (f32[72,128]{1,0:T(8,128)S(1)}, f32[72,128]{1,0:T(8,128)S(1)}, u32[]{:S(2)}, u32[]{:S(2)}) collective-permute-start(f32[72,128]{1,0:T(8,128)S(1)} %get-tuple-element.35.after_ref.mine_ref), channel_id=1, source_target_pairs={{0,8},{4,12},{8,0},{12,4},{16,24},{20,28},{24,16},{28,20},{1,9},{5... | collective-permute-start | bytes 110600 | tf_op jit(solution)/shard_map/ppermute | solution.py:462
  20.1 2.7 %factor.3 = (f32[16,64,128]{2,1,0:T(8,128)S(1)}, f32[8,128]{1,0:T(8,128)S(1)}) custom-call(f32[16,64,64]{2,1,0:T(8,128)S(1)} %get-tuple-element.36.grams_ref, f32[72,128]{1,0:T(8,128)S(1)} %get-tuple-element.35.after_ref.mine_ref), custom_call_target="tpu_custom_call" | custom-call | flops 5000000000 | bytes 8000000 | tf_op jit(solution)/shard_map/factor/pallas_call | solution.py:545
  22.8 0.0 collective-permute-done.3.got_ref
  22.8 0.4 %leaf_hop.3 = (f32[32,128]{1,0:T(8,128)S(1)}, f32[112,128]{1,0:T(8,128)S(1)}) custom-call(f32[72,128]{1,0:T(8,128)S(1)} %get-tuple-element.35.after_ref.mine_ref, f32[72,128]{1,0:T(8,128)S(1)} %collective-permute-done.3.got_ref, f32[30,64,64]{2,1,0:T(8,128)S(1)} %copy-done, f32[8,128]{1,0:T(8,128)S(1)} %get-tuple-element.37.after_ref), custom_call_target="tpu_custom_call" | custom-call | tf_op jit(solution)/shard_map/leaf_hop/pallas_call | solution.py:556
  23.3 2.6 %collective-permute-start.4 = (f32[112,128]{1,0:T(8,128)S(1)}, f32[112,128]{1,0:T(8,128)S(1)}, u32[]{:S(2)}, u32[]{:S(2)}) collective-permute-start(f32[112,128]{1,0:T(8,128)S(1)} %get-tuple-element.38.after_ref.mine_ref), channel_id=1, source_target_pairs={{0,16},{4,20},{8,24},{12,28},{16,0},{20,4},{24,8},{28,12},{1,17},{... | collective-permute-start | bytes 172040 | tf_op jit(solution)/shard_map/ppermute | solution.py:462
  25.9 2.8 %leaf.1 = (f32[32,64,256]{2,1,0:T(8,128)}, f32[32,64,64]{2,1,0:T(8,128)}, bf16[32,64,128]{2,1,0:T(8,128)(2,1)S(1)}) custom-call(f32[32,64,256]{2,1,0:T(8,128)S(1)} %copy-done.3, f32[32,64,64]{2,1,0:T(8,128)S(1)} %copy-done.4, f32[32,64,64]{2,1,0:T(8,128)S(1)} %copy-done.5, f32[64,128]{1,0:T(8,128)S(1)} %get-tuple-element.30.own_ref.refs_6_, ...), custom_call_target="tpu_custom_call" | custom-call | flops 5000000000 | bytes 8000000 | tf_op jit(solution)/shard_map/leaf/pallas_call | solution.py:566
  28.7 0.0 collective-permute-done.4.got_ref
  28.7 5.1 %top.1 = (f32[1,5,64,64]{3,2,1,0:T(8,128)}, f32[32,64,64]{2,1,0:T(8,128)}) custom-call(f32[112,128]{1,0:T(8,128)S(1)} %get-tuple-element.38.after_ref.mine_ref, f32[112,128]{1,0:T(8,128)S(1)} %collective-permute-done.4.got_ref, f32[32,128]{1,0:T(8,128)S(1)} %get-tuple-element.43.refs_0_, f32[32,128]{1,0:T(8,128)S(1)} %get-tuple-element.44.refs_1_, ...), custom_call_target="tpu_custom_call" | custom-call | tf_op jit(solution)/shard_map/top/pallas_call | solution.py:586
  (8 shorter events, 0.0 us)
Async XLA Ops:
  0.6 6.7 %copy-start = (f32[30,64,64]{2,1,0:T(8,128)S(1)}, f32[30,64,64]{2,1,0:T(8,128)}, u32[]{:S(2)}) copy-start(f32[30,64,64]{2,1,0:T(8,128)} %refs_4_.1) | copy-start | bytes 1474564
  0.6 0.8 %copy-start.1 = (f32[1,64,64]{2,1,0:T(8,128)S(1)}, f32[1,64,64]{2,1,0:T(8,128)}, u32[]{:S(2)}) copy-start(f32[1,64,64]{2,1,0:T(8,128)} %refs_5_.1) | copy-start | bytes 49156
  6.0 1.4 %collective-permute-start = (f32[32,128]{1,0:T(8,128)S(1)}, f32[32,128]{1,0:T(8,128)S(1)}, u32[]{:S(2)}, u32[]{:S(2)}) collective-permute-start(f32[32,128]{1,0:T(8,128)S(1)} %get-tuple-element.28.mine_ref), channel_id=1, source_target_pairs={{0,1},{1,0},{2,3},{3,2},{4,5},{5,4},{6,7},{7,6},{8,9},{9,8},{10,11... | collective-permute-start | bytes 49160 | tf_op jit(solution)/shard_map/ppermute | solution.py:462
  7.8 5.5 %collective-permute-start.1 = (f32[32,128]{1,0:T(8,128)S(1)}, f32[32,128]{1,0:T(8,128)S(1)}, u32[]{:S(2)}, u32[]{:S(2)}) collective-permute-start(f32[32,128]{1,0:T(8,128)S(1)} %get-tuple-element.29.after_ref.mine_ref), channel_id=1, source_target_pairs={{0,2},{1,3},{2,0},{3,1},{4,6},{5,7},{6,4},{7,5},{8,10},{9,11},{10,... | collective-permute-start | bytes 49160 | tf_op jit(solution)/shard_map/ppermute | solution.py:462
  13.7 4.3 %collective-permute-start.2 = (f32[64,128]{1,0:T(8,128)S(1)}, f32[64,128]{1,0:T(8,128)S(1)}, u32[]{:S(2)}, u32[]{:S(2)}) collective-permute-start(f32[64,128]{1,0:T(8,128)S(1)} %get-tuple-element.32.after_ref.mine_ref), channel_id=1, source_target_pairs={{0,4},{4,0},{8,12},{12,8},{16,20},{20,16},{24,28},{28,24},{1,5},{5... | collective-permute-start | bytes 98312 | tf_op jit(solution)/shard_map/ppermute | solution.py:462
  18.5 4.4 %collective-permute-start.3 = (f32[72,128]{1,0:T(8,128)S(1)}, f32[72,128]{1,0:T(8,128)S(1)}, u32[]{:S(2)}, u32[]{:S(2)}) collective-permute-start(f32[72,128]{1,0:T(8,128)S(1)} %get-tuple-element.35.after_ref.mine_ref), channel_id=1, source_target_pairs={{0,8},{4,12},{8,0},{12,4},{16,24},{20,28},{24,16},{28,20},{1,9},{5... | collective-permute-start | bytes 110600 | tf_op jit(solution)/shard_map/ppermute | solution.py:462
  20.1 5.8 %copy-start.3 = (f32[32,64,256]{2,1,0:T(8,128)S(1)}, f32[32,64,256]{2,1,0:T(8,128)}, u32[]{:S(2)}) copy-start(f32[32,64,256]{2,1,0:T(8,128)} %basis_ref.1) | copy-start | bytes 6291460
  20.1 5.8 %copy-start.4 = (f32[32,64,64]{2,1,0:T(8,128)S(1)}, f32[32,64,64]{2,1,0:T(8,128)}, u32[]{:S(2)}) copy-start(f32[32,64,64]{2,1,0:T(8,128)} %trans_ref.1) | copy-start | bytes 1572868
  20.1 5.8 %copy-start.5 = (f32[32,64,64]{2,1,0:T(8,128)S(1)}, f32[32,64,64]{2,1,0:T(8,128)}, u32[]{:S(2)}) copy-start(f32[32,64,64]{2,1,0:T(8,128)} %coup_ref.1) | copy-start | bytes 1572868
  23.3 5.4 %collective-permute-start.4 = (f32[112,128]{1,0:T(8,128)S(1)}, f32[112,128]{1,0:T(8,128)S(1)}, u32[]{:S(2)}, u32[]{:S(2)}) collective-permute-start(f32[112,128]{1,0:T(8,128)S(1)} %get-tuple-element.38.after_ref.mine_ref), channel_id=1, source_target_pairs={{0,16},{4,20},{8,24},{12,28},{16,0},{20,4},{24,8},{28,12},{1,17},{... | collective-permute-start | bytes 172040 | tf_op jit(solution)/shard_map/ppermute | solution.py:462
  25.9 2.8 %copy-start.2 = (s32[32]{0:T(128)S(1)}, s32[32]{0:T(128)}, u32[]{:S(2)}) copy-start(s32[32]{0:T(128)} %refs_8_.1) | copy-start | bytes 388
